TPU v7x, 128 devices: a whole 4x4x4 slice. The times are simulated.
128 devices in a mesh: dp: 4 (over y), expert: 8 (over z, core), tensor: 4 (over x).
Axes of the slice: x: 4, y: 4, z: 4, core: 2. Of those that a mesh axis runs over, the one named last changes fastest.
Arguments:
- tokens: bfloat16 [16384, 1536], P(('dp', 'expert', 'tensor')), may hold values from -6 to 6
- documents: int32 [16384], P(('dp', 'expert')), may hold values from 0 to 2, as said below
- expert_routes: int32 [16384, 8], P(('dp', 'expert', 'tensor')), may hold values from 0 to 39, all different within a row; in each aligned block of 128 rows (0 to 127, 128 to 255, ...) at most 36 rows name the same one
- attention_gain: bfloat16 [1536], replicated, may hold values from 0.5 to 1.5
- query_weight: bfloat16 [1536, 1536], P(None, 'tensor'), may hold values from -0.15625 to 0.15625
- key_matrix: bfloat16 [1536, 512], P(None, 'tensor'), may hold values from -0.15625 to 0.15625
- value_matrix: bfloat16 [1536, 512], P(None, 'tensor'), may hold values from -0.15625 to 0.15625
- output_weight: bfloat16 [1536, 1536], P('tensor'), may hold values from -1.25 to 1.25
- expert_gain: bfloat16 [1536], replicated, may hold values from 0.5 to 1.5
- router_weight: bfloat16 [1536, 40], replicated, may hold values from -0.078125 to 0.078125
- gate_weight: bfloat16 [40, 1536, 512], P('expert', None, 'tensor'), may hold values from -0.15625 to 0.15625
- up_weight: bfloat16 [40, 1536, 512], P('expert', None, 'tensor'), may hold values from -0.15625 to 0.15625
- down_weight: bfloat16 [40, 512, 1536], P('expert', 'tensor'), may hold values from -1 to 1
- out_cotangent: bfloat16 [16384, 1536], P(('dp', 'expert', 'tensor')), may hold values from -6 to 6
Outputs:
- layer_output: bfloat16 [16384, 1536], P(('dp', 'expert', 'tensor'))
- input_gradient: float32 [16384, 1536], P(('dp', 'expert', 'tensor'))
- attention_gain_gradient: float32 [1536], replicated
- query_gradient: float32 [1536, 1536], P(None, 'tensor')
- key_gradient: float32 [1536, 512], P(None, 'tensor')
- value_gradient: float32 [1536, 512], P(None, 'tensor')
- output_gradient: float32 [1536, 1536], P('tensor')
- expert_gain_gradient: float32 [1536], replicated
- router_gradient: float32 [1536, 40], replicated
- gate_gradient: float32 [40, 1536, 512], P('expert', None, 'tensor')
- up_gradient: float32 [40, 1536, 512], P('expert', None, 'tensor')
- down_gradient: float32 [40, 512, 1536], P('expert', 'tensor')
Inputs may be any that keep to these rules, and one draw needn't show every extreme that they name: `documents`: in each group of 512 consecutive tokens the ids never fall and begin at 0. `expert_routes`: each token names 8 different experts; among the pairs of the 128 tokens of one device no expert is named more than 36 times.
All inputs are finite; a program needn't handle non-finite values.
Results may differ from a plain program's by a relative error of at most 0.025.
Values may be sent and summed in bfloat16 or wider, within the bound.
A program may use at most 384 MiB of HBM per device.

v0:
```python
import math

import jax
import jax.numpy as jnp
from jax import lax
from jax.sharding import PartitionSpec as P

HEAD_SIZE = 64
CAP = 36


epsilon = 1e-06
theta = 10000.0
highest = lax.Precision.HIGHEST


def normalize(value_rows, gain):
    scale = lax.rsqrt(jnp.mean(value_rows * value_rows, -1, keepdims=True) + epsilon)
    return (value_rows * scale * gain, scale)


def norm_back(value_rows, scale, gain, upstream):
    weighted = upstream * gain
    inner = jnp.mean(weighted * value_rows, -1, keepdims=True)
    result = scale * weighted - value_rows * scale**3 * inner
    gain_part = jnp.sum(upstream * value_rows * scale, 0)
    return (result, gain_part)


def rope_tables(positions, width):
    half = width // 2
    freq = theta ** (-(jnp.arange(half, dtype=jnp.float32) * 2.0 / width))
    angle = positions.astype(jnp.float32)[:, None] * freq[None, :]
    return (jnp.cos(angle), jnp.sin(angle))


def apply_rotation(value_rows, cosine_table, sine_table):
    half = value_rows.shape[-1] // 2
    first = value_rows[..., :half]
    second = value_rows[..., half:]
    cosine_table = cosine_table[:, None, :]
    sine_table = sine_table[:, None, :]
    return jnp.concatenate(
        [first * cosine_table - second * sine_table, second * cosine_table + first * sine_table], -1
    )


def rotate_back(value_rows, cosine_table, sine_table):
    half = value_rows.shape[-1] // 2
    first = value_rows[..., :half]
    second = value_rows[..., half:]
    cosine_table = cosine_table[:, None, :]
    sine_table = sine_table[:, None, :]
    return jnp.concatenate(
        [first * cosine_table + second * sine_table, second * cosine_table - first * sine_table], -1
    )


def to_experts(own, n_expert, n_tensor, local_experts, capacity):
    width = own.shape[-1]
    by_owner = own.reshape(n_expert, local_experts * capacity, width)
    copies = jnp.broadcast_to(
        by_owner[:, None], (n_expert, n_tensor, local_experts * capacity, width)
    )
    copies = copies.reshape(n_expert * n_tensor, local_experts * capacity, width)
    arrived = lax.all_to_all(copies, ("expert", "tensor"), split_axis=0, concat_axis=0, tiled=True)
    return arrived.reshape(n_expert, n_tensor, local_experts, capacity, width)


def to_sources(partial_value, n_expert, n_tensor):
    width = partial_value.shape[-1]
    sent = partial_value.reshape(n_expert * n_tensor, -1, width)
    arrived = lax.all_to_all(
        sent.astype(jnp.bfloat16), ("expert", "tensor"), split_axis=0, concat_axis=0, tiled=True
    ).astype(sent.dtype)
    summed = jnp.sum(arrived.reshape(n_expert, n_tensor, -1, width), 1)
    return summed.astype(jnp.bfloat16).reshape(-1, width)


def shards(
    tokens,
    documents,
    expert_routes,
    attention_gain,
    query_weight,
    key_matrix,
    value_matrix,
    output_weight,
    expert_gain,
    router_weight,
    gate_weight,
    up_weight,
    down_weight,
    out_cotangent,
):
    n_tensor = lax.axis_size("tensor")
    n_expert = lax.axis_size("expert")
    tok_local = tokens.shape[0]
    width = tokens.shape[1]
    group_len = documents.shape[0]
    query_heads = query_weight.shape[1] // HEAD_SIZE
    pair_heads = key_matrix.shape[1] // HEAD_SIZE
    frequency_ratio = query_heads // pair_heads
    local_experts = gate_weight.shape[0]
    experts_all = router_weight.shape[1]
    top_count = expert_routes.shape[1]
    capacity = CAP
    scale = 1.0 / math.sqrt(HEAD_SIZE)
    inputs = tokens.astype(jnp.float32)
    first_gain = attention_gain.astype(jnp.float32)
    first_normed, first_scale = normalize(inputs, first_gain)
    group_rows = lax.all_gather(first_normed.astype(jnp.bfloat16), "tensor", axis=0, tiled=True)
    index = jnp.arange(group_len, dtype=jnp.int32)
    positions = index - jnp.sum((documents[None, :] < documents[:, None]).astype(jnp.int32), 1)
    cosine_table, sine_table = rope_tables(positions, HEAD_SIZE)
    query_linear = jnp.dot(group_rows, query_weight, preferred_element_type=jnp.float32).reshape(
        group_len, query_heads, HEAD_SIZE
    )
    key_linear = jnp.dot(group_rows, key_matrix, preferred_element_type=jnp.float32).reshape(
        group_len, pair_heads, HEAD_SIZE
    )
    value_low = (
        jnp.dot(group_rows, value_matrix, preferred_element_type=jnp.float32)
        .astype(jnp.bfloat16)
        .reshape(group_len, pair_heads, HEAD_SIZE)
    )
    query_low = (
        apply_rotation(query_linear, cosine_table, sine_table)
        .astype(jnp.bfloat16)
        .reshape(group_len, pair_heads, frequency_ratio, HEAD_SIZE)
    )
    key_low = apply_rotation(key_linear, cosine_table, sine_table).astype(jnp.bfloat16)
    block_rows = min(512, group_len)
    count = group_len // block_rows
    starts = jnp.arange(count, dtype=jnp.int32) * block_rows

    def block_scores(start):
        rows_index = start + jnp.arange(block_rows, dtype=jnp.int32)
        scores = (
            jnp.einsum("qhgd,khd->hgqk", query_low, key_low, preferred_element_type=jnp.float32)
            * scale
        )
        allowed = (documents[:, None] == documents[None, :]) & (
            index[None, :] <= rows_index[:, None]
        )
        return (jnp.where(allowed, scores, -1e30), query_low)

    def forward_block(start):
        scores, block_query = block_scores(start)
        top = jnp.max(scores, -1, keepdims=True)
        weights = jnp.exp(scores - top)
        total = jnp.sum(weights, -1, keepdims=True)
        probs = (weights / total).astype(jnp.bfloat16)
        mixed = jnp.einsum("hgqk,khd->qhgd", probs, value_low, preferred_element_type=jnp.float32)
        return (
            mixed.astype(jnp.bfloat16).reshape(block_rows, query_heads * HEAD_SIZE),
            (top + jnp.log(total))[..., 0],
        )

    mixed_blocks, logsum_blocks = lax.map(forward_block, starts)
    attended = mixed_blocks.reshape(group_len, query_heads * HEAD_SIZE)
    head_part = jnp.dot(attended, output_weight, preferred_element_type=jnp.float32)
    branch = lax.psum_scatter(
        head_part.astype(jnp.bfloat16), "tensor", scatter_dimension=0, tiled=True
    ).astype(jnp.float32)
    residual = inputs + branch
    second_gain = expert_gain.astype(jnp.float32)
    second_normed, second_scale = normalize(residual, second_gain)
    second_low = second_normed.astype(jnp.bfloat16)
    logits = jnp.dot(second_low, router_weight, preferred_element_type=jnp.float32)
    onehot = (
        expert_routes[:, :, None] == jnp.arange(experts_all, dtype=jnp.int32)[None, None, :]
    ).astype(jnp.float32)
    chosen = jnp.sum(onehot * logits[:, None, :], -1)
    chosen_exp = jnp.exp(chosen - jnp.max(chosen, -1, keepdims=True))
    gates = chosen_exp / jnp.sum(chosen_exp, -1, keepdims=True)
    flat_routes = expert_routes.reshape(-1)
    route_total = flat_routes.shape[0]
    flat_hot = (flat_routes[:, None] == jnp.arange(experts_all, dtype=jnp.int32)[None, :]).astype(
        jnp.int32
    )
    rank = jnp.sum((jnp.cumsum(flat_hot, 0) - 1) * flat_hot, 1)
    slot_of = flat_routes * capacity + rank
    source_of = (
        jnp.full((experts_all * capacity,), route_total, jnp.int32)
        .at[slot_of]
        .set(jnp.arange(route_total, dtype=jnp.int32))
    )
    filled = source_of < route_total
    source_safe = jnp.minimum(source_of, route_total - 1)
    token_of = source_safe // top_count
    zero_low = jnp.zeros((), jnp.bfloat16)
    send_rows = jnp.where(filled[:, None], second_low[token_of], zero_low)
    arrived = to_experts(send_rows, n_expert, n_tensor, local_experts, capacity)
    gate_pre = jnp.einsum(
        "abxcd,xdf->abxcf", arrived, gate_weight, preferred_element_type=jnp.float32
    )
    up_pre = jnp.einsum("abxcd,xdf->abxcf", arrived, up_weight, preferred_element_type=jnp.float32)
    sigmoid_gate = jax.nn.sigmoid(gate_pre)
    silu_gate = gate_pre * sigmoid_gate
    activated = (silu_gate * up_pre).astype(jnp.bfloat16)
    down_part = jnp.einsum(
        "abxcf,xfd->abxcd", activated, down_weight, preferred_element_type=jnp.float32
    )
    returned = to_sources(down_part, n_expert, n_tensor)
    picked = returned[slot_of].reshape(tok_local, top_count, width)
    mixture = jnp.sum(gates[:, :, None] * picked.astype(jnp.float32), 1)
    layer_output = (residual + mixture).astype(jnp.bfloat16)
    upstream = out_cotangent.astype(jnp.float32)
    gate_grad = jnp.sum(picked.astype(jnp.float32) * upstream[:, None, :], -1)
    pair_grad = (
        (gates[:, :, None] * upstream[:, None, :]).astype(jnp.bfloat16).reshape(route_total, width)
    )
    send_grads = jnp.where(filled[:, None], pair_grad[source_safe], zero_low)
    arrived_grad = to_experts(send_grads, n_expert, n_tensor, local_experts, capacity)
    down_local = jnp.einsum(
        "abxcf,abxcd->xfd", activated, arrived_grad, preferred_element_type=jnp.float32
    )
    act_grad = jnp.einsum(
        "abxcd,xfd->abxcf", arrived_grad, down_weight, preferred_element_type=jnp.float32
    )
    gate_pre_grad = (
        act_grad * up_pre * sigmoid_gate * (1.0 + gate_pre * (1.0 - sigmoid_gate))
    ).astype(jnp.bfloat16)
    up_pre_grad = (act_grad * silu_gate).astype(jnp.bfloat16)
    gate_local = jnp.einsum(
        "abxcd,abxcf->xdf", arrived, gate_pre_grad, preferred_element_type=jnp.float32
    )
    up_local = jnp.einsum(
        "abxcd,abxcf->xdf", arrived, up_pre_grad, preferred_element_type=jnp.float32
    )
    rows_part = jnp.einsum(
        "abxcf,xdf->abxcd", gate_pre_grad, gate_weight, preferred_element_type=jnp.float32
    )
    rows_part = rows_part + jnp.einsum(
        "abxcf,xdf->abxcd", up_pre_grad, up_weight, preferred_element_type=jnp.float32
    )
    rows_back = to_sources(rows_part, n_expert, n_tensor)
    route_rows = rows_back[slot_of].reshape(tok_local, top_count, width).astype(jnp.float32)
    gate_mean = jnp.sum(gates * gate_grad, -1, keepdims=True)
    chosen_grad = gates * (gate_grad - gate_mean)
    logit_grad = jnp.sum(onehot * chosen_grad[:, :, None], 1)
    router_local = jnp.einsum(
        "td,te->de",
        second_low.astype(jnp.float32),
        logit_grad,
        precision=highest,
        preferred_element_type=jnp.float32,
    )
    normed_back = jnp.sum(route_rows, 1) + jnp.einsum(
        "te,de->td",
        logit_grad,
        router_weight.astype(jnp.float32),
        precision=highest,
        preferred_element_type=jnp.float32,
    )
    residual_back, expert_gain_local = norm_back(residual, second_scale, second_gain, normed_back)
    residual_grad = upstream + residual_back
    group_grad = lax.all_gather(residual_grad.astype(jnp.bfloat16), "tensor", axis=0, tiled=True)
    attended_grad = jnp.einsum(
        "td,hd->th", group_grad, output_weight, preferred_element_type=jnp.float32
    ).astype(jnp.bfloat16)
    attended_grad = attended_grad.reshape(group_len, pair_heads, frequency_ratio, HEAD_SIZE)
    output_local = jnp.einsum("th,td->hd", attended, group_grad, preferred_element_type=jnp.float32)

    def backward_block(carry, pieces):
        key_acc, value_acc = carry
        start, logsum = pieces
        scores, block_query = block_scores(start)
        probs = jnp.exp(scores - logsum[..., None])
        prob_grad = jnp.einsum(
            "qhgd,khd->hgqk", attended_grad, value_low, preferred_element_type=jnp.float32
        )
        value_acc = value_acc + jnp.einsum(
            "hgqk,qhgd->khd",
            probs.astype(jnp.bfloat16),
            attended_grad,
            preferred_element_type=jnp.float32,
        )
        inner = jnp.sum(probs * prob_grad, -1, keepdims=True)
        score_grad = (probs * (prob_grad - inner)).astype(jnp.bfloat16)
        query_turned = (
            jnp.einsum("hgqk,khd->qhgd", score_grad, key_low, preferred_element_type=jnp.float32)
            * scale
        )
        key_acc = (
            key_acc
            + jnp.einsum(
                "hgqk,qhgd->khd", score_grad, block_query, preferred_element_type=jnp.float32
            )
            * scale
        )
        return ((key_acc, value_acc), query_turned)

    zero_keys = jnp.zeros((group_len, pair_heads, HEAD_SIZE), jnp.float32)
    (key_turned, value_acc), query_blocks = lax.scan(
        backward_block, (zero_keys, zero_keys), (starts, logsum_blocks)
    )
    query_turned = query_blocks.reshape(group_len, query_heads, HEAD_SIZE)
    query_back = (
        rotate_back(query_turned, cosine_table, sine_table)
        .astype(jnp.bfloat16)
        .reshape(group_len, query_heads * HEAD_SIZE)
    )
    key_back = (
        rotate_back(key_turned, cosine_table, sine_table)
        .astype(jnp.bfloat16)
        .reshape(group_len, pair_heads * HEAD_SIZE)
    )
    value_back = value_acc.astype(jnp.bfloat16).reshape(group_len, pair_heads * HEAD_SIZE)
    query_local = jnp.einsum(
        "td,th->dh", group_rows, query_back, preferred_element_type=jnp.float32
    )
    key_local = jnp.einsum("td,th->dh", group_rows, key_back, preferred_element_type=jnp.float32)
    value_local = jnp.einsum(
        "td,th->dh", group_rows, value_back, preferred_element_type=jnp.float32
    )
    normed_part = jnp.einsum(
        "th,dh->td", query_back, query_weight, preferred_element_type=jnp.float32
    )
    normed_part = normed_part + jnp.einsum(
        "th,dh->td", key_back, key_matrix, preferred_element_type=jnp.float32
    )
    normed_part = normed_part + jnp.einsum(
        "th,dh->td", value_back, value_matrix, preferred_element_type=jnp.float32
    )
    normed_grad = lax.psum_scatter(
        normed_part.astype(jnp.bfloat16), "tensor", scatter_dimension=0, tiled=True
    ).astype(jnp.float32)
    input_back, attention_gain_local = norm_back(inputs, first_scale, first_gain, normed_grad)
    input_gradient = residual_grad + input_back
    query_gradient, key_gradient, value_gradient, output_gradient = (
        lax.psum(query_local.astype(jnp.bfloat16), ("dp", "expert")).astype(jnp.float32),
        lax.psum(key_local.astype(jnp.bfloat16), ("dp", "expert")).astype(jnp.float32),
        lax.psum(value_local.astype(jnp.bfloat16), ("dp", "expert")).astype(jnp.float32),
        lax.psum(output_local.astype(jnp.bfloat16), ("dp", "expert")).astype(jnp.float32),
    )
    router_gradient, attention_gain_gradient, expert_gain_gradient = lax.psum(
        (router_local, attention_gain_local, expert_gain_local), ("dp", "expert", "tensor")
    )
    gate_gradient, up_gradient, down_gradient = (
        lax.psum(gate_local.astype(jnp.bfloat16), "dp").astype(jnp.float32),
        lax.psum(up_local.astype(jnp.bfloat16), "dp").astype(jnp.float32),
        lax.psum(down_local.astype(jnp.bfloat16), "dp").astype(jnp.float32),
    )
    return (
        layer_output,
        input_gradient,
        attention_gain_gradient,
        query_gradient,
        key_gradient,
        value_gradient,
        output_gradient,
        expert_gain_gradient,
        router_gradient,
        gate_gradient,
        up_gradient,
        down_gradient,
    )


def solution(mesh):
    placed = (
        P(("dp", "expert", "tensor"), None),
        P(("dp", "expert")),
        P(("dp", "expert", "tensor"), None),
        P(),
        P(None, "tensor"),
        P(None, "tensor"),
        P(None, "tensor"),
        P("tensor", None),
        P(),
        P(),
        P("expert", None, "tensor"),
        P("expert", None, "tensor"),
        P("expert", "tensor", None),
        P(("dp", "expert", "tensor"), None),
    )
    return jax.shard_map(
        shards,
        mesh=mesh,
        in_specs=placed,
        out_specs=(
            P(("dp", "expert", "tensor"), None),
            P(("dp", "expert", "tensor"), None),
            P(),
            P(None, "tensor"),
            P(None, "tensor"),
            P(None, "tensor"),
            P("tensor", None),
            P(),
            P(),
            P("expert", None, "tensor"),
            P("expert", None, "tensor"),
            P("expert", "tensor", None),
        ),
        check_vma=False,
    )
```

profile of v0, /device:TPU:1, one launch (start us, length us, event | category | flops | bytes accessed | tf_op | source)
XLA Modules:
  0.0 1637.9 jit_solution(6292448702647533752)
XLA Ops:
  10.5 1.9 fusion.64
  14.7 27.5 %all-gather.3.cloned.1.call-done = bf16[512,1536]{1,0:T(8,128)(2,1)} async-done(((bf16[128,1536]{1,0:T(8,128)(2,1)}), bf16[512,1536]{1,0:T(8,128)(2,1)}) %all-gather.3.cloned.1.call-update) | async-done | bytes 1572880 | tf_op jit(solution)/shard_map/all_gather | solution.py:112
  42.3 2.1 fusion.83
  44.5 2.3 fusion.84
  53.9 2.1 convolution_convert_fusion
  56.6 11.3 reduce-window.6
  68.4 4.6 scatter_custom_fusion
  74.6 6.5 reduce-scatter.3.cloned.1.call-done
  87.3 2.1 fusion.18
  89.4 12.7 gather_fusion.2
  102.1 5.2 gather.20
  107.3 6.1 gather_fusion
  113.4 5.2 gather.17
  118.6 4.0 broadcast_select_fusion
  124.0 206.9 %all_to_all.20 = bf16[32,180,1536]{2,1,0:T(8,128)(2,1)} all-to-all(bf16[32,180,1536]{2,1,0:T(8,128)(2,1)S(1)} %bitcast.209), channel_id=1, replica_groups=mesh['dp'=4,'expert'=8,'tensor'=4] {'expert','tensor'}, dimensions={0} | all-to-all | bytes 35389440 | tf_op jit(solution)/shard_map/all_to_all | solution.py:66
  330.9 6.4 broadcast_in_dim.74
  337.3 5.6 all-to-all-start.2
  342.9 24.0 %reshape.469 = bf16[8,4,5,36,1536]{4,3,2,1,0:T(8,128)(2,1)} reshape(bf16[32,180,1536]{2,1,0:T(8,128)(2,1)} %all_to_all.20) | data formatting | bytes 35389440 | tf_op jit(solution)/shard_map/reshape | solution.py:67
  366.9 11.2 fusion.9
  378.1 11.2 fusion.11
  389.3 193.2 %all-to-all-done.2 = bf16[32,180,1536]{2,1,0:T(8,128)(2,1)} async-done(((bf16[32,180,1536]{2,1,0:T(8,128)(2,1)}), bf16[32,180,1536]{2,1,0:T(8,128)(2,1)}, u32[]{:S(2)}, u32[]{:S(2)}) %all-to-all-start.2) | async-done | bytes 17694752 | tf_op jit(solution)/shard_map/all_to_all | solution.py:66
  582.5 24.0 %reshape.471 = bf16[8,4,5,36,1536]{4,3,2,1,0:T(8,128)(2,1)} reshape(bf16[32,180,1536]{2,1,0:T(8,128)(2,1)} %all-to-all-done.2) | data formatting | bytes 35389440 | tf_op jit(solution)/shard_map/reshape | solution.py:67
  606.5 12.8 fusion.30
  619.3 9.5 convert_bitcast_fusion
  628.7 16.6 %copy.156 = bf16[8,4,5,36,1536]{4,3,2,1,0:T(8,128)(2,1)} copy(bf16[8,4,5,36,1536]{4,3,1,0,2:T(8,128)(2,1)} %convert_bitcast_fusion) | data formatting | bytes 35389440 | tf_op jit(solution)/shard_map/convert_element_type | solution.py:74
  645.3 24.1 %reshape.470 = bf16[32,180,1536]{2,1,0:T(8,128)(2,1)} reshape(bf16[8,4,5,36,1536]{4,3,2,1,0:T(8,128)(2,1)} %copy.156) | data formatting | bytes 35389440 | tf_op jit(solution)/shard_map/convert_element_type | solution.py:74
  669.4 5.2 all-to-all-start.1
  674.6 17.3 %fusion.43 = f32[5,8,4,36,1536]{4,3,2,1,0:T(8,128)} fusion(bf16[8,4,5,36,128]{4,3,1,0,2:T(8,128)(2,1)} %get-tuple-element.85, bf16[5,1536,128]{2,1,0:T(8,128)(2,1)} %param.24), kind=kOutput, calls=%fused_computation.74 | convolution fusion | flops 2264924160 | bytes 38830080 | tf_op jit(solution)/shard_map/abxcf,xdf->abxcd/dot_general | solution.py:232
  691.9 22.4 %fusion.4 = bf16[8,4,5,36,1536]{4,3,1,0,2:T(8,128)(2,1)} fusion(f32[5,8,4,36,1536]{4,3,2,1,0:T(8,128)} %fusion.43, bf16[8,4,5,36,128]{4,3,1,0,2:T(8,128)(2,1)} %get-tuple-element.84, bf16[5,1536,128]{2,1,0:T(8,128)(2,1)S(1)} %copy-done.14), kind=kOutput, calls=%fused_computation.13 | convolution fusion | flops 2282618880 | bytes 56524800 | tf_op jit(solution)/shard_map/abxcf,xdf->abxcd/dot_general | solution.py:235
  714.3 16.6 %copy.159 = bf16[8,4,5,36,1536]{4,3,2,1,0:T(8,128)(2,1)} copy(bf16[8,4,5,36,1536]{4,3,1,0,2:T(8,128)(2,1)} %fusion.4) | data formatting | bytes 35389440 | tf_op jit(solution)/shard_map/convert_element_type | solution.py:74
  730.9 24.1 %reshape.472 = bf16[32,180,1536]{2,1,0:T(8,128)(2,1)} reshape(bf16[8,4,5,36,1536]{4,3,2,1,0:T(8,128)(2,1)} %copy.159) | data formatting | bytes 35389440 | tf_op jit(solution)/shard_map/convert_element_type | solution.py:74
  754.9 157.9 %all-to-all-done.1 = bf16[32,180,1536]{2,1,0:T(8,128)(2,1)} async-done(((bf16[32,180,1536]{2,1,0:T(8,128)(2,1)}), bf16[32,180,1536]{2,1,0:T(8,128)(2,1)}, u32[]{:S(2)}, u32[]{:S(2)}) %all-to-all-start.1) | async-done | bytes 17694752 | tf_op jit(solution)/shard_map/all_to_all | solution.py:73
  912.8 5.0 all-to-all-start.3
  917.9 11.3 bitcast_convert_fusion.1
  929.3 12.3 bitcast_reduce_fusion.1
  941.6 5.2 convert_element_type.223
  946.8 10.2 gather_fusion.1
  957.0 4.8 fusion.14
  962.0 195.5 %all-to-all-done.3 = bf16[32,180,1536]{2,1,0:T(8,128)(2,1)} async-done(((bf16[32,180,1536]{2,1,0:T(8,128)(2,1)}), bf16[32,180,1536]{2,1,0:T(8,128)(2,1)}, u32[]{:S(2)}, u32[]{:S(2)}) %all-to-all-start.3) | async-done | bytes 17694752 | tf_op jit(solution)/shard_map/all_to_all | solution.py:73
  1157.5 12.4 bitcast_reduce_fusion
  1169.9 5.2 convert_element_type.235
  1175.1 10.3 gather_fusion.3
  1185.5 4.0 convert_reduce_fusion
  1192.1 11.4 bitcast_convert_fusion
  1203.5 11.3 bitcast_convert_fusion.2
  1216.4 2.2 convolution_convert_fusion.5
  1218.7 4.3 fusion.15
  1223.4 1.8 fusion.17
  1231.9 1.8 convolution_convert_fusion.1
  1233.7 2.1 convolution_convert_fusion.2
  1236.8 2.3 fusion.86
  1242.1 98.8 %all-reduce.11.cloned.1.call-done = (bf16[5,1536,128]{2,1,0:T(8,128)(2,1)}, bf16[5,1536,128]{2,1,0:T(8,128)(2,1)}, bf16[5,128,1536]{2,1,0:T(8,128)(2,1)}) async-done(((bf16[5,1536,128]{2,1,0:T(8,128)(2,1)}, bf16[5,1536,128]{2,1,0:T(8,128)(2,1)}, bf16[5,128,1536]{2,1,0:T(8,128)(2,1)}), (bf16[5,1536,128]{2,1,0:T(8,128)(2,1)}, bf16[5,1536,128]{2,1,0:T(8,128)(2,1)}, ...) | async-done | bytes 5898256 | tf_op jit(solution)/shard_map/psum | solution.py:342
  1340.9 3.9 convert_element_type.257
  1344.8 2.2 convert_element_type.259
  1347.1 2.5 convert_element_type.261
  1350.6 104.7 %all-reduce.9.cloned.1.call-done = (bf16[1536,384]{1,0:T(8,128)(2,1)}, bf16[1536,128]{1,0:T(8,128)(2,1)}, bf16[1536,128]{1,0:T(8,128)(2,1)}, bf16[384,1536]{1,0:T(8,128)(2,1)}) async-done(((bf16[1536,384]{1,0:T(8,128)(2,1)}, bf16[1536,128]{1,0:T(8,128)(2,1)}, bf16[1536,128]{1,0:T(8,128)(2,1)}, bf16[384,1536]{1,0:T(8,128)(2,1)}), (bf16[1536,384]{1,0:T(8,128)(2,1)}, bf16[1536,128]{1,0:T(8,128)(2,1)}, ...) | async-done | bytes 3145744 | tf_op jit(solution)/shard_map/psum | solution.py:333
  1455.3 2.0 convert_element_type.251
  1457.3 1.9 convert_element_type.253
  1459.3 2.9 convert_element_type.249
  1463.8 18.0 %reduce-scatter.5.cloned.1.call-done = bf16[128,1536]{1,0:T(8,128)(2,1)} async-done(((bf16[512,1536]{1,0:T(8,128)(2,1)}), bf16[128,1536]{1,0:T(8,128)(2,1)}) %reduce-scatter.5.cloned.1.call-update) | async-done | bytes 393232 | tf_op jit(solution)/shard_map/reduce_scatter | solution.py:327
  1481.8 1.9 fusion.68
  1483.7 3.0 fusion.61
  1486.6 66.6 %all-reduce = (f32[1536]{0:T(1024)}, f32[1536]{0:T(1024)}) all-reduce(f32[1536]{0:T(1024)} %get-tuple-element.62, f32[1536]{0:T(1024)} %get-tuple-element.60), channel_id=1, replica_groups=mesh['dp'=4,'expert'=8,'tensor'=4] {'dp','expert','tensor'}, use_global_device_ids=true, to_apply=%region_25.26 | all-reduce | flops 3072 | bytes 24576 | tf_op jit(solution)/shard_map/psum | solution.py:338
  1553.3 75.9 %all-reduce.7.cloned.1.call-done = f32[1536,40]{0,1:T(8,128)} async-done(((f32[1536,40]{0,1:T(8,128)}), f32[1536,40]{0,1:T(8,128)}) %all-reduce.7.cloned.1.call-update) | async-done | bytes 245776 | tf_op jit(solution)/shard_map/psum | solution.py:338
  (256 shorter events, 42.2 us)
Async XLA Ops:
  7.2 599.3 %copy-start = (bf16[5,128,1536]{2,1,0:T(8,128)(2,1)S(1)}, bf16[5,128,1536]{2,1,0:T(8,128)(2,1)}, u32[]{:S(2)}) copy-start(bf16[5,128,1536]{2,1,0:T(8,128)(2,1)} %param.26) | copy-start | bytes 5898244
  7.2 37.2 %copy-start.33 = (bf16[1536,384]{1,0:T(8,128)(2,1)S(1)}, bf16[1536,384]{1,0:T(8,128)(2,1)}, u32[]{:S(2)}) copy-start(bf16[1536,384]{1,0:T(8,128)(2,1)} %param.18) | copy-start | bytes 3538948
  7.2 35.0 %all-gather.3.cloned.1.call-start = ((), (), s32[]{:S(2)}) async-start(), calls=%async_computation.6 | async-start | bytes 1966080 | tf_op jit(solution)/shard_map/all_gather | solution.py:112
  12.4 68.6 %reduce-scatter.3.cloned.1.call-start = ((), (), s32[]{:S(2)}) async-start(), calls=%async_computation.7 | async-start | bytes 1966080 | tf_op jit(solution)/shard_map/reduce_scatter | solution.py:163
  13.7 33.0 %copy-start.20 = (f32[512,32]{0,1:T(8,128)}, f32[512,32]{0,1:T(8,128)S(1)}, u32[]{:S(2)}) copy-start(f32[512,32]{0,1:T(8,128)S(1)} %get-tuple-element.99) | copy-start | bytes 196612
  13.7 33.0 %copy-start.22 = (f32[512,32]{0,1:T(8,128)}, f32[512,32]{0,1:T(8,128)S(1)}, u32[]{:S(2)}) copy-start(f32[512,32]{0,1:T(8,128)S(1)} %get-tuple-element.100) | copy-start | bytes 196612
  44.4 3.7 copy-start.49
  44.4 3.7 copy-start.51
  48.2 3.7 copy-start.4
  48.2 3.7 copy-start.62
  48.2 3.0 copy-start.25
  53.1 3.0 copy-start.66
  53.1 3.2 copy-start.78
  53.9 19.9 %copy-start.12 = (bf16[128,1536]{1,0:T(8,128)(2,1)S(1)}, bf16[128,1536]{1,0:T(8,128)(2,1)}, u32[]{:S(2)}) copy-start(bf16[128,1536]{1,0:T(8,128)(2,1)} %param.27) | copy-start | bytes 1179652
  53.9 27.2 %copy-start.5 = (bf16[128,1536]{1,0:T(8,128)(2,1)S(1)}, bf16[128,1536]{1,0:T(8,128)(2,1)}, u32[]{:S(2)}) copy-start(bf16[128,1536]{1,0:T(8,128)(2,1)} %param.14) | copy-start | bytes 1179652
  56.3 33.0 %copy-start.53 = (f32[1536]{0:T(1024)}, f32[1536]{0:T(1024)S(1)}, u32[]{:S(2)}) copy-start(f32[1536]{0:T(1024)S(1)} %convert_element_type.215) | copy-start | bytes 18436
  68.4 4.7 copy-start.68
  73.8 15.6 copy-start.10
  83.9 23.4 %copy-start.2 = (bf16[128,1536]{1,0:T(8,128)(2,1)}, bf16[128,1536]{1,0:T(8,128)(2,1)S(1)}, u32[]{:S(2)}) copy-start(bf16[128,1536]{1,0:T(8,128)(2,1)S(1)} %multiply_convert_fusion) | copy-start | bytes 1179652
  87.2 14.9 copy-start.42
  113.4 5.2 copy-start.74
  337.3 245.2 %all-to-all-start.2 = ((bf16[32,180,1536]{2,1,0:T(8,128)(2,1)}), bf16[32,180,1536]{2,1,0:T(8,128)(2,1)}, u32[]{:S(2)}, u32[]{:S(2)}) async-start(bf16[32,180,1536]{2,1,0:T(8,128)(2,1)} %bitcast.208), calls=%async_computation.3 | async-start | bytes 36175872 | tf_op jit(solution)/shard_map/all_to_all | solution.py:66
  366.9 11.2 copy-start.17
  619.3 9.5 copy-start.19
  669.4 243.4 %all-to-all-start.1 = ((bf16[32,180,1536]{2,1,0:T(8,128)(2,1)}), bf16[32,180,1536]{2,1,0:T(8,128)(2,1)}, u32[]{:S(2)}, u32[]{:S(2)}) async-start(bf16[32,180,1536]{2,1,0:T(8,128)(2,1)} %reshape.470), calls=%async_computation.2 | async-start | bytes 36175872 | tf_op jit(solution)/shard_map/all_to_all | solution.py:73
  674.6 17.3 %copy-start.14 = (bf16[5,1536,128]{2,1,0:T(8,128)(2,1)S(1)}, bf16[5,1536,128]{2,1,0:T(8,128)(2,1)}, u32[]{:S(2)}) copy-start(bf16[5,1536,128]{2,1,0:T(8,128)(2,1)} %param.25) | copy-start | bytes 5898244
  754.9 163.0 %copy-start.69 = (s32[1024,1]{0,1:T(1,128)S(1)}, s32[1024,1]{0,1:T(1,128)}, u32[]{:S(2)}) copy-start(s32[1024,1]{0,1:T(1,128)} %copy-done.68) | copy-start | bytes 12292
  754.9 163.0 %copy-start.18 = (bf16[8,4,5,36,128]{4,3,1,0,2:T(8,128)(2,1)S(1)}, bf16[8,4,5,36,128]{4,3,1,0,2:T(8,128)(2,1)}, u32[]{:S(2)}) copy-start(bf16[8,4,5,36,128]{4,3,1,0,2:T(8,128)(2,1)} %get-tuple-element.84) | copy-start | bytes 4423684
  912.8 244.7 %all-to-all-start.3 = ((bf16[32,180,1536]{2,1,0:T(8,128)(2,1)}), bf16[32,180,1536]{2,1,0:T(8,128)(2,1)}, u32[]{:S(2)}, u32[]{:S(2)}) async-start(bf16[32,180,1536]{2,1,0:T(8,128)(2,1)} %reshape.472), calls=%async_computation.4 | async-start | bytes 36175872 | tf_op jit(solution)/shard_map/all_to_all | solution.py:73
  917.8 298.6 %all-gather.5.cloned.1.call-start = ((), (), s32[]{:S(2)}) async-start(), calls=%async_computation.8 | async-start | bytes 1966080 | tf_op jit(solution)/shard_map/all_gather | solution.py:259
  946.8 10.2 copy-start.11
  946.8 10.2 copy-start.43
  957.0 4.9 copy-start.59
  957.0 4.9 copy-start.71
  957.0 4.9 copy-start.76
  957.0 4.9 copy-start.67
  962.0 227.5 %copy-start.56 = (f32[128,40]{0,1:T(8,128)}, f32[128,40]{0,1:T(8,128)S(1)}, u32[]{:S(2)}) copy-start(f32[128,40]{0,1:T(8,128)S(1)} %select_reduce_fusion) | copy-start | bytes 61444
  1185.4 4.1 copy-start.6
  1185.4 4.1 copy-start.9
  1185.4 4.1 copy-start.46
  1185.4 4.1 copy-start.54
  1185.4 4.1 copy-start.73
  1185.4 5.4 copy-start.13
  1185.5 5.4 copy-start.79
  1192.0 11.5 copy-start.24
  1192.0 148.9 %all-reduce.11.cloned.1.call-start = ((), (), s32[]{:S(2)}) async-start(), calls=%async_computation.12 | async-start | bytes 11796480 | tf_op jit(solution)/shard_map/psum | solution.py:342
  1214.9 3.8 copy-start.45
  1214.9 240.4 %all-reduce.9.cloned.1.call-start = ((), (), s32[]{:S(2)}) async-start(), calls=%async_computation.11 | async-start | bytes 6291456 | tf_op jit(solution)/shard_map/psum | solution.py:333
  1218.7 4.3 slice-start
  1218.7 4.7 slice-start.1
  1226.4 4.1 copy-start.36
  1227.3 6.5 copy-start.27
  1228.4 5.3 copy-start.34
  1228.4 3.5 copy-start.48
  1228.4 3.5 copy-start.81
  1235.8 3.3 copy-start.29
  1235.8 3.3 copy-start.37
  1235.8 246.0 %reduce-scatter.5.cloned.1.call-start = ((), (), s32[]{:S(2)}) async-start(), calls=%async_computation.9 | async-start | bytes 1966080 | tf_op jit(solution)/shard_map/reduce_scatter | solution.py:327
  1241.9 387.3 %all-reduce.7.cloned.1.call-start = ((), (), s32[]{:S(2)}) async-start(), calls=%async_computation.10 | async-start | bytes 491520 | tf_op jit(solution)/shard_map/psum | solution.py:338
  1340.9 3.9 copy-start.16
  1455.3 6.8 copy-start.32
  1459.3 22.6 %copy-start.61 = (f32[1536]{0:T(1024)S(1)}, f32[1536]{0:T(1024)}, u32[]{:S(2)}) copy-start(f32[1536]{0:T(1024)} %copy-done.60) | copy-start | bytes 18436
  1459.3 24.4 %copy-start.55 = (f32[1536]{0:T(1024)S(1)}, f32[1536]{0:T(1024)}, u32[]{:S(2)}) copy-start(f32[1536]{0:T(1024)} %copy-done.53) | copy-start | bytes 18436
  1462.1 168.7 %copy-start.1 = (bf16[5,128,1536]{2,1,0:T(8,128)(2,1)S(1)}, bf16[5,128,1536]{2,1,0:T(8,128)(2,1)}, u32[]{:S(2)}) copy-start(bf16[5,128,1536]{2,1,0:T(8,128)(2,1)} %param.26) | copy-start | bytes 5898244
  (30 other events, 41.2 us)
Sparse Core Ops, SparseCore 0:
  12.5 29.6 all-gather.2
  56.2 24.8 reduce-scatter.2
  1192.2 24.2 all-gather.4
  1220.0 120.9 all-reduce.10
  1345.1 110.1 all-reduce.8
  1457.6 24.1 reduce-scatter.4
  1487.1 141.9 all-reduce.6
where the time goes:
time: 1650 us; the launch traced here: 1640 us
  waiting for transfers between devices  879 us (53%)
  blocking collectives  274 us (17%)
  local copies, waits for them, and re-layouts  213 us (13%)
  matrix products  152 us (9%)
  other arithmetic  88.5 us (5%)
  starting transfers between devices  16.7 us (1%)
    all_to_all x2, waiting for transfers between devices, to_sources(): lax.all_to_all(sent.astype(jnp.bfloat16), ('expert', 'tensor'), split_axi...  353 us
    all_to_all x1, blocking collectives, to_experts(): lax.all_to_all(copies, ('expert', 'tensor'), split_axis=0, concat_axis=0,...  207 us
    all_to_all x1, waiting for transfers between devices, to_experts(): lax.all_to_all(copies, ('expert', 'tensor'), split_axis=0, concat_axis=0,...  193 us
    psum x1, waiting for transfers between devices, shards(): lax.psum(query_local.astype(jnp.bfloat16), ('dp', 'expert'))  105 us
    psum x1, waiting for transfers between devices, shards(): lax.psum(gate_local.astype(jnp.bfloat16), 'dp').astype(jnp.float32)  98.8 us
    convert_element_type x4, local copies, waits for them, and re-layouts, to_sources(): sent.astype(jnp.bfloat16)  81.3 us
    psum x1, waiting for transfers between devices, shards(): lax.psum((router_local, attention_gain_local, expert_gain_local), ('dp',...  75.9 us
    psum x1, blocking collectives, shards(): lax.psum((router_local, attention_gain_local, expert_gain_local), ('dp',...  66.6 us
  transfers between devices with their start and end apart: 10, of which 10 were waited for; matrix products, arithmetic and copies ran while one was open for 16% of the time, Pallas kernels for 0%

commit v1 on v0

--- a/solution.py
+++ b/solution.py
@@ -6,7 +6,6 @@
 from jax.sharding import PartitionSpec as P
 
 HEAD_SIZE = 64
-CAP = 36
 
 
 epsilon = 1e-06
@@ -54,27 +53,6 @@
     return jnp.concatenate(
         [first * cosine_table + second * sine_table, second * cosine_table - first * sine_table], -1
     )
-
-
-def to_experts(own, n_expert, n_tensor, local_experts, capacity):
-    width = own.shape[-1]
-    by_owner = own.reshape(n_expert, local_experts * capacity, width)
-    copies = jnp.broadcast_to(
-        by_owner[:, None], (n_expert, n_tensor, local_experts * capacity, width)
-    )
-    copies = copies.reshape(n_expert * n_tensor, local_experts * capacity, width)
-    arrived = lax.all_to_all(copies, ("expert", "tensor"), split_axis=0, concat_axis=0, tiled=True)
-    return arrived.reshape(n_expert, n_tensor, local_experts, capacity, width)
-
-
-def to_sources(partial_value, n_expert, n_tensor):
-    width = partial_value.shape[-1]
-    sent = partial_value.reshape(n_expert * n_tensor, -1, width)
-    arrived = lax.all_to_all(
-        sent.astype(jnp.bfloat16), ("expert", "tensor"), split_axis=0, concat_axis=0, tiled=True
-    ).astype(sent.dtype)
-    summed = jnp.sum(arrived.reshape(n_expert, n_tensor, -1, width), 1)
-    return summed.astype(jnp.bfloat16).reshape(-1, width)
 
 
 def shards(
@@ -103,8 +81,6 @@
     frequency_ratio = query_heads // pair_heads
     local_experts = gate_weight.shape[0]
     experts_all = router_weight.shape[1]
-    top_count = expert_routes.shape[1]
-    capacity = CAP
     scale = 1.0 / math.sqrt(HEAD_SIZE)
     inputs = tokens.astype(jnp.float32)
     first_gain = attention_gain.astype(jnp.float32)
@@ -167,79 +143,82 @@
     second_gain = expert_gain.astype(jnp.float32)
     second_normed, second_scale = normalize(residual, second_gain)
     second_low = second_normed.astype(jnp.bfloat16)
-    logits = jnp.dot(second_low, router_weight, preferred_element_type=jnp.float32)
-    onehot = (
-        expert_routes[:, :, None] == jnp.arange(experts_all, dtype=jnp.int32)[None, None, :]
-    ).astype(jnp.float32)
-    chosen = jnp.sum(onehot * logits[:, None, :], -1)
-    chosen_exp = jnp.exp(chosen - jnp.max(chosen, -1, keepdims=True))
-    gates = chosen_exp / jnp.sum(chosen_exp, -1, keepdims=True)
-    flat_routes = expert_routes.reshape(-1)
-    route_total = flat_routes.shape[0]
-    flat_hot = (flat_routes[:, None] == jnp.arange(experts_all, dtype=jnp.int32)[None, :]).astype(
-        jnp.int32
-    )
-    rank = jnp.sum((jnp.cumsum(flat_hot, 0) - 1) * flat_hot, 1)
-    slot_of = flat_routes * capacity + rank
-    source_of = (
-        jnp.full((experts_all * capacity,), route_total, jnp.int32)
-        .at[slot_of]
-        .set(jnp.arange(route_total, dtype=jnp.int32))
-    )
-    filled = source_of < route_total
-    source_safe = jnp.minimum(source_of, route_total - 1)
-    token_of = source_safe // top_count
-    zero_low = jnp.zeros((), jnp.bfloat16)
-    send_rows = jnp.where(filled[:, None], second_low[token_of], zero_low)
-    arrived = to_experts(send_rows, n_expert, n_tensor, local_experts, capacity)
-    gate_pre = jnp.einsum(
-        "abxcd,xdf->abxcf", arrived, gate_weight, preferred_element_type=jnp.float32
-    )
-    up_pre = jnp.einsum("abxcd,xdf->abxcf", arrived, up_weight, preferred_element_type=jnp.float32)
+    plane = ("expert", "tensor")
+    experts_index = jnp.arange(experts_all, dtype=jnp.int32)
+    plane_routes = lax.all_gather(expert_routes, plane, axis=0, tiled=True)
+    plane_upstream = lax.all_gather(out_cotangent, plane, axis=0, tiled=True)
+    plane_rows = lax.all_gather(second_low, plane, axis=0, tiled=True)
+
+    def dense_gates(rows, routes):
+        named = jnp.any(routes[:, :, None] == experts_index[None, None, :], 1)
+        logits = jnp.dot(rows, router_weight, preferred_element_type=jnp.float32)
+        logits = jnp.where(named, logits, -1e30)
+        raised = jnp.exp(logits - jnp.max(logits, -1, keepdims=True))
+        return raised / jnp.sum(raised, -1, keepdims=True)
+
+    first_expert = lax.axis_index("expert") * local_experts
+    plane_gates = lax.dynamic_slice_in_dim(
+        dense_gates(plane_rows, plane_routes), first_expert, local_experts, 1
+    )
+    plane_len = plane_rows.shape[0]
+    hidden = gate_weight.shape[2]
+    wide = local_experts * hidden
+    gate_flat = gate_weight.transpose(1, 0, 2).reshape(width, wide)
+    up_flat = up_weight.transpose(1, 0, 2).reshape(width, wide)
+    down_flat = down_weight.reshape(wide, width)
+    gate_pre = jnp.dot(plane_rows, gate_flat, preferred_element_type=jnp.float32)
+    up_pre = jnp.dot(plane_rows, up_flat, preferred_element_type=jnp.float32)
+    raw_grad = jnp.einsum(
+        "td,fd->tf", plane_upstream, down_flat, preferred_element_type=jnp.float32
+    )
+    gates_wide = jnp.repeat(plane_gates, hidden, axis=1)
     sigmoid_gate = jax.nn.sigmoid(gate_pre)
     silu_gate = gate_pre * sigmoid_gate
-    activated = (silu_gate * up_pre).astype(jnp.bfloat16)
-    down_part = jnp.einsum(
-        "abxcf,xfd->abxcd", activated, down_weight, preferred_element_type=jnp.float32
-    )
-    returned = to_sources(down_part, n_expert, n_tensor)
-    picked = returned[slot_of].reshape(tok_local, top_count, width)
-    mixture = jnp.sum(gates[:, :, None] * picked.astype(jnp.float32), 1)
-    layer_output = (residual + mixture).astype(jnp.bfloat16)
-    upstream = out_cotangent.astype(jnp.float32)
-    gate_grad = jnp.sum(picked.astype(jnp.float32) * upstream[:, None, :], -1)
-    pair_grad = (
-        (gates[:, :, None] * upstream[:, None, :]).astype(jnp.bfloat16).reshape(route_total, width)
-    )
-    send_grads = jnp.where(filled[:, None], pair_grad[source_safe], zero_low)
-    arrived_grad = to_experts(send_grads, n_expert, n_tensor, local_experts, capacity)
-    down_local = jnp.einsum(
-        "abxcf,abxcd->xfd", activated, arrived_grad, preferred_element_type=jnp.float32
-    )
-    act_grad = jnp.einsum(
-        "abxcd,xfd->abxcf", arrived_grad, down_weight, preferred_element_type=jnp.float32
-    )
+    activated = silu_gate * up_pre
+    gate_grad_part = jnp.sum(
+        (activated * raw_grad).reshape(plane_len, local_experts, hidden), -1
+    )
+    gated = (gates_wide * activated).astype(jnp.bfloat16)
+    act_grad = gates_wide * raw_grad
     gate_pre_grad = (
         act_grad * up_pre * sigmoid_gate * (1.0 + gate_pre * (1.0 - sigmoid_gate))
     ).astype(jnp.bfloat16)
     up_pre_grad = (act_grad * silu_gate).astype(jnp.bfloat16)
-    gate_local = jnp.einsum(
-        "abxcd,abxcf->xdf", arrived, gate_pre_grad, preferred_element_type=jnp.float32
-    )
-    up_local = jnp.einsum(
-        "abxcd,abxcf->xdf", arrived, up_pre_grad, preferred_element_type=jnp.float32
-    )
+    mixture_part = jnp.dot(gated, down_flat, preferred_element_type=jnp.float32)
+    mixture = lax.psum_scatter(
+        mixture_part.astype(jnp.bfloat16), plane, scatter_dimension=0, tiled=True
+    ).astype(jnp.float32)
+    layer_output = (residual + mixture).astype(jnp.bfloat16)
     rows_part = jnp.einsum(
-        "abxcf,xdf->abxcd", gate_pre_grad, gate_weight, preferred_element_type=jnp.float32
-    )
-    rows_part = rows_part + jnp.einsum(
-        "abxcf,xdf->abxcd", up_pre_grad, up_weight, preferred_element_type=jnp.float32
-    )
-    rows_back = to_sources(rows_part, n_expert, n_tensor)
-    route_rows = rows_back[slot_of].reshape(tok_local, top_count, width).astype(jnp.float32)
+        "tf,df->td", gate_pre_grad, gate_flat, preferred_element_type=jnp.float32
+    ) + jnp.einsum("tf,df->td", up_pre_grad, up_flat, preferred_element_type=jnp.float32)
+    route_rows = lax.psum_scatter(
+        rows_part.astype(jnp.bfloat16), plane, scatter_dimension=0, tiled=True
+    ).astype(jnp.float32)
+    down_local = jnp.einsum(
+        "tf,td->fd", gated, plane_upstream, preferred_element_type=jnp.float32
+    ).reshape(local_experts, hidden, width)
+    gate_local = (
+        jnp.einsum("td,tf->df", plane_rows, gate_pre_grad, preferred_element_type=jnp.float32)
+        .reshape(width, local_experts, hidden)
+        .transpose(1, 0, 2)
+    )
+    up_local = (
+        jnp.einsum("td,tf->df", plane_rows, up_pre_grad, preferred_element_type=jnp.float32)
+        .reshape(width, local_experts, hidden)
+        .transpose(1, 0, 2)
+    )
+    sent_grads = gate_grad_part.reshape(n_expert * n_tensor, tok_local, local_experts)
+    come_grads = lax.all_to_all(sent_grads, plane, split_axis=0, concat_axis=0, tiled=True)
+    gate_grad = (
+        jnp.sum(come_grads.reshape(n_expert, n_tensor, tok_local, local_experts), 1)
+        .transpose(1, 0, 2)
+        .reshape(tok_local, experts_all)
+    )
+    gates = dense_gates(second_low, expert_routes)
+    upstream = out_cotangent.astype(jnp.float32)
     gate_mean = jnp.sum(gates * gate_grad, -1, keepdims=True)
-    chosen_grad = gates * (gate_grad - gate_mean)
-    logit_grad = jnp.sum(onehot * chosen_grad[:, :, None], 1)
+    logit_grad = gates * (gate_grad - gate_mean)
     router_local = jnp.einsum(
         "td,te->de",
         second_low.astype(jnp.float32),
@@ -247,7 +226,7 @@
         precision=highest,
         preferred_element_type=jnp.float32,
     )
-    normed_back = jnp.sum(route_rows, 1) + jnp.einsum(
+    normed_back = route_rows + jnp.einsum(
         "te,de->td",
         logit_grad,
         router_weight.astype(jnp.float32),

time: 1650 us -> 953 us (0.58)
  waiting for transfers between devices: 879 us -> 557 us
  local copies, waits for them, and re-layouts: 213 us -> 23.6 us
  blocking collectives: 274 us -> 105 us
  other arithmetic: 88.5 us -> 47.2 us
  matrix products: 152 us -> 189 us
    all_to_all x3 -> x1, waiting for transfers between devices: 547 us -> 0.01 us  [shards(): lax.all_to_all(sent_grads, plane, split_axis=0, concat_axis=0, tiled=True)]
    all_to_all x1 -> x0, blocking collectives: 207 us -> none  [to_experts(): lax.all_to_all(copies, ('expert', 'tensor'), split_axis=0, concat_axis=0,...]
    reduce_scatter x0 -> x2, waiting for transfers between devices: none -> 177 us  [the longest x1 107 us: shards(): lax.psum_scatter(mixture_part.astype(jnp.bfloat16), plane, scatter_dimens...]
    convert_element_type x6 -> x2, local copies, waits for them, and re-layouts: 91.7 us -> 7.94 us  [the longest x1 3.97 us: shards(): up_local.astype(jnp.bfloat16)]
    all_gather x0 -> x2, waiting for transfers between devices: none -> 49.9 us  [the longest x1 33.8 us: shards(): plane_upstream = lax.all_gather(out_cotangent, plane, axis=0, tiled=True)]
    gather x6 -> x0, local copies, waits for them, and re-layouts: 49.7 us -> none  [the longest x2 17.9 us: shards(): send_grads = jnp.where(filled[:, None], pair_grad[source_safe], zero_low)]
    reshape x2 -> x1, local copies, waits for them, and re-layouts: 48 us -> 1.37 us  [shards(): gate_grad = jnp.sum(come_grads.reshape(n_expert, n_tensor, tok_local, loc...]
    all_gather x0 -> x1, blocking collectives: none -> 39.2 us  [shards(): plane_routes = lax.all_gather(expert_routes, plane, axis=0, tiled=True)]
  transfers between devices with their start and end apart: 10 -> 12, of which waited for: 10 -> 10; matrix products, arithmetic and copies ran while one was open for 16% -> 18% of each run, Pallas kernels for 0% -> 0%
where the time goes in v1:
time: 953 us; the launch traced here: 944 us
  waiting for transfers between devices  557 us (58%)
  matrix products  189 us (20%)
  blocking collectives  105 us (11%)
  other arithmetic  47.2 us (5%)
  local copies, waits for them, and re-layouts  23.6 us (2%)
  between operations  14.9 us (2%)
    reduce_scatter x1, waiting for transfers between devices, shards(): lax.psum_scatter(mixture_part.astype(jnp.bfloat16), plane, scatter_dimens...  107 us
    psum x1, waiting for transfers between devices, shards(): lax.psum(query_local.astype(jnp.bfloat16), ('dp', 'expert'))  106 us
    psum x1, waiting for transfers between devices, shards(): lax.psum((router_local, attention_gain_local, expert_gain_local), ('dp',...  78.2 us
    psum x1, waiting for transfers between devices, shards(): lax.psum(gate_local.astype(jnp.bfloat16), 'dp').astype(jnp.float32)  73.6 us
    reduce_scatter x1, waiting for transfers between devices, shards(): lax.psum_scatter(rows_part.astype(jnp.bfloat16), plane, scatter_dimension...  70.3 us
    psum x1, blocking collectives, shards(): lax.psum((router_local, attention_gain_local, expert_gain_local), ('dp',...  65.6 us
    all_gather x1, blocking collectives, shards(): plane_routes = lax.all_gather(expert_routes, plane, axis=0, tiled=True)  39.2 us
    all_gather x1, waiting for transfers between devices, shards(): plane_upstream = lax.all_gather(out_cotangent, plane, axis=0, tiled=True)  33.8 us
  transfers between devices with their start and end apart: 12, of which 10 were waited for; matrix products, arithmetic and copies ran while one was open for 18% of the time, Pallas kernels for 0%

profile of v1, /device:TPU:1, one launch (start us, length us, event | category | flops | bytes accessed | tf_op | source)
XLA Modules:
  0.0 943.6 jit_solution(15629976770753677491)
XLA Ops:
  7.3 1.3 fusion.26
  9.8 1.9 fusion.28
  13.1 1.0 fusion.22
  14.1 27.5 %all-gather.5.cloned.1.call-done = bf16[512,1536]{1,0:T(8,128)(2,1)} async-done(((bf16[128,1536]{1,0:T(8,128)(2,1)}), bf16[512,1536]{1,0:T(8,128)(2,1)}) %all-gather.5.cloned.1.call-update) | async-done | bytes 1572880 | tf_op jit(solution)/shard_map/all_gather | solution.py:88
  41.6 2.7 fusion.48
  45.2 1.2 fusion.44
  48.1 1.2 fusion.13
  50.1 2.1 convolution_convert_fusion.4
  52.4 24.8 %reduce-scatter.5.cloned.1.call-done = bf16[128,1536]{1,0:T(8,128)(2,1)} async-done(((bf16[512,1536]{1,0:T(8,128)(2,1)}), bf16[128,1536]{1,0:T(8,128)(2,1)}) %reduce-scatter.5.cloned.1.call-update) | async-done | bytes 393232 | tf_op jit(solution)/shard_map/reduce_scatter | solution.py:139
  77.2 1.2 multiply_reduce_fusion.2
  79.0 1.9 multiply_convert_fusion.2
  81.5 4.0 copy.56
  85.5 4.0 copy.57
  89.5 39.2 %all_gather.16 = s32[4096,8]{0,1:T(8,128)S(1)} all-gather(s32[128,8]{0,1:T(8,128)S(1)} %copy-done.48), channel_id=1, replica_groups=mesh['dp'=4,'expert'=8,'tensor'=4] {'expert','tensor'}, dimensions={0}, use_global_device_ids=true | all-gather | bytes 135168 | tf_op jit(solution)/shard_map/all_gather | solution.py:148
  129.5 16.0 %all-gather.7.cloned.1.call-done = bf16[4096,1536]{1,0:T(8,128)(2,1)} async-done(((bf16[128,1536]{1,0:T(8,128)(2,1)}), bf16[4096,1536]{1,0:T(8,128)(2,1)}) %all-gather.7.cloned.1.call-update) | async-done | bytes 12582928 | tf_op jit(solution)/shard_map/all_gather | solution.py:150
  145.6 8.5 fusion.45
  154.3 11.1 %fusion.49 = f32[4096,640]{0,1:T(8,128)} fusion(bf16[4096,1536]{1,0:T(8,128)(2,1)S(1)} %copy-done.5, bf16[1536,640]{0,1:T(8,128)(2,1)S(1)} %bitcast.147), kind=kOutput, calls=%fused_computation.119 | convolution fusion | flops 8053063680 | bytes 25034752 | tf_op jit(solution)/shard_map/dot_general | solution.py:169
  165.4 10.8 %fusion.50 = f32[4096,640]{0,1:T(8,128)} fusion(bf16[4096,1536]{1,0:T(8,128)(2,1)S(1)} %copy-done.5, bf16[1536,640]{0,1:T(8,128)(2,1)S(1)} %bitcast.146), kind=kOutput, calls=%fused_computation.120 | convolution fusion | flops 8053063680 | bytes 25034752 | tf_op jit(solution)/shard_map/dot_general | solution.py:170
  176.2 33.8 %all-gather.9.cloned.1.call-done = bf16[4096,1536]{1,0:T(8,128)(2,1)} async-done(((bf16[128,1536]{1,0:T(8,128)(2,1)}), bf16[4096,1536]{1,0:T(8,128)(2,1)}) %all-gather.9.cloned.1.call-update) | async-done | bytes 12582928 | tf_op jit(solution)/shard_map/all_gather | solution.py:149
  210.0 30.1 %multiply_multiply_fusion = (f32[4096,640]{0,1:T(8,128)}, bf16[4096,640]{0,1:T(8,128)(2,1)S(1)}, bf16[4096,640]{0,1:T(8,128)(2,1)}, bf16[4096,640]{0,1:T(8,128)(2,1)}) fusion(f32[4096,640]{0,1:T(8,128)} %fusion.50, f32[4096,640]{0,1:T(8,128)} %fusion.49, f32[4096,5]{0,1:T(8,128)S(1)} %dynamic-slice_divide_fusion, ...), kind=kOutput, calls=%fused_computation.22 | convolution fusion | flops 8100249600 | bytes 61816832 | tf_op jit(solution)/shard_map/td,fd->tf/dot_general | solution.py:171
  240.2 13.5 %fusion.51 = f32[4096,1536]{1,0:T(8,128)} fusion(bf16[4096,640]{0,1:T(8,128)(2,1)S(1)} %get-tuple-element.85, bf16[1536,640]{0,1:T(8,128)(2,1)S(1)} %bitcast.148), kind=kOutput, calls=%fused_computation.121 | convolution fusion | flops 8053063680 | bytes 32374784 | tf_op jit(solution)/shard_map/tf,df->td/dot_general | solution.py:192
  253.6 19.8 %add_convert_fusion = bf16[4096,1536]{1,0:T(8,128)(2,1)} fusion(f32[4096,1536]{1,0:T(8,128)} %fusion.51, bf16[4096,640]{0,1:T(8,128)(2,1)} %get-tuple-element.87, bf16[1536,640]{0,1:T(8,128)(2,1)} %bitcast.145), kind=kOutput, calls=%fused_computation | convolution fusion | flops 8065646592 | bytes 44957696 | tf_op jit(solution)/shard_map/tf,df->td/dot_general | solution.py:194
  275.9 5.3 reduce_sum.134
  281.2 5.5 all-to-all-start
  286.8 14.6 %convolution_convert_fusion.2 = bf16[1536,640]{0,1:T(8,128)(2,1)} fusion(bf16[4096,640]{0,1:T(8,128)(2,1)} %copy-done.8, bf16[4096,1536]{1,0:T(8,128)(2,1)} %all-gather.7.cloned.1.call-done), kind=kOutput, calls=%fused_computation.27 | convolution fusion | flops 8054046720 | bytes 19791872 | tf_op jit(solution)/shard_map/td,tf->df/dot_general | solution.py:202
  301.4 1.6 bitcast_reduce_fusion
  303.0 1.4 reshape.226
  304.3 1.4 multiply_reduce_fusion.3
  305.7 70.3 %reduce-scatter.9.cloned.1.call-done = bf16[128,1536]{1,0:T(8,128)(2,1)} async-done(((bf16[4096,1536]{1,0:T(8,128)(2,1)}), bf16[128,1536]{1,0:T(8,128)(2,1)}) %reduce-scatter.9.cloned.1.call-update) | async-done | bytes 393232 | tf_op jit(solution)/shard_map/reduce_scatter | solution.py:195
  375.9 2.5 multiply_reduce_fusion
  379.4 1.8 fusion.42
  381.2 14.1 %convolution_convert_fusion.1 = bf16[1536,640]{0,1:T(8,128)(2,1)} fusion(bf16[4096,640]{0,1:T(8,128)(2,1)} %get-tuple-element.87, bf16[4096,1536]{1,0:T(8,128)(2,1)} %all-gather.7.cloned.1.call-done), kind=kOutput, calls=%fused_computation.26 | convolution fusion | flops 8054046720 | bytes 19791872 | tf_op jit(solution)/shard_map/td,tf->df/dot_general | solution.py:207
  395.3 4.0 copy.62
  399.3 4.0 copy.63
  403.3 13.7 %convolution_convert_fusion.3 = bf16[640,1536]{1,0:T(8,128)(2,1)} fusion(bf16[4096,640]{0,1:T(8,128)(2,1)} %get-tuple-element.86, bf16[4096,1536]{1,0:T(8,128)(2,1)} %all-gather.9.cloned.1.call-done), kind=kOutput, calls=%fused_computation.28 | convolution fusion | flops 8054046720 | bytes 19791872 | tf_op jit(solution)/shard_map/tf,td->fd/dot_general | solution.py:198
  418.1 2.7 convolution_convert_fusion.9
  420.8 4.9 fusion.2
  425.8 2.7 fusion.4
  428.5 2.1 fusion.18
  430.7 1.6 convolution_multiply_fusion
  432.5 1.1 fusion.19
  434.3 1.4 convolution_convert_fusion.7
  435.6 1.4 convolution_convert_fusion.8
  437.0 1.9 convolution_convert_fusion.5
  438.9 2.1 convolution_convert_fusion.6
  441.0 2.5 fusion.52
  443.6 1.7 convolution_add_fusion.1
  445.3 1.8 fusion.12
  447.3 15.1 %convolution_convert_fusion = bf16[4096,1536]{1,0:T(8,128)(2,1)} fusion(bf16[4096,640]{0,1:T(8,128)(2,1)} %get-tuple-element.86, bf16[640,1536]{1,0:T(8,128)(2,1)S(1)} %bitcast.136), kind=kOutput, calls=%fused_computation.3 | convolution fusion | flops 8059355136 | bytes 19791872 | tf_op jit(solution)/shard_map/dot_general | solution.py:187
  463.0 1.7 fusion.36
  464.8 73.6 %all-reduce.11.cloned.1.call-done = (bf16[5,1536,128]{2,1,0:T(8,128)(2,1)}, bf16[5,1536,128]{2,1,0:T(8,128)(2,1)}, bf16[5,128,1536]{2,1,0:T(8,128)(2,1)}) async-done(((bf16[5,1536,128]{2,1,0:T(8,128)(2,1)}, bf16[5,1536,128]{2,1,0:T(8,128)(2,1)}, bf16[5,128,1536]{2,1,0:T(8,128)(2,1)}), (bf16[5,1536,128]{2,1,0:T(8,128)(2,1)}, bf16[5,1536,128]{2,1,0:T(8,128)(2,1)}, ...) | async-done | bytes 5898256 | tf_op jit(solution)/shard_map/psum | solution.py:321
  538.4 3.9 convert_element_type.213
  542.2 2.2 convert_element_type.217
  544.4 2.5 convert_element_type.220
  546.9 106.4 %all-reduce.9.cloned.1.call-done = (bf16[1536,384]{1,0:T(8,128)(2,1)}, bf16[1536,128]{1,0:T(8,128)(2,1)}, bf16[1536,128]{1,0:T(8,128)(2,1)}, bf16[384,1536]{1,0:T(8,128)(2,1)}) async-done(((bf16[1536,384]{1,0:T(8,128)(2,1)}, bf16[1536,128]{1,0:T(8,128)(2,1)}, bf16[1536,128]{1,0:T(8,128)(2,1)}, bf16[384,1536]{1,0:T(8,128)(2,1)}), (bf16[1536,384]{1,0:T(8,128)(2,1)}, bf16[1536,128]{1,0:T(8,128)(2,1)}, ...) | async-done | bytes 3145744 | tf_op jit(solution)/shard_map/psum | solution.py:312
  653.3 2.9 convert_element_type.203
  656.2 3.0 convert_element_type.209
  661.1 19.0 %reduce-scatter.11.cloned.1.call-done = bf16[128,1536]{1,0:T(8,128)(2,1)} async-done(((bf16[512,1536]{1,0:T(8,128)(2,1)}), bf16[128,1536]{1,0:T(8,128)(2,1)}) %reduce-scatter.11.cloned.1.call-update) | async-done | bytes 393232 | tf_op jit(solution)/shard_map/reduce_scatter | solution.py:306
  680.1 1.3 fusion.32
  681.4 107.0 %reduce-scatter.7.cloned.1.call-done = bf16[128,1536]{1,0:T(8,128)(2,1)} async-done(((bf16[4096,1536]{1,0:T(8,128)(2,1)}), bf16[128,1536]{1,0:T(8,128)(2,1)}) %reduce-scatter.7.cloned.1.call-update) | async-done | bytes 393232 | tf_op jit(solution)/shard_map/reduce_scatter | solution.py:188
  788.4 3.0 fusion.25
  791.4 65.6 %all-reduce = (f32[1536]{0:T(1024)}, f32[1536]{0:T(1024)}) all-reduce(f32[1536]{0:T(1024)S(1)} %get-tuple-element.60, f32[1536]{0:T(1024)S(1)} %copy-done.51), channel_id=1, replica_groups=mesh['dp'=4,'expert'=8,'tensor'=4] {'dp','expert','tensor'}, use_global_device_ids=true, to_apply=%region_22.23 | all-reduce | flops 3072 | bytes 24576 | tf_op jit(solution)/shard_map/psum | solution.py:317
  857.0 78.2 %all-reduce.7.cloned.1.call-done = f32[1536,40]{0,1:T(8,128)} async-done(((f32[1536,40]{0,1:T(8,128)}), f32[1536,40]{0,1:T(8,128)}) %all-reduce.7.cloned.1.call-update) | async-done | bytes 245776 | tf_op jit(solution)/shard_map/psum | solution.py:317
  935.2 1.7 copy.80
  (185 shorter events, 16.4 us)
Async XLA Ops:
  7.2 202.8 %copy-start = (bf16[5,128,1536]{2,1,0:T(8,128)(2,1)S(1)}, bf16[5,128,1536]{2,1,0:T(8,128)(2,1)}, u32[]{:S(2)}) copy-start(bf16[5,128,1536]{2,1,0:T(8,128)(2,1)} %param.26) | copy-start | bytes 5898244
  7.2 37.2 %copy-start.25 = (bf16[1536,128]{1,0:T(8,128)(2,1)S(1)}, bf16[1536,128]{1,0:T(8,128)(2,1)}, u32[]{:S(2)}) copy-start(bf16[1536,128]{1,0:T(8,128)(2,1)} %param.19) | copy-start | bytes 1179652
  7.2 34.4 %all-gather.5.cloned.1.call-start = ((), (), s32[]{:S(2)}) async-start(), calls=%async_computation.5 | async-start | bytes 1966080 | tf_op jit(solution)/shard_map/all_gather | solution.py:88
  9.1 2.7 copy-start.55
  9.8 2.9 copy-start.42
  11.7 65.4 %reduce-scatter.5.cloned.1.call-start = ((), (), s32[]{:S(2)}) async-start(), calls=%async_computation.6 | async-start | bytes 1966080 | tf_op jit(solution)/shard_map/reduce_scatter | solution.py:139
  13.1 33.3 %copy-start.16 = (f32[512,32]{0,1:T(8,128)}, f32[512,32]{0,1:T(8,128)S(1)}, u32[]{:S(2)}) copy-start(f32[512,32]{0,1:T(8,128)S(1)} %get-tuple-element.98) | copy-start | bytes 196612
  13.1 33.3 %copy-start.18 = (f32[512,32]{0,1:T(8,128)}, f32[512,32]{0,1:T(8,128)S(1)}, u32[]{:S(2)}) copy-start(f32[512,32]{0,1:T(8,128)S(1)} %get-tuple-element.99) | copy-start | bytes 196612
  41.6 2.8 copy-start.2
  44.4 2.0 copy-start.30
  45.2 2.2 copy-start.20
  46.4 2.9 copy-start.1
  46.5 2.9 copy-start.46
  48.1 2.0 copy-start.26
  48.1 4.2 copy-start.57
  48.1 29.1 %copy-start.4 = (bf16[128,1536]{1,0:T(8,128)(2,1)S(1)}, bf16[128,1536]{1,0:T(8,128)(2,1)}, u32[]{:S(2)}) copy-start(bf16[128,1536]{1,0:T(8,128)(2,1)} %param.14) | copy-start | bytes 1179652
  52.3 93.3 %all-gather.7.cloned.1.call-start = ((), (), s32[]{:S(2)}) async-start(), calls=%async_computation.7 | async-start | bytes 12976128 | tf_op jit(solution)/shard_map/all_gather | solution.py:150
  52.4 326.1 %copy-start.44 = (f32[1536]{0:T(1024)}, f32[1536]{0:T(1024)S(1)}, u32[]{:S(2)}) copy-start(f32[1536]{0:T(1024)S(1)} %convert_element_type.181) | copy-start | bytes 18436
  52.4 37.1 %copy-start.48 = (s32[128,8]{0,1:T(8,128)S(1)}, s32[128,8]{0,1:T(8,128)}, u32[]{:S(2)}) copy-start(s32[128,8]{0,1:T(8,128)} %param.16) | copy-start | bytes 12292
  78.4 67.2 %copy-start.34 = (bf16[1536,40]{0,1:T(8,128)(2,1)S(1)}, bf16[1536,40]{0,1:T(8,128)(2,1)}, u32[]{:S(2)}) copy-start(bf16[1536,40]{0,1:T(8,128)(2,1)} %param.23) | copy-start | bytes 368644
  79.0 299.5 %copy-start.52 = (f32[128]{0:T(128)}, f32[128]{0:T(128)S(1)}, u32[]{:S(2)}) copy-start(f32[128]{0:T(128)S(1)} %get-tuple-element.103) | copy-start | bytes 1540
  80.9 129.1 %all-gather.9.cloned.1.call-start = ((), (), s32[]{:S(2)}) async-start(), calls=%async_computation.9 | async-start | bytes 12976128 | tf_op jit(solution)/shard_map/all_gather | solution.py:149
  81.5 294.4 %reduce-scatter.9.cloned.1.call-start = ((), (), s32[]{:S(2)}) async-start(), calls=%async_computation.10 | async-start | bytes 12976128 | tf_op jit(solution)/shard_map/reduce_scatter | solution.py:195
  145.6 8.7 copy-start.5
  145.6 8.7 copy-start.14
  154.3 11.1 %copy-start.13 = (bf16[5,1536,128]{1,2,0:T(8,128)(2,1)S(1)}, bf16[5,1536,128]{1,2,0:T(8,128)(2,1)}, u32[]{:S(2)}) copy-start(bf16[5,1536,128]{1,2,0:T(8,128)(2,1)} %copy.57) | copy-start | bytes 5898244
  210.0 30.1 %copy-start.15 = (bf16[5,1536,128]{1,2,0:T(8,128)(2,1)S(1)}, bf16[5,1536,128]{1,2,0:T(8,128)(2,1)}, u32[]{:S(2)}) copy-start(bf16[5,1536,128]{1,2,0:T(8,128)(2,1)} %copy.56) | copy-start | bytes 5898244
  240.1 13.5 %copy-start.8 = (bf16[4096,640]{0,1:T(8,128)(2,1)}, bf16[4096,640]{0,1:T(8,128)(2,1)S(1)}, u32[]{:S(2)}) copy-start(bf16[4096,640]{0,1:T(8,128)(2,1)S(1)} %get-tuple-element.85) | copy-start | bytes 15728644
  274.7 101.3 %copy-start.49 = (f32[128]{0:T(128)}, f32[128]{0:T(128)S(1)}, u32[]{:S(2)}) copy-start(f32[128]{0:T(128)S(1)} %get-tuple-element.108) | copy-start | bytes 1540
  281.2 20.2 %all-to-all-start = ((f32[32,128,5]{1,2,0:T(8,128)}), f32[32,128,5]{1,2,0:T(8,128)}, u32[]{:S(2)}, u32[]{:S(2)}) async-start(f32[32,128,5]{1,2,0:T(8,128)} %bitcast.21), calls=%async_computation.3 | async-start | bytes 262144 | tf_op jit(solution)/shard_map/all_to_all | solution.py:212
  286.7 89.2 %copy-start.7 = (bf16[128,1536]{1,0:T(8,128)(2,1)S(1)}, bf16[128,1536]{1,0:T(8,128)(2,1)}, u32[]{:S(2)}) copy-start(bf16[128,1536]{1,0:T(8,128)(2,1)} %reduce-scatter.5.cloned.1.call-done) | copy-start | bytes 1179652
  286.7 92.6 %copy-start.9 = (bf16[128,1536]{1,0:T(8,128)(2,1)S(1)}, bf16[128,1536]{1,0:T(8,128)(2,1)}, u32[]{:S(2)}) copy-start(bf16[128,1536]{1,0:T(8,128)(2,1)} %param.27) | copy-start | bytes 1179652
  286.7 131.3 %all-gather.11.cloned.1.call-start = ((), (), s32[]{:S(2)}) async-start(), calls=%async_computation.11 | async-start | bytes 1966080 | tf_op jit(solution)/shard_map/all_gather | solution.py:238
  378.5 16.9 %copy-start.59 = (f32[128]{0:T(128)}, f32[128]{0:T(128)S(1)}, u32[]{:S(2)}) copy-start(f32[128]{0:T(128)S(1)} %broadcast_multiply_fusion.1) | copy-start | bytes 1540
  381.1 157.2 %all-reduce.11.cloned.1.call-start = ((), (), s32[]{:S(2)}) async-start(), calls=%async_computation.15 | async-start | bytes 11796480 | tf_op jit(solution)/shard_map/psum | solution.py:321
  417.0 236.3 %all-reduce.9.cloned.1.call-start = ((), (), s32[]{:S(2)}) async-start(), calls=%async_computation.14 | async-start | bytes 6291456 | tf_op jit(solution)/shard_map/psum | solution.py:312
  418.1 2.7 copy-start.33
  418.1 7.7 slice-start
  420.8 5.0 copy-start.22
  420.8 4.9 slice-start.1
  425.8 4.8 copy-start.17
  425.8 4.8 copy-start.19
  428.4 4.0 copy-start.23
  430.7 4.9 copy-start.29
  432.5 6.4 copy-start.24
  432.5 4.5 copy-start.36
  432.5 4.5 copy-start.63
  441.0 239.2 %reduce-scatter.11.cloned.1.call-start = ((), (), s32[]{:S(2)}) async-start(), calls=%async_computation.12 | async-start | bytes 1966080 | tf_op jit(solution)/shard_map/reduce_scatter | solution.py:306
  441.0 4.2 copy-start.21
  441.0 4.2 copy-start.28
  447.0 341.4 %reduce-scatter.7.cloned.1.call-start = ((), (), s32[]{:S(2)}) async-start(), calls=%async_computation.8 | async-start | bytes 12976128 | tf_op jit(solution)/shard_map/reduce_scatter | solution.py:188
  462.4 472.8 %all-reduce.7.cloned.1.call-start = ((), (), s32[]{:S(2)}) async-start(), calls=%async_computation.13 | async-start | bytes 491520 | tf_op jit(solution)/shard_map/psum | solution.py:317
  538.4 3.9 copy-start.12
  538.4 6.1 copy-start.11
  546.9 133.2 %copy-start.43 = (f32[1536]{0:T(1024)S(1)}, f32[1536]{0:T(1024)}, u32[]{:S(2)}) copy-start(f32[1536]{0:T(1024)} %copy-done.42) | copy-start | bytes 18436
  546.9 133.2 %copy-start.56 = (f32[128]{0:T(128)S(1)}, f32[128]{0:T(128)}, u32[]{:S(2)}) copy-start(f32[128]{0:T(128)} %copy-done.55) | copy-start | bytes 1540
  546.9 241.5 %copy-start.45 = (f32[1536]{0:T(1024)S(1)}, f32[1536]{0:T(1024)}, u32[]{:S(2)}) copy-start(f32[1536]{0:T(1024)} %copy-done.44) | copy-start | bytes 18436
  546.9 241.5 %copy-start.53 = (f32[128]{0:T(128)S(1)}, f32[128]{0:T(128)}, u32[]{:S(2)}) copy-start(f32[128]{0:T(128)} %copy-done.52) | copy-start | bytes 1540
  546.9 241.5 %copy-start.58 = (f32[128]{0:T(128)S(1)}, f32[128]{0:T(128)}, u32[]{:S(2)}) copy-start(f32[128]{0:T(128)} %get-tuple-element.102) | copy-start | bytes 1540
  546.9 241.5 %copy-start.60 = (f32[128]{0:T(128)S(1)}, f32[128]{0:T(128)}, u32[]{:S(2)}) copy-start(f32[128]{0:T(128)} %copy-done.59) | copy-start | bytes 1540
  546.9 241.5 %copy-start.62 = (f32[128]{0:T(128)S(1)}, f32[128]{0:T(128)}, u32[]{:S(2)}) copy-start(f32[128]{0:T(128)} %get-tuple-element.100) | copy-start | bytes 1540
  653.3 5.9 copy-start.38
  653.3 6.8 copy-start.37
  656.2 135.2 %copy-start.51 = (f32[1536]{0:T(1024)S(1)}, f32[1536]{0:T(1024)}, u32[]{:S(2)}) copy-start(f32[1536]{0:T(1024)} %get-tuple-element.58) | copy-start | bytes 18436
  (14 other events, 15.7 us)
Sparse Core Ops, SparseCore 0:
  11.9 29.6 all-gather.4
  52.4 24.7 reduce-scatter.4
  81.0 64.4 all-gather.6
  147.7 62.3 all-gather.8
  273.6 102.3 reduce-scatter.8
  381.3 26.8 all-gather.10
  417.2 121.1 all-reduce.10
  543.1 110.1 all-reduce.8
  655.9 24.1 reduce-scatter.10
  684.3 104.0 reduce-scatter.6
  793.7 141.3 all-reduce.6

commit v2 on v1

--- a/solution.py
+++ b/solution.py
@@ -1,8 +1,11 @@
+import functools
 import math
 
 import jax
 import jax.numpy as jnp
 from jax import lax
+from jax.experimental import pallas as pl
+from jax.experimental.pallas import tpu as pltpu
 from jax.sharding import PartitionSpec as P
 
 HEAD_SIZE = 64
@@ -53,6 +56,246 @@
     return jnp.concatenate(
         [first * cosine_table + second * sine_table, second * cosine_table - first * sine_table], -1
     )
+
+
+MESH = pl.DeviceIdType.MESH
+
+def ag_plane_kernel(src, out, own_sem, send_sem, recv_sem, sib_send, sib_recv):
+    x = lax.axis_index("tensor"); e = lax.axis_index("expert")
+    z = e // 2; c = e % 2
+    def peer(ox, oz):
+        return {"expert": ((z + oz) % 4) * 2 + c, "tensor": (x + ox) % 4}
+    sib = {"expert": z * 2 + 1 - c}
+    def blk(dx, dz):
+        return (((z + dz) % 4) * 2 + c) * 4 + (x + dx) % 4
+    def sblk(dx, dz):
+        return (((z + dz) % 4) * 2 + 1 - c) * 4 + (x + dx) % 4
+    barrier = pltpu.get_barrier_semaphore()
+    near = [peer(1, 0), peer(-1, 0), peer(0, 1), peer(0, -1), sib]
+    for p in near:
+        pl.semaphore_signal(barrier, inc=1, device_id=p, device_id_type=MESH)
+    pl.semaphore_wait(barrier, len(near))
+    n = [0]
+    pend = []
+    def desc(dx, dz, ox, oz, q, nq, sidx, own=False):
+        rows = pl.ds(q * 32, nq * 32)
+        s = src.at[rows] if own else out.at[blk(dx, dz), rows]
+        return pltpu.make_async_remote_copy(
+            src_ref=s, dst_ref=out.at[blk(dx, dz), rows],
+            send_sem=send_sem.at[sidx],
+            recv_sem=recv_sem.at[(dx - ox) % 4, (dz - oz) % 4, q],
+            device_id=peer(ox, oz), device_id_type=MESH)
+    def send(dx, dz, ox, oz, q, nq, own=False):
+        cp = desc(dx, dz, ox, oz, q, nq, n[0], own)
+        n[0] += 1
+        cp.start(); pend.append(cp)
+    def recv(dx, dz, q, nq):
+        rows = pl.ds(q * 32, nq * 32)
+        pltpu.make_async_remote_copy(
+            src_ref=out.at[blk(dx, dz), rows], dst_ref=out.at[blk(dx, dz), rows],
+            send_sem=send_sem.at[0], recv_sem=recv_sem.at[dx % 4, dz % 4, q],
+            device_id=peer(1, 0), device_id_type=MESH).wait_recv()
+    sn = [0]
+    def sibsend(dx, dz, own=False):
+        cp = pltpu.make_async_remote_copy(
+            src_ref=src if own else out.at[blk(dx, dz)], dst_ref=out.at[blk(dx, dz)],
+            send_sem=sib_send.at[dx % 4, dz % 4], recv_sem=sib_recv.at[dx % 4, dz % 4],
+            device_id=sib, device_id_type=MESH)
+        cp.start(); pend.append(cp)
+    for ox, oz in ((1, 0), (-1, 0), (0, 1), (0, -1)):
+        send(0, 0, ox, oz, 0, 4, own=True)
+    mine = pltpu.make_async_copy(src, out.at[blk(0, 0)], own_sem)
+    mine.start()
+    sibsend(0, 0, own=True)
+    for s in (1, -1):
+        recv(s, 0, 0, 4)
+        if s == -1:
+            send(s, 0, 1, 0, 1, 2)
+        else:
+            send(s, 0, -1, 0, 0, 1); send(s, 0, -1, 0, 3, 1)
+        for oz in (1, -1):
+            send(s, 0, 0, oz, 0, 2)
+        recv(0, s, 0, 4)
+        if s == -1:
+            send(0, s, 0, 1, 1, 2)
+        else:
+            send(0, s, 0, -1, 0, 1); send(0, s, 0, -1, 3, 1)
+        for ox in (1, -1):
+            send(0, s, ox, 0, 2, 2)
+        sibsend(s, 0); sibsend(0, s)
+    recv(2, 0, 1, 2); recv(2, 0, 0, 1); recv(2, 0, 3, 1)
+    for oz in (1, -1):
+        send(2, 0, 0, oz, 0, 2)
+    recv(0, 2, 1, 2); recv(0, 2, 0, 1); recv(0, 2, 3, 1)
+    for ox in (1, -1):
+        send(0, 2, ox, 0, 2, 2)
+    sibsend(2, 0); sibsend(0, 2)
+    for dx in (1, -1, 2):
+        for s in (1, -1):
+            recv(dx, s, 0, 2)
+            send(dx, s, 0, -s, 0 if s == 1 else 1, 1)
+            recv(s, dx, 2, 2)
+            send(s, dx, -s, 0, 2 if s == 1 else 3, 1)
+    for dx in (1, -1):
+        for dz in (1, -1):
+            sibsend(dx, dz)
+    for dx in (1, -1, 2):
+        recv(dx, 2, 0, 1); recv(dx, 2, 1, 1)
+        recv(2, dx, 2, 1); recv(2, dx, 3, 1)
+    for dx in (1, -1, 2):
+        sibsend(dx, 2)
+        if dx != 2: sibsend(2, dx)
+    for dx in range(4):
+        for dz in range(4):
+            pltpu.make_async_remote_copy(
+                src_ref=src, dst_ref=out.at[sblk(dx, dz)],
+                send_sem=sib_send.at[dx, dz], recv_sem=sib_recv.at[dx, dz],
+                device_id=sib, device_id_type=MESH).wait_recv()
+    mine.wait()
+    for cp in pend:
+        cp.wait_send()
+
+def ag_plane(shard, cid):
+    rows, width = shard.shape
+    return pl.pallas_call(
+        ag_plane_kernel,
+        out_shape=jax.ShapeDtypeStruct((32, rows, width), shard.dtype),
+        in_specs=[pl.BlockSpec(memory_space=pl.ANY)],
+        out_specs=pl.BlockSpec(memory_space=pl.ANY),
+        scratch_shapes=[pltpu.SemaphoreType.DMA(()), pltpu.SemaphoreType.DMA((40,)),
+                        pltpu.SemaphoreType.DMA((4, 4, 4)), pltpu.SemaphoreType.DMA((4, 4)), pltpu.SemaphoreType.DMA((4, 4))],
+        compiler_params=pltpu.CompilerParams(collective_id=cid, has_side_effects=True),
+        name="ag_plane",
+    )(shard)
+
+
+def rs_plane_kernel(nk, p0, p1, out, q, sib, a3, b3, a4, b4, a5, b5, a6, b6,
+                    load_sem, sib_send, sib_recv, ssem, rsem):
+    x = lax.axis_index("tensor"); e = lax.axis_index("expert")
+    z = e // 2; c = e % 2
+    def zi(d): return (z + d) % 4
+    def xi(d): return (x + d) % 4
+    def peer(oz, ox):
+        return {"expert": zi(oz) * 2 + c, "tensor": xi(ox)}
+    partner = {"expert": z * 2 + 1 - c}
+    barrier = pltpu.get_barrier_semaphore()
+    near = [peer(1, 0), peer(-1, 0), peer(0, 1), peer(0, -1), partner]
+    for p in near:
+        pl.semaphore_signal(barrier, inc=1, device_id=p, device_id_type=MESH)
+    pl.semaphore_wait(barrier, len(near))
+    H = slice(0, 32)
+    f32 = jnp.float32
+
+    def cols(k): return pl.ds(pl.multiple_of(k * 128, 128), 128)
+    def loads(k):
+        return [pltpu.make_async_copy(p.at[:, c, :, :, cols(k)], q.at[k, :, :, :, pl.ds(128 * i, 128)], load_sem.at[k, i])
+                for i, p in enumerate((p0, p1))]
+    def sibs(k):
+        return [pltpu.make_async_remote_copy(
+            src_ref=p.at[:, 1 - c, :, :, cols(k)], dst_ref=sib.at[k, :, :, :, pl.ds(128 * i, 128)],
+            send_sem=sib_send.at[k, i], recv_sem=sib_recv.at[k, i], device_id=partner, device_id_type=MESH)
+            for i, p in enumerate((p0, p1))]
+    def rc(k, n, src, dst, to):
+        return pltpu.make_async_remote_copy(src_ref=src, dst_ref=dst, send_sem=ssem.at[k, n], recv_sem=rsem.at[k, n],
+                                            device_id=to, device_id_type=MESH)
+    def copies3(k):
+        return [rc(k, 0, q.at[k, zi(2), :, pl.ds(0, 32)], a3.at[k, 0], peer(1, 0)),
+                rc(k, 1, q.at[k, zi(2), :, pl.ds(32, 32)], a3.at[k, 1], peer(-1, 0)),
+                rc(k, 2, q.at[k, :, xi(2), pl.ds(64, 32)], b3.at[k, 0], peer(0, 1)),
+                rc(k, 3, q.at[k, :, xi(2), pl.ds(96, 32)], b3.at[k, 1], peer(0, -1))]
+    def copies4(k):
+        return [rc(k, 4, q.at[k, zi(1), :, pl.ds(0, 64)], a4.at[k, 0], peer(1, 0)),
+                rc(k, 5, q.at[k, zi(-1), :, pl.ds(0, 64)], a4.at[k, 1], peer(-1, 0)),
+                rc(k, 6, q.at[k, :, xi(1), pl.ds(64, 64)], b4.at[k, 0], peer(0, 1)),
+                rc(k, 7, q.at[k, :, xi(-1), pl.ds(64, 64)], b4.at[k, 1], peer(0, -1))]
+    def copies5(k):
+        return [rc(k, 8, q.at[k, z, xi(2), pl.ds(0, 32)], a5.at[k, 0], peer(0, 1)),
+                rc(k, 9, q.at[k, z, xi(2), pl.ds(32, 32)], a5.at[k, 1], peer(0, -1)),
+                rc(k, 10, q.at[k, zi(2), x, pl.ds(64, 32)], b5.at[k, 0], peer(1, 0)),
+                rc(k, 11, q.at[k, zi(2), x, pl.ds(96, 32)], b5.at[k, 1], peer(-1, 0))]
+    def copies6(k):
+        return [rc(k, 12, q.at[k, z, xi(1), pl.ds(0, 64)], a6.at[k, 0], peer(0, 1)),
+                rc(k, 13, q.at[k, z, xi(-1), pl.ds(0, 64)], a6.at[k, 1], peer(0, -1)),
+                rc(k, 14, q.at[k, zi(1), x, pl.ds(64, 64)], b6.at[k, 0], peer(1, 0)),
+                rc(k, 15, q.at[k, zi(-1), x, pl.ds(64, 64)], b6.at[k, 1], peer(-1, 0))]
+    def add(k, i, j, rows, *terms):
+        t = q[k, i, j, rows].astype(f32)
+        for s in terms:
+            t = t + s.astype(f32)
+        q[k, i, j, rows] = t.astype(jnp.bfloat16)
+
+    def stage1(k):
+        for cp in sibs(k): cp.start()
+        for cp in loads(k): cp.start()
+    def stage2(k):
+        for cp in loads(k): cp.wait()
+        for cp in sibs(k): cp.wait_recv()
+        def body(n, _):
+            add(k, n // 4, n % 4, pl.ds(0, 128), sib[k, n // 4, n % 4])
+            return 0
+        lax.fori_loop(0, 16, body, 0)
+        for cp in copies3(k): cp.start()
+    def stage4(k):
+        for cp in copies3(k): cp.wait_recv()
+        def body(n, _):
+            add(k, zi(1), n, pl.ds(0, 32), a3[k, 0, n])
+            add(k, zi(-1), n, pl.ds(32, 32), a3[k, 1, n])
+            add(k, n, xi(1), pl.ds(64, 32), b3[k, 0, n])
+            add(k, n, xi(-1), pl.ds(96, 32), b3[k, 1, n])
+            return 0
+        lax.fori_loop(0, 4, body, 0)
+        for cp in copies4(k): cp.start()
+    def stage5(k):
+        for cp in copies4(k): cp.wait_recv()
+        def body(n, _):
+            add(k, z, n, pl.ds(0, 64), a4[k, 0, n], a4[k, 1, n])
+            add(k, n, x, pl.ds(64, 64), b4[k, 0, n], b4[k, 1, n])
+            return 0
+        lax.fori_loop(0, 4, body, 0)
+        for cp in copies5(k): cp.start()
+    def stage6(k):
+        for cp in copies5(k): cp.wait_recv()
+        add(k, z, xi(1), pl.ds(0, 32), a5[k, 0])
+        add(k, z, xi(-1), pl.ds(32, 32), a5[k, 1])
+        add(k, zi(1), x, pl.ds(64, 32), b5[k, 0])
+        add(k, zi(-1), x, pl.ds(96, 32), b5[k, 1])
+        for cp in copies6(k): cp.start()
+    def stage7(k):
+        for cp in copies6(k): cp.wait_recv()
+        for h, m in ((0, a6), (64, b6)):
+            t = q[k, z, x, pl.ds(h, 64)].astype(f32) + m[k, 0].astype(f32) + m[k, 1].astype(f32)
+            out[0, pl.ds(h, 64), cols(k)] = t[:, :128]
+            out[1, pl.ds(h, 64), cols(k)] = t[:, 128:]
+        for cp in sibs(k) + copies3(k) + copies4(k) + copies5(k) + copies6(k): cp.wait_send()
+    def step(i, _):
+        for lag, st in ((8, stage7), (7, stage6), (5, stage5), (3, stage4), (1, stage2), (0, stage1)):
+            k = i - lag
+            @pl.when((k >= 0) & (k < nk))
+            def _():
+                st(k)
+        return 0
+    lax.fori_loop(0, nk + 8, step, 0)
+
+def rs_plane(p0, p1, cid, nk=12):
+    bf = jnp.bfloat16
+    width = p0.shape[-1]
+    p0 = p0.reshape(4, 2, 4, 128, width); p1 = p1.reshape(4, 2, 4, 128, width)
+    V = pltpu.VMEM
+    return pl.pallas_call(
+        functools.partial(rs_plane_kernel, nk),
+        out_shape=jax.ShapeDtypeStruct((2, 128, width), jnp.float32),
+        in_specs=[pl.BlockSpec(memory_space=pl.ANY)] * 2,
+        out_specs=pl.BlockSpec(memory_space=pltpu.VMEM),
+        scratch_shapes=[V((nk, 4, 4, 128, 256), bf), V((nk, 4, 4, 128, 256), bf),
+                        V((nk, 2, 4, 32, 256), bf), V((nk, 2, 4, 32, 256), bf),
+                        V((nk, 2, 4, 64, 256), bf), V((nk, 2, 4, 64, 256), bf),
+                        V((nk, 2, 32, 256), bf), V((nk, 2, 32, 256), bf),
+                        V((nk, 2, 64, 256), bf), V((nk, 2, 64, 256), bf),
+                        pltpu.SemaphoreType.DMA((nk, 2)), pltpu.SemaphoreType.DMA((nk, 2)), pltpu.SemaphoreType.DMA((nk, 2)),
+                        pltpu.SemaphoreType.DMA((nk, 16)), pltpu.SemaphoreType.DMA((nk, 16))],
+        compiler_params=pltpu.CompilerParams(collective_id=cid, has_side_effects=True, vmem_limit_bytes=56 << 20),
+        name="rs_plane",
+    )(p0, p1)
 
 
 def shards(
@@ -147,7 +390,7 @@
     experts_index = jnp.arange(experts_all, dtype=jnp.int32)
     plane_routes = lax.all_gather(expert_routes, plane, axis=0, tiled=True)
     plane_upstream = lax.all_gather(out_cotangent, plane, axis=0, tiled=True)
-    plane_rows = lax.all_gather(second_low, plane, axis=0, tiled=True)
+    plane_rows = ag_plane(second_low, 1).reshape(-1, width)
 
     def dense_gates(rows, routes):
         named = jnp.any(routes[:, :, None] == experts_index[None, None, :], 1)
@@ -185,16 +428,27 @@
     ).astype(jnp.bfloat16)
     up_pre_grad = (act_grad * silu_gate).astype(jnp.bfloat16)
     mixture_part = jnp.dot(gated, down_flat, preferred_element_type=jnp.float32)
-    mixture = lax.psum_scatter(
-        mixture_part.astype(jnp.bfloat16), plane, scatter_dimension=0, tiled=True
-    ).astype(jnp.float32)
-    layer_output = (residual + mixture).astype(jnp.bfloat16)
     rows_part = jnp.einsum(
         "tf,df->td", gate_pre_grad, gate_flat, preferred_element_type=jnp.float32
     ) + jnp.einsum("tf,df->td", up_pre_grad, up_flat, preferred_element_type=jnp.float32)
-    route_rows = lax.psum_scatter(
-        rows_part.astype(jnp.bfloat16), plane, scatter_dimension=0, tiled=True
-    ).astype(jnp.float32)
+    weighted = plane_gates * gate_grad_part
+    weighted_high = weighted.astype(jnp.bfloat16)
+    weighted_low = (weighted - weighted_high.astype(jnp.float32)).astype(jnp.bfloat16)
+    own_router = lax.dynamic_slice_in_dim(router_weight, first_expert, local_experts, 1)
+    rows_part = rows_part + jnp.einsum(
+        "te,de->td", weighted_high, own_router, preferred_element_type=jnp.float32
+    )
+    mixture, route_rows = rs_plane(
+        mixture_part.astype(jnp.bfloat16), rows_part.astype(jnp.bfloat16), 2
+    )
+    layer_output = (residual + mixture).astype(jnp.bfloat16)
+    router_pairs = jnp.einsum(
+        "td,te->de",
+        plane_rows,
+        jnp.concatenate([weighted_high, weighted_low], 1),
+        preferred_element_type=jnp.float32,
+    )
+    router_pairs = router_pairs[:, :local_experts] + router_pairs[:, local_experts:]
     down_local = jnp.einsum(
         "tf,td->fd", gated, plane_upstream, preferred_element_type=jnp.float32
     ).reshape(local_experts, hidden, width)
@@ -208,27 +462,21 @@
         .reshape(width, local_experts, hidden)
         .transpose(1, 0, 2)
     )
-    sent_grads = gate_grad_part.reshape(n_expert * n_tensor, tok_local, local_experts)
-    come_grads = lax.all_to_all(sent_grads, plane, split_axis=0, concat_axis=0, tiled=True)
-    gate_grad = (
-        jnp.sum(come_grads.reshape(n_expert, n_tensor, tok_local, local_experts), 1)
-        .transpose(1, 0, 2)
-        .reshape(tok_local, experts_all)
-    )
     gates = dense_gates(second_low, expert_routes)
     upstream = out_cotangent.astype(jnp.float32)
-    gate_mean = jnp.sum(gates * gate_grad, -1, keepdims=True)
-    logit_grad = gates * (gate_grad - gate_mean)
-    router_local = jnp.einsum(
+    shared = gates * jnp.sum(mixture * upstream, -1, keepdims=True)
+    router_local = -jnp.einsum(
         "td,te->de",
         second_low.astype(jnp.float32),
-        logit_grad,
+        shared,
         precision=highest,
         preferred_element_type=jnp.float32,
-    )
-    normed_back = route_rows + jnp.einsum(
+    ) + lax.dynamic_update_slice_in_dim(
+        jnp.zeros((width, experts_all), jnp.float32), router_pairs, first_expert, 1
+    )
+    normed_back = route_rows - jnp.einsum(
         "te,de->td",
-        logit_grad,
+        shared,
         router_weight.astype(jnp.float32),
         precision=highest,
         preferred_element_type=jnp.float32,

time: 953 us -> 862 us (0.905)
  waiting for transfers between devices: 557 us -> 319 us
  Pallas kernels: 0 us -> 140 us
  matrix products: 189 us -> 200 us
  other arithmetic: 47.2 us -> 57.2 us
  local copies, waits for them, and re-layouts: 23.6 us -> 13.8 us
    reduce_scatter x2 -> x0, waiting for transfers between devices: 177 us -> none  [the longest x1 107 us: shards(): lax.psum_scatter(mixture_part.astype(jnp.bfloat16), plane, scatter_dimens...]
    pallas_call x0 -> x2, Pallas kernels: none -> 140 us  [the longest x1 82.6 us: rs_plane(): pl.pallas_call(functools.partial(rs_plane_kernel, nk), out_shape=jax.Shap...]
    psum x1, waiting for transfers between devices: 78.2 us -> 138 us  [shards(): lax.psum((router_local, attention_gain_local, expert_gain_local), ('dp',...]
    psum x1, waiting for transfers between devices: 106 us -> 53.7 us  [shards(): lax.psum(query_local.astype(jnp.bfloat16), ('dp', 'expert'))]
    all_gather x1, waiting for transfers between devices: 33.8 us -> 0.01 us  [shards(): plane_upstream = lax.all_gather(out_cotangent, plane, axis=0, tiled=True)]
    all_gather x1, waiting for transfers between devices: 0.02 us -> 28.1 us  [shards(): lax.all_gather(residual_grad.astype(jnp.bfloat16), 'tensor', axis=0, tile...]
    dot_general x2 -> x4, matrix products: 4.26 us -> 31.1 us  [the longest x1 22 us: shards(): jnp.einsum('te,de->td', weighted_high, own_router, preferred_element_type...]
    reduce_scatter x1, waiting for transfers between devices: 24.8 us -> 0.02 us  [shards(): lax.psum_scatter(head_part.astype(jnp.bfloat16), 'tensor', scatter_dimens...]
  transfers between devices with their start and end apart: 12 -> 8, of which waited for: 10 -> 6; matrix products, arithmetic and copies ran while one was open for 18% -> 14% of each run, Pallas kernels for 0% -> 7%
where the time goes in v2:
time: 862 us; the launch traced here: 855 us
  waiting for transfers between devices  319 us (37%)
  matrix products  200 us (23%)
  Pallas kernels  140 us (16%)
  blocking collectives  108 us (13%)
  other arithmetic  57.2 us (7%)
  between operations  17 us (2%)
  local copies, waits for them, and re-layouts  13.8 us (2%)
    psum x1, waiting for transfers between devices, shards(): lax.psum((router_local, attention_gain_local, expert_gain_local), ('dp',...  138 us
    pallas_call x1, Pallas kernels, rs_plane(): pl.pallas_call(functools.partial(rs_plane_kernel, nk), out_shape=jax.Shap...  82.6 us
    psum x1, blocking collectives, shards(): lax.psum((router_local, attention_gain_local, expert_gain_local), ('dp',...  68.5 us
    pallas_call x1, Pallas kernels, ag_plane(): pl.pallas_call(ag_plane_kernel, out_shape=jax.ShapeDtypeStruct((32, rows,...  57.2 us
    psum x1, waiting for transfers between devices, shards(): lax.psum(query_local.astype(jnp.bfloat16), ('dp', 'expert'))  53.7 us
    psum x1, waiting for transfers between devices, shards(): lax.psum(gate_local.astype(jnp.bfloat16), 'dp').astype(jnp.float32)  53.5 us
    all_gather x1, blocking collectives, shards(): plane_routes = lax.all_gather(expert_routes, plane, axis=0, tiled=True)  39.1 us
    all_gather x1, waiting for transfers between devices, shards(): lax.all_gather(residual_grad.astype(jnp.bfloat16), 'tensor', axis=0, tile...  28.1 us
  transfers between devices with their start and end apart: 8, of which 6 were waited for; matrix products, arithmetic and copies ran while one was open for 14% of the time, Pallas kernels for 7%

profile of v2, /device:TPU:1, one launch (start us, length us, event | category | flops | bytes accessed | tf_op | source)
XLA Modules:
  0.0 855.0 jit_solution(16899510667247530840)
XLA Ops:
  8.1 1.3 fusion.29
  11.2 1.9 fusion.31
  13.2 0.9 convert_reduce_fusion
  14.5 1.0 fusion.24
  15.4 27.5 %all-gather.4.cloned.1.call-done = bf16[512,1536]{1,0:T(8,128)(2,1)} async-done(((bf16[128,1536]{1,0:T(8,128)(2,1)}), bf16[512,1536]{1,0:T(8,128)(2,1)}) %all-gather.4.cloned.1.call-update) | async-done | bytes 1572880 | tf_op jit(solution)/shard_map/all_gather | solution.py:331
  43.0 2.1 fusion.55
  45.2 2.6 fusion.56
  48.0 1.2 fusion.52
  49.3 0.9 fusion.5
  50.9 1.2 fusion.15
  52.9 2.1 convolution_convert_fusion.4
  55.7 4.0 copy.45
  59.7 4.0 copy.46
  63.7 39.1 %all_gather.13 = s32[4096,8]{0,1:T(8,128)S(1)} all-gather(s32[128,8]{0,1:T(8,128)S(1)} %copy-done.67), channel_id=1, replica_groups=mesh['dp'=4,'expert'=8,'tensor'=4] {'expert','tensor'}, dimensions={0}, use_global_device_ids=true | all-gather | bytes 135168 | tf_op jit(solution)/shard_map/all_gather | solution.py:391
  103.7 1.2 multiply_reduce_fusion.2
  106.1 1.9 multiply_convert_fusion.2.src
  108.0 57.2 %ag_plane.1 = bf16[32,128,1536]{2,1,0:T(8,128)(2,1)} custom-call(bf16[128,1536]{1,0:T(8,128)(2,1)} %multiply_convert_fusion.2.src), custom_call_target="tpu_custom_call" | custom-call | tf_op jit(solution)/shard_map/ag_plane/pallas_call | solution.py:160
  166.1 8.5 fusion.53
  174.8 10.9 %fusion.58 = f32[4096,640]{0,1:T(8,128)} fusion(bf16[4096,1536]{1,0:T(8,128)(2,1)S(1)} %bitcast.157, bf16[1536,640]{0,1:T(8,128)(2,1)S(1)} %bitcast.170), kind=kOutput, calls=%fused_computation.133 | convolution fusion | flops 8053063680 | bytes 25034752 | tf_op jit(solution)/shard_map/dot_general | solution.py:413
  185.7 10.8 %fusion.57 = f32[4096,640]{0,1:T(8,128)} fusion(bf16[4096,1536]{1,0:T(8,128)(2,1)S(1)} %bitcast.158, bf16[1536,640]{0,1:T(8,128)(2,1)S(1)} %bitcast.168), kind=kOutput, calls=%fused_computation.132 | convolution fusion | flops 8053063680 | bytes 25034752 | tf_op jit(solution)/shard_map/dot_general | solution.py:412
  196.6 20.6 %multiply_multiply_fusion = (f32[4096,640]{0,1:T(8,128)}, f32[4096,640]{0,1:T(8,128)}) fusion(f32[4096,640]{0,1:T(8,128)} %fusion.58, f32[4096,640]{0,1:T(8,128)} %fusion.57, bf16[4096,1536]{1,0:T(8,128)(2,1)} %all-gather.6.cloned.1.call-done, bf16[640,1536]{1,0:T(8,128)(2,1)S(1)} %bitcast.152), kind=kOutput, calls=%fused_computation.22 | convolution fusion | flops 8068792320 | bytes 56492032 | tf_op jit(solution)/shard_map/td,fd->tf/dot_general | solution.py:414
  217.2 4.7 reduce_sum.124
  222.5 12.8 %multiply_convert_fusion = (bf16[4096,640]{0,1:T(8,128)(2,1)S(1)}, bf16[4096,640]{0,1:T(8,128)(2,1)S(1)}, bf16[4096,640]{0,1:T(8,128)(2,1)S(1)}) fusion(f32[4096,640]{0,1:T(8,128)} %get-tuple-element.109, f32[4096,5]{0,1:T(8,128)S(1)} %get-tuple-element.84, f32[4096,640]{0,1:T(8,128)} %fusion.57, f32[4096,640]{0,1:T(8,128)} %fusion.58), kind=kLoop, calls=%fused_computation.5 | loop fusion | flops 44564480 | bytes 47267840 | tf_op jit(solution)/shard_map/convert_element_type | solution.py:429
  235.4 13.3 %convolution_convert_fusion = bf16[4096,1536]{1,0:T(8,128)(2,1)} fusion(bf16[4096,640]{0,1:T(8,128)(2,1)S(1)} %get-tuple-element.89, bf16[640,1536]{1,0:T(8,128)(2,1)S(1)} %bitcast.151), kind=kOutput, calls=%fused_computation.3 | convolution fusion | flops 8059355136 | bytes 19791872 | tf_op jit(solution)/shard_map/dot_general | solution.py:430
  248.7 13.5 %fusion.60 = f32[4096,1536]{1,0:T(8,128)} fusion(bf16[4096,640]{0,1:T(8,128)(2,1)S(1)} %get-tuple-element.87, bf16[1536,640]{0,1:T(8,128)(2,1)S(1)} %bitcast.171), kind=kOutput, calls=%fused_computation.135 | convolution fusion | flops 8053063680 | bytes 32374784 | tf_op jit(solution)/shard_map/tf,df->td/dot_general | solution.py:433
  262.2 13.5 %fusion.59 = f32[4096,1536]{1,0:T(8,128)} fusion(bf16[4096,640]{0,1:T(8,128)(2,1)S(1)} %get-tuple-element.88, bf16[1536,640]{0,1:T(8,128)(2,1)S(1)} %bitcast.169), kind=kOutput, calls=%fused_computation.134 | convolution fusion | flops 8053063680 | bytes 32374784 | tf_op jit(solution)/shard_map/tf,df->td/dot_general | solution.py:431
  275.6 22.0 %add_convert_fusion = bf16[4096,1536]{1,0:T(8,128)(2,1)} fusion(f32[4096,1536]{1,0:T(8,128)} %fusion.59, f32[4096,1536]{1,0:T(8,128)} %fusion.60, bf16[4096,5]{0,1:T(8,128)(2,1)S(1)} %get-tuple-element.83, bf16[1536,40]{0,1:T(8,128)(2,1)S(1)} %copy-done.30, s32[]{:T(128)S(6)} %select_n.22), kind=kOutput, calls=%fused_computation | convolution fusion | flops 81788928 | bytes 63004676 | tf_op jit(solution)/shard_map/te,de->td/dot_general | solution.py:438
  297.7 82.6 %rs_plane.1 = f32[2,128,1536]{2,1,0:T(8,128)} custom-call(bf16[4,2,4,128,1536]{4,3,2,1,0:T(8,128)(2,1)} %bitcast.162, bf16[4,2,4,128,1536]{4,3,2,1,0:T(8,128)(2,1)} %bitcast.159), custom_call_target="tpu_custom_call" | custom-call | tf_op jit(solution)/shard_map/rs_plane/pallas_call | solution.py:284
  380.4 2.2 fusion.28
  382.6 2.5 multiply_reduce_fusion
  385.1 1.1 fusion.50
  386.4 28.1 %all-gather.8.cloned.1.call-done = bf16[512,1536]{1,0:T(8,128)(2,1)} async-done(((bf16[128,1536]{1,0:T(8,128)(2,1)}), bf16[512,1536]{1,0:T(8,128)(2,1)}) %all-gather.8.cloned.1.call-update) | async-done | bytes 1572880 | tf_op jit(solution)/shard_map/all_gather | solution.py:486
  414.5 2.2 convolution_convert_fusion.9
  416.7 4.0 fusion.21
  420.8 4.3 fusion.2
  425.2 1.8 fusion.4
  427.1 1.1 fusion.20
  428.1 1.6 convolution_multiply_fusion
  430.1 1.8 convolution_convert_fusion.5
  431.9 1.4 convolution_convert_fusion.7
  433.3 1.4 convolution_convert_fusion.8
  434.6 2.0 convolution_convert_fusion.6
  436.8 15.1 %fusion.13 = bf16[5,1536,128]{2,1,0:T(8,128)(2,1)} fusion(bf16[4096,1536,1]{1,0,2:T(8,128)(2,1)} %bitcast.154, bf16[5,128,4096]{2,1,0:T(8,128)(2,1)} %bitcast.165), kind=kOutput, calls=%fused_computation.34 | convolution fusion | flops 8054046720 | bytes 19791872 | tf_op jit(solution)/shard_map/td,tf->df/dot_general | solution.py:456
  452.0 1.0 fusion.61
  453.7 1.8 fusion.12
  455.5 14.1 %convolution_convert_fusion.1 = bf16[640,1536]{1,0:T(8,128)(2,1)} fusion(bf16[4096,640]{0,1:T(8,128)(2,1)} %copy-done.13, bf16[4096,1536]{1,0:T(8,128)(2,1)} %all-gather.6.cloned.1.call-done), kind=kOutput, calls=%fused_computation.26 | convolution fusion | flops 8054046720 | bytes 19791872 | tf_op jit(solution)/shard_map/tf,td->fd/dot_general | solution.py:452
  469.6 15.1 %fusion.14 = bf16[5,1536,128]{2,1,0:T(8,128)(2,1)} fusion(bf16[4096,1536,1]{1,0,2:T(8,128)(2,1)} %bitcast.155, bf16[5,128,4096]{2,1,0:T(8,128)(2,1)} %bitcast.164), kind=kOutput, calls=%fused_computation.35 | convolution fusion | flops 8054046720 | bytes 19791872 | tf_op jit(solution)/shard_map/td,tf->df/dot_general | solution.py:461
  484.8 0.9 copy-done.10
  486.0 6.3 fusion.38
  493.5 53.7 %all-reduce.9.cloned.1.call-done = (bf16[1536,384]{1,0:T(8,128)(2,1)}, bf16[1536,128]{1,0:T(8,128)(2,1)}, bf16[1536,128]{1,0:T(8,128)(2,1)}, bf16[384,1536]{1,0:T(8,128)(2,1)}) async-done(((bf16[1536,384]{1,0:T(8,128)(2,1)}, bf16[1536,128]{1,0:T(8,128)(2,1)}, bf16[1536,128]{1,0:T(8,128)(2,1)}, bf16[384,1536]{1,0:T(8,128)(2,1)}), (bf16[1536,384]{1,0:T(8,128)(2,1)}, bf16[1536,128]{1,0:T(8,128)(2,1)}, ...) | async-done | bytes 3145744 | tf_op jit(solution)/shard_map/psum | solution.py:560
  547.2 2.0 convert_element_type.201
  549.2 1.9 convert_element_type.203
  551.1 2.8 convert_element_type.199
  554.0 1.7 convert_element_type.205
  555.7 18.0 %reduce-scatter.5.cloned.1.call-done = bf16[128,1536]{1,0:T(8,128)(2,1)} async-done(((bf16[512,1536]{1,0:T(8,128)(2,1)}), bf16[128,1536]{1,0:T(8,128)(2,1)}) %reduce-scatter.5.cloned.1.call-update) | async-done | bytes 393232 | tf_op jit(solution)/shard_map/reduce_scatter | solution.py:554
  573.7 1.3 fusion.35
  575.0 2.5 fusion.27
  577.5 68.5 %all-reduce = (f32[1536]{0:T(1024)}, f32[1536]{0:T(1024)}) all-reduce(f32[1536]{0:T(1024)S(1)} %get-tuple-element.60, f32[1536]{0:T(1024)S(1)} %copy-done.66), channel_id=1, replica_groups=mesh['dp'=4,'expert'=8,'tensor'=4] {'dp','expert','tensor'}, use_global_device_ids=true, to_apply=%region_19.20 | all-reduce | flops 3072 | bytes 24576 | tf_op jit(solution)/shard_map/psum | solution.py:565
  646.0 53.5 %all-reduce.11.cloned.1.call-done = (bf16[5,1536,128]{2,1,0:T(8,128)(2,1)}, bf16[5,1536,128]{2,1,0:T(8,128)(2,1)}, bf16[5,128,1536]{2,1,0:T(8,128)(2,1)}) async-done(((bf16[5,1536,128]{2,1,0:T(8,128)(2,1)}, bf16[5,1536,128]{2,1,0:T(8,128)(2,1)}, bf16[5,128,1536]{2,1,0:T(8,128)(2,1)}), (bf16[5,1536,128]{2,1,0:T(8,128)(2,1)}, bf16[5,1536,128]{2,1,0:T(8,128)(2,1)}, ...) | async-done | bytes 5898256 | tf_op jit(solution)/shard_map/psum | solution.py:569
  699.4 3.9 convert_element_type.210
  703.3 2.2 convert_element_type.213
  705.5 2.5 convert_element_type.216
  708.0 137.7 %all-reduce.7.cloned.1.call-done = f32[1536,40]{0,1:T(8,128)} async-done(((f32[1536,40]{0,1:T(8,128)}), f32[1536,40]{0,1:T(8,128)}) %all-reduce.7.cloned.1.call-update) | async-done | bytes 245776 | tf_op jit(solution)/shard_map/psum | solution.py:565
  845.7 1.7 copy.73
  (223 shorter events, 11.0 us)
Async XLA Ops:
  8.0 188.6 %copy-start = (bf16[5,128,1536]{2,1,0:T(8,128)(2,1)S(1)}, bf16[5,128,1536]{2,1,0:T(8,128)(2,1)}, u32[]{:S(2)}) copy-start(bf16[5,128,1536]{2,1,0:T(8,128)(2,1)} %param.26) | copy-start | bytes 5898244
  8.0 34.9 %all-gather.4.cloned.1.call-start = ((), (), s32[]{:S(2)}) async-start(), calls=%async_computation.2 | async-start | bytes 1966080 | tf_op jit(solution)/shard_map/all_gather | solution.py:331
  13.1 90.6 %reduce-scatter.3.cloned.1.call-start = ((), (), s32[]{:S(2)}) async-start(), calls=%async_computation.3 | async-start | bytes 1966080 | tf_op jit(solution)/shard_map/reduce_scatter | solution.py:382
  14.4 34.7 %copy-start.21 = (f32[512,32]{0,1:T(8,128)}, f32[512,32]{0,1:T(8,128)S(1)}, u32[]{:S(2)}) copy-start(f32[512,32]{0,1:T(8,128)S(1)} %get-tuple-element.100) | copy-start | bytes 196612
  14.5 34.7 %copy-start.23 = (f32[512,32]{0,1:T(8,128)}, f32[512,32]{0,1:T(8,128)S(1)}, u32[]{:S(2)}) copy-start(f32[512,32]{0,1:T(8,128)S(1)} %get-tuple-element.101) | copy-start | bytes 196612
  45.1 4.0 copy-start.55
  45.2 4.0 copy-start.56
  50.9 4.8 copy-start.80
  55.0 8.7 %copy-start.67 = (s32[128,8]{0,1:T(8,128)S(1)}, s32[128,8]{0,1:T(8,128)}, u32[]{:S(2)}) copy-start(s32[128,8]{0,1:T(8,128)} %param.16) | copy-start | bytes 12292
  55.0 48.7 %copy-start.4 = (bf16[128,1536]{1,0:T(8,128)(2,1)S(1)}, bf16[128,1536]{1,0:T(8,128)(2,1)}, u32[]{:S(2)}) copy-start(bf16[128,1536]{1,0:T(8,128)(2,1)} %param.14) | copy-start | bytes 1179652
  55.0 141.5 %all-gather.6.cloned.1.call-start = ((), (), s32[]{:S(2)}) async-start(), calls=%async_computation.4 | async-start | bytes 12976128 | tf_op jit(solution)/shard_map/all_gather | solution.py:392
  55.6 358.9 %all-gather.8.cloned.1.call-start = ((), (), s32[]{:S(2)}) async-start(), calls=%async_computation.5 | async-start | bytes 1966080 | tf_op jit(solution)/shard_map/all_gather | solution.py:486
  55.7 49.8 %copy-start.57 = (f32[1536]{0:T(1024)}, f32[1536]{0:T(1024)S(1)}, u32[]{:S(2)}) copy-start(f32[1536]{0:T(1024)S(1)} %convert_element_type.178) | copy-start | bytes 18436
  108.0 57.2 %copy-start.9 = (bf16[128,1536]{1,0:T(8,128)(2,1)S(1)}, bf16[128,1536]{1,0:T(8,128)(2,1)}, u32[]{:S(2)}) copy-start(bf16[128,1536]{1,0:T(8,128)(2,1)} %multiply_convert_fusion.2.src) | copy-start | bytes 1179652
  108.0 57.2 %copy-start.30 = (bf16[1536,40]{0,1:T(8,128)(2,1)S(1)}, bf16[1536,40]{0,1:T(8,128)(2,1)}, u32[]{:S(2)}) copy-start(bf16[1536,40]{0,1:T(8,128)(2,1)} %param.23) | copy-start | bytes 368644
  166.1 8.6 %copy-start.2 = (bf16[32,128,1536]{2,1,0:T(8,128)(2,1)S(1)}, bf16[32,128,1536]{2,1,0:T(8,128)(2,1)}, u32[]{:S(2)}) copy-start(bf16[32,128,1536]{2,1,0:T(8,128)(2,1)} %ag_plane.1) | copy-start | bytes 37748740
  166.1 8.7 %copy-start.19 = (bf16[5,1536,128]{1,2,0:T(8,128)(2,1)S(1)}, bf16[5,1536,128]{1,2,0:T(8,128)(2,1)}, u32[]{:S(2)}) copy-start(bf16[5,1536,128]{1,2,0:T(8,128)(2,1)} %copy.46) | copy-start | bytes 5898244
  174.8 10.9 %copy-start.17 = (bf16[5,1536,128]{1,2,0:T(8,128)(2,1)S(1)}, bf16[5,1536,128]{1,2,0:T(8,128)(2,1)}, u32[]{:S(2)}) copy-start(bf16[5,1536,128]{1,2,0:T(8,128)(2,1)} %copy.45) | copy-start | bytes 5898244
  222.5 53.1 %copy-start.41 = (bf16[4096,5]{0,1:T(8,128)(2,1)}, bf16[4096,5]{0,1:T(8,128)(2,1)S(1)}, u32[]{:S(2)}) copy-start(bf16[4096,5]{0,1:T(8,128)(2,1)S(1)} %get-tuple-element.83) | copy-start | bytes 122884
  235.3 13.3 %copy-start.13 = (bf16[4096,640]{0,1:T(8,128)(2,1)}, bf16[4096,640]{0,1:T(8,128)(2,1)S(1)}, u32[]{:S(2)}) copy-start(bf16[4096,640]{0,1:T(8,128)(2,1)S(1)} %get-tuple-element.89) | copy-start | bytes 15728644
  235.3 13.3 %copy-start.12 = (bf16[4096,640]{0,1:T(8,128)(2,1)}, bf16[4096,640]{0,1:T(8,128)(2,1)S(1)}, u32[]{:S(2)}) copy-start(bf16[4096,640]{0,1:T(8,128)(2,1)S(1)} %get-tuple-element.87) | copy-start | bytes 15728644
  235.4 26.8 %copy-start.14 = (bf16[4096,640]{0,1:T(8,128)(2,1)}, bf16[4096,640]{0,1:T(8,128)(2,1)S(1)}, u32[]{:S(2)}) copy-start(bf16[4096,640]{0,1:T(8,128)(2,1)S(1)} %get-tuple-element.88) | copy-start | bytes 15728644
  235.4 13.3 %copy-start.20 = (bf16[5,1536,128]{1,2,0:T(8,128)(2,1)S(1)}, bf16[5,1536,128]{1,2,0:T(8,128)(2,1)}, u32[]{:S(2)}) copy-start(bf16[5,1536,128]{1,2,0:T(8,128)(2,1)} %copy.46) | copy-start | bytes 5898244
  248.7 13.5 %copy-start.18 = (bf16[5,1536,128]{1,2,0:T(8,128)(2,1)S(1)}, bf16[5,1536,128]{1,2,0:T(8,128)(2,1)}, u32[]{:S(2)}) copy-start(bf16[5,1536,128]{1,2,0:T(8,128)(2,1)} %copy.45) | copy-start | bytes 5898244
  297.6 82.7 %copy-start.5 = (bf16[128,1536]{1,0:T(8,128)(2,1)S(1)}, bf16[128,1536]{1,0:T(8,128)(2,1)}, u32[]{:S(2)}) copy-start(bf16[128,1536]{1,0:T(8,128)(2,1)} %param.14) | copy-start | bytes 1179652
  297.6 82.7 %copy-start.8 = (bf16[128,1536]{1,0:T(8,128)(2,1)S(1)}, bf16[128,1536]{1,0:T(8,128)(2,1)}, u32[]{:S(2)}) copy-start(bf16[128,1536]{1,0:T(8,128)(2,1)} %reduce-scatter.3.cloned.1.call-done) | copy-start | bytes 1179652
  297.6 82.7 %copy-start.11 = (bf16[128,1536]{1,0:T(8,128)(2,1)S(1)}, bf16[128,1536]{1,0:T(8,128)(2,1)}, u32[]{:S(2)}) copy-start(bf16[128,1536]{1,0:T(8,128)(2,1)} %param.27) | copy-start | bytes 1179652
  297.6 84.9 %copy-start.31 = (bf16[1536,40]{0,1:T(8,128)(2,1)S(1)}, bf16[1536,40]{0,1:T(8,128)(2,1)}, u32[]{:S(2)}) copy-start(bf16[1536,40]{0,1:T(8,128)(2,1)} %param.23) | copy-start | bytes 368644
  297.6 84.9 %copy-start.52 = (f32[128,40]{0,1:T(8,128)S(1)}, f32[128,40]{0,1:T(8,128)}, u32[]{:S(2)}) copy-start(f32[128,40]{0,1:T(8,128)} %copy-done.51) | copy-start | bytes 61444
  297.6 84.9 %copy-start.58 = (f32[1536]{0:T(1024)S(1)}, f32[1536]{0:T(1024)}, u32[]{:S(2)}) copy-start(f32[1536]{0:T(1024)} %copy-done.57) | copy-start | bytes 18436
  297.7 84.9 %copy-start.69 = (f32[128]{0:T(128)S(1)}, f32[128]{0:T(128)}, u32[]{:S(2)}) copy-start(f32[128]{0:T(128)} %copy-done.68) | copy-start | bytes 1540
  297.7 84.9 %copy-start.72 = (f32[128]{0:T(128)S(1)}, f32[128]{0:T(128)}, u32[]{:S(2)}) copy-start(f32[128]{0:T(128)} %copy-done.71) | copy-start | bytes 1540
  297.7 84.9 %copy-start.78 = (f32[128]{0:T(128)S(1)}, f32[128]{0:T(128)}, u32[]{:S(2)}) copy-start(f32[128]{0:T(128)} %fusion.44) | copy-start | bytes 1540
  297.7 87.4 %copy-start.81 = (f32[128]{0:T(128)S(1)}, f32[128]{0:T(128)}, u32[]{:S(2)}) copy-start(f32[128]{0:T(128)} %get-tuple-element.104) | copy-start | bytes 1540
  380.3 6.0 copy-start.63
  380.3 6.0 copy-start.65
  380.3 34.1 %copy-start.34 = (bf16[384,1536]{1,0:T(8,128)(2,1)S(1)}, bf16[384,1536]{1,0:T(8,128)(2,1)}, u32[]{:S(2)}) copy-start(bf16[384,1536]{1,0:T(8,128)(2,1)} %param.21) | copy-start | bytes 3538948
  382.5 3.8 copy-start.76
  386.3 160.9 %all-reduce.9.cloned.1.call-start = ((), (), s32[]{:S(2)}) async-start(), calls=%async_computation.8 | async-start | bytes 6291456 | tf_op jit(solution)/shard_map/psum | solution.py:560
  414.5 6.3 copy-start.48
  416.7 8.4 slice-start
  420.8 11.1 %copy-start.37 = (bf16[2,64,512]{2,1,0:T(8,128)(2,1)}, bf16[2,64,512]{2,1,0:T(8,128)(2,1)S(1)}, u32[]{:S(2)}) copy-start(bf16[2,64,512]{2,1,0:T(8,128)(2,1)S(1)} %fusion.21) | copy-start | bytes 393220
  420.8 4.3 slice-start.1
  428.1 3.8 copy-start.7
  430.1 4.6 copy-start.27
  436.7 137.0 %reduce-scatter.5.cloned.1.call-start = ((), (), s32[]{:S(2)}) async-start(), calls=%async_computation.6 | async-start | bytes 1966080 | tf_op jit(solution)/shard_map/reduce_scatter | solution.py:554
  436.8 15.2 %copy-start.28 = (bf16[512,6,64]{0,2,1:T(8,128)(2,1)S(1)}, bf16[512,6,64]{0,2,1:T(8,128)(2,1)}, u32[]{:S(2)}) copy-start(bf16[512,6,64]{0,2,1:T(8,128)(2,1)} %copy-done.27) | copy-start | bytes 1179652
  436.8 15.2 %copy-start.36 = (bf16[1536,384]{1,0:T(8,128)(2,1)S(1)}, bf16[1536,384]{1,0:T(8,128)(2,1)}, u32[]{:S(2)}) copy-start(bf16[1536,384]{1,0:T(8,128)(2,1)} %param.18) | copy-start | bytes 3538948
  436.8 16.2 %copy-start.29 = (bf16[1536,128]{1,0:T(8,128)(2,1)S(1)}, bf16[1536,128]{1,0:T(8,128)(2,1)}, u32[]{:S(2)}) copy-start(bf16[1536,128]{1,0:T(8,128)(2,1)} %param.19) | copy-start | bytes 1179652
  436.8 16.2 %copy-start.40 = (bf16[512,2,64]{0,2,1:T(8,128)(2,1)S(1)}, bf16[512,2,64]{0,2,1:T(8,128)(2,1)}, u32[]{:S(2)}) copy-start(bf16[512,2,64]{0,2,1:T(8,128)(2,1)} %copy-done.39) | copy-start | bytes 393220
  455.4 244.0 %all-reduce.11.cloned.1.call-start = ((), (), s32[]{:S(2)}) async-start(), calls=%async_computation.9 | async-start | bytes 11796480 | tf_op jit(solution)/shard_map/psum | solution.py:569
  484.7 360.9 %all-reduce.7.cloned.1.call-start = ((), (), s32[]{:S(2)}) async-start(), calls=%async_computation.7 | async-start | bytes 491520 | tf_op jit(solution)/shard_map/psum | solution.py:565
  492.3 81.4 %copy-start.61 = (f32[1536]{0:T(1024)S(1)}, f32[1536]{0:T(1024)}, u32[]{:S(2)}) copy-start(f32[1536]{0:T(1024)} %copy-done.60) | copy-start | bytes 18436
  492.3 81.4 %copy-start.75 = (f32[128]{0:T(128)S(1)}, f32[128]{0:T(128)}, u32[]{:S(2)}) copy-start(f32[128]{0:T(128)} %copy-done.74) | copy-start | bytes 1540
  492.8 82.2 %copy-start.59 = (f32[1536]{0:T(1024)S(1)}, f32[1536]{0:T(1024)}, u32[]{:S(2)}) copy-start(f32[1536]{0:T(1024)} %copy-done.57) | copy-start | bytes 18436
  492.8 82.2 %copy-start.70 = (f32[128]{0:T(128)S(1)}, f32[128]{0:T(128)}, u32[]{:S(2)}) copy-start(f32[128]{0:T(128)} %copy-done.68) | copy-start | bytes 1540
  492.8 82.2 %copy-start.82 = (f32[128]{0:T(128)S(1)}, f32[128]{0:T(128)}, u32[]{:S(2)}) copy-start(f32[128]{0:T(128)} %get-tuple-element.104) | copy-start | bytes 1540
  492.8 82.2 %copy-start.84 = (f32[128]{0:T(128)S(1)}, f32[128]{0:T(128)}, u32[]{:S(2)}) copy-start(f32[128]{0:T(128)} %copy-done.83) | copy-start | bytes 1540
  492.8 82.2 %copy-start.85 = (f32[128]{0:T(128)S(1)}, f32[128]{0:T(128)}, u32[]{:S(2)}) copy-start(f32[128]{0:T(128)} %get-tuple-element.102) | copy-start | bytes 1540
  547.2 6.8 copy-start.35
  551.1 26.3 %copy-start.66 = (f32[1536]{0:T(1024)S(1)}, f32[1536]{0:T(1024)}, u32[]{:S(2)}) copy-start(f32[1536]{0:T(1024)} %get-tuple-element.58) | copy-start | bytes 18436
  699.4 3.9 copy-start.16
  699.4 6.1 copy-start.15
  703.3 144.0 %copy-start.1 = (bf16[5,128,1536]{2,1,0:T(8,128)(2,1)S(1)}, bf16[5,128,1536]{2,1,0:T(8,128)(2,1)}, u32[]{:S(2)}) copy-start(bf16[5,128,1536]{2,1,0:T(8,128)(2,1)} %param.26) | copy-start | bytes 5898244
  (33 other events, 53.3 us)
Sparse Core Ops, SparseCore 0:
  13.2 29.6 all-gather.3
  55.2 29.8 reduce-scatter.2
  386.4 28.0 all-gather.7
  436.8 110.3 all-reduce.8
  549.4 24.1 reduce-scatter.4
  576.7 122.7 all-reduce.10
  704.7 140.8 all-reduce.6
Sparse Core Ops, SparseCore 1:
  57.8 76.1 all-gather.5

commit v3 on v2

--- a/solution.py
+++ b/solution.py
@@ -67,9 +67,9 @@
         return {"expert": ((z + oz) % 4) * 2 + c, "tensor": (x + ox) % 4}
     sib = {"expert": z * 2 + 1 - c}
     def blk(dx, dz):
-        return (((z + dz) % 4) * 2 + c) * 4 + (x + dx) % 4
+        return (c * 4 + (z + dz) % 4) * 4 + (x + dx) % 4
     def sblk(dx, dz):
-        return (((z + dz) % 4) * 2 + 1 - c) * 4 + (x + dx) % 4
+        return ((1 - c) * 4 + (z + dz) % 4) * 4 + (x + dx) % 4
     barrier = pltpu.get_barrier_semaphore()
     near = [peer(1, 0), peer(-1, 0), peer(0, 1), peer(0, -1), sib]
     for p in near:
@@ -169,133 +169,304 @@
     )(shard)
 
 
-def rs_plane_kernel(nk, p0, p1, out, q, sib, a3, b3, a4, b4, a5, b5, a6, b6,
-                    load_sem, sib_send, sib_recv, ssem, rsem):
-    x = lax.axis_index("tensor"); e = lax.axis_index("expert")
+def expert_forward_kernel(x_ref, u_ref, routes_ref, w_ref, down_ref, acts_ref):
+    f32, low = jnp.float32, jnp.bfloat16
+    rows = x_ref.shape[0]
+    wide = down_ref.shape[0]
+    count = wide // 128
+    first = lax.axis_index("expert") * count
+    pre = jnp.dot(x_ref[...], w_ref[...], preferred_element_type=f32)
+    raw = lax.dot_general(u_ref[...], down_ref[...], (((1,), (1,)), ((), ())), preferred_element_type=f32)
+    lane = lax.broadcasted_iota(jnp.int32, (rows, 128), 1)
+    named = lane == routes_ref[:, 0:1]
+    for n in range(1, routes_ref.shape[1]):
+        named = named | (lane == routes_ref[:, n : n + 1])
+    logits = jnp.where(named, pre[:, 2 * wide :], -1e30)
+    raised = jnp.exp(logits - jnp.max(logits, -1, keepdims=True))
+    gates = raised / jnp.sum(raised, -1, keepdims=True)
+    weighted = jnp.zeros((rows, 128), f32)
+    for n in range(count):
+        here = slice(128 * n, 128 * (n + 1))
+        gate = jnp.sum(jnp.where(lane == first + n, gates, 0.0), -1, keepdims=True)
+        gate_pre = pre[:, here]
+        up_pre = pre[:, wide + 128 * n : wide + 128 * (n + 1)]
+        sig = jax.nn.sigmoid(gate_pre)
+        silu = gate_pre * sig
+        active = silu * up_pre
+        back = raw[:, here]
+        share = gate * jnp.sum(active * back, -1, keepdims=True)
+        high = share.astype(low).astype(f32)
+        weighted = weighted + jnp.where(lane == first + n, high, 0.0)
+        weighted = weighted + jnp.where(lane == first + n + 64, share - high, 0.0)
+        back = gate * back
+        acts_ref[:, here] = (gate * active).astype(low)
+        acts_ref[:, wide + 128 * n : wide + 128 * (n + 1)] = (
+            back * up_pre * (sig * (1.0 + gate_pre * (1.0 - sig)))
+        ).astype(low)
+        acts_ref[:, 2 * wide + 128 * n : 2 * wide + 128 * (n + 1)] = (back * silu).astype(low)
+    acts_ref[:, 3 * wide :] = weighted.astype(low)
+
+
+def expert_forward(x, u, routes, w_all, down, block=256):
+    rows, width = x.shape
+    wide = down.shape[0]
+    total = w_all.shape[1]
+    half = 512 // block
+
+    def place(i):
+        core, z = i // (4 * half), i // half % 4
+        return (z * 2 + core) * half + i % half
+
+    return pl.pallas_call(
+        expert_forward_kernel,
+        grid=(rows // block,),
+        out_shape=jax.ShapeDtypeStruct((rows, 3 * wide + 128), jnp.bfloat16),
+        in_specs=[
+            pl.BlockSpec((block, width), lambda i: (i, 0)),
+            pl.BlockSpec((block, width), lambda i: (place(i), 0)),
+            pl.BlockSpec((block, routes.shape[1]), lambda i: (place(i), 0)),
+            pl.BlockSpec((width, total), lambda i: (0, 0)),
+            pl.BlockSpec((wide, width), lambda i: (0, 0)),
+        ],
+        out_specs=pl.BlockSpec((block, 3 * wide + 128), lambda i: (i, 0)),
+        compiler_params=pltpu.CompilerParams(vmem_limit_bytes=48 << 20),
+        name="expert_forward",
+    )(x, u, routes, w_all, down)
+
+
+def expert_back_kernel(acts_hbm, x_hbm, u_hbm, w_ref, down_ref, out, dw_out, router_out,
+                       acts, stage, q, sib, a3, b3, a4, b4, a5, b5, a6, b6, xu, acc, dwb, ya, yb,
+                       act_sem, load_sem, sib_send, sib_recv, ssem, rsem, ysend, yrecv):
+    f32, low = jnp.float32, jnp.bfloat16
+    nk = 12
+    wide = 640
+    x = lax.axis_index("tensor"); e = lax.axis_index("expert"); y = lax.axis_index("dp")
     z = e // 2; c = e % 2
     def zi(d): return (z + d) % 4
     def xi(d): return (x + d) % 4
+    def yi(d): return (y + d) % 4
     def peer(oz, ox):
         return {"expert": zi(oz) * 2 + c, "tensor": xi(ox)}
+    def ypeer(o):
+        return {"dp": yi(o)}
     partner = {"expert": z * 2 + 1 - c}
+
+    def act_load(n):
+        rows = pl.ds(pl.multiple_of(n * 2048, 2048), 2048)
+        return pltpu.make_async_copy(acts_hbm.at[rows], acts.at[rows], act_sem.at[n])
+    def x_load(j, k):
+        cols = pl.ds(pl.multiple_of(j * 256, 256), 256)
+        return [pltpu.make_async_copy(x_hbm.at[:, cols], xu.at[k % 2], load_sem.at[k % 2, 0])]
+    def u_load(j, k):
+        cols = pl.ds(pl.multiple_of(j * 256, 256), 256)
+        return [pltpu.make_async_copy(u_hbm.at[:, n, :, cols], xu.at[k % 2, pl.ds(2048 * n, 2048)].reshape(4, 512, 256),
+                                      load_sem.at[k % 2, n]) for n in range(2)]
+    act_load(1 - c).start()
+    act_load(c).start()
+    for cp in x_load(0, 0): cp.start()
     barrier = pltpu.get_barrier_semaphore()
-    near = [peer(1, 0), peer(-1, 0), peer(0, 1), peer(0, -1), partner]
+    near = [peer(1, 0), peer(-1, 0), peer(0, 1), peer(0, -1), partner, ypeer(1), ypeer(-1)]
     for p in near:
         pl.semaphore_signal(barrier, inc=1, device_id=p, device_id_type=MESH)
     pl.semaphore_wait(barrier, len(near))
-    H = slice(0, 32)
-    f32 = jnp.float32
-
-    def cols(k): return pl.ds(pl.multiple_of(k * 128, 128), 128)
-    def loads(k):
-        return [pltpu.make_async_copy(p.at[:, c, :, :, cols(k)], q.at[k, :, :, :, pl.ds(128 * i, 128)], load_sem.at[k, i])
-                for i, p in enumerate((p0, p1))]
+
     def sibs(k):
         return [pltpu.make_async_remote_copy(
-            src_ref=p.at[:, 1 - c, :, :, cols(k)], dst_ref=sib.at[k, :, :, :, pl.ds(128 * i, 128)],
-            send_sem=sib_send.at[k, i], recv_sem=sib_recv.at[k, i], device_id=partner, device_id_type=MESH)
-            for i, p in enumerate((p0, p1))]
+            src_ref=stage.at[k % 2], dst_ref=sib.at[k % 2],
+            send_sem=sib_send.at[k], recv_sem=sib_recv.at[k], device_id=partner, device_id_type=MESH)]
     def rc(k, n, src, dst, to):
         return pltpu.make_async_remote_copy(src_ref=src, dst_ref=dst, send_sem=ssem.at[k, n], recv_sem=rsem.at[k, n],
                                             device_id=to, device_id_type=MESH)
     def copies3(k):
-        return [rc(k, 0, q.at[k, zi(2), :, pl.ds(0, 32)], a3.at[k, 0], peer(1, 0)),
-                rc(k, 1, q.at[k, zi(2), :, pl.ds(32, 32)], a3.at[k, 1], peer(-1, 0)),
-                rc(k, 2, q.at[k, :, xi(2), pl.ds(64, 32)], b3.at[k, 0], peer(0, 1)),
-                rc(k, 3, q.at[k, :, xi(2), pl.ds(96, 32)], b3.at[k, 1], peer(0, -1))]
+        s = k % 4
+        return [rc(k, 0, q.at[k % 9, zi(2), :, pl.ds(0, 32)], a3.at[s, 0], peer(1, 0)),
+                rc(k, 1, q.at[k % 9, zi(2), :, pl.ds(32, 32)], a3.at[s, 1], peer(-1, 0)),
+                rc(k, 2, q.at[k % 9, :, xi(2), pl.ds(64, 32)], b3.at[s, 0], peer(0, 1)),
+                rc(k, 3, q.at[k % 9, :, xi(2), pl.ds(96, 32)], b3.at[s, 1], peer(0, -1))]
     def copies4(k):
-        return [rc(k, 4, q.at[k, zi(1), :, pl.ds(0, 64)], a4.at[k, 0], peer(1, 0)),
-                rc(k, 5, q.at[k, zi(-1), :, pl.ds(0, 64)], a4.at[k, 1], peer(-1, 0)),
-                rc(k, 6, q.at[k, :, xi(1), pl.ds(64, 64)], b4.at[k, 0], peer(0, 1)),
-                rc(k, 7, q.at[k, :, xi(-1), pl.ds(64, 64)], b4.at[k, 1], peer(0, -1))]
+        s = k % 4
+        return [rc(k, 4, q.at[k % 9, zi(1), :, pl.ds(0, 64)], a4.at[s, 0], peer(1, 0)),
+                rc(k, 5, q.at[k % 9, zi(-1), :, pl.ds(0, 64)], a4.at[s, 1], peer(-1, 0)),
+                rc(k, 6, q.at[k % 9, :, xi(1), pl.ds(64, 64)], b4.at[s, 0], peer(0, 1)),
+                rc(k, 7, q.at[k % 9, :, xi(-1), pl.ds(64, 64)], b4.at[s, 1], peer(0, -1))]
     def copies5(k):
-        return [rc(k, 8, q.at[k, z, xi(2), pl.ds(0, 32)], a5.at[k, 0], peer(0, 1)),
-                rc(k, 9, q.at[k, z, xi(2), pl.ds(32, 32)], a5.at[k, 1], peer(0, -1)),
-                rc(k, 10, q.at[k, zi(2), x, pl.ds(64, 32)], b5.at[k, 0], peer(1, 0)),
-                rc(k, 11, q.at[k, zi(2), x, pl.ds(96, 32)], b5.at[k, 1], peer(-1, 0))]
+        s = k % 4
+        return [rc(k, 8, q.at[k % 9, z, xi(2), pl.ds(0, 32)], a5.at[s, 0], peer(0, 1)),
+                rc(k, 9, q.at[k % 9, z, xi(2), pl.ds(32, 32)], a5.at[s, 1], peer(0, -1)),
+                rc(k, 10, q.at[k % 9, zi(2), x, pl.ds(64, 32)], b5.at[s, 0], peer(1, 0)),
+                rc(k, 11, q.at[k % 9, zi(2), x, pl.ds(96, 32)], b5.at[s, 1], peer(-1, 0))]
     def copies6(k):
-        return [rc(k, 12, q.at[k, z, xi(1), pl.ds(0, 64)], a6.at[k, 0], peer(0, 1)),
-                rc(k, 13, q.at[k, z, xi(-1), pl.ds(0, 64)], a6.at[k, 1], peer(0, -1)),
-                rc(k, 14, q.at[k, zi(1), x, pl.ds(64, 64)], b6.at[k, 0], peer(1, 0)),
-                rc(k, 15, q.at[k, zi(-1), x, pl.ds(64, 64)], b6.at[k, 1], peer(-1, 0))]
+        s = k % 4
+        return [rc(k, 12, q.at[k % 9, z, xi(1), pl.ds(0, 64)], a6.at[s, 0], peer(0, 1)),
+                rc(k, 13, q.at[k % 9, z, xi(-1), pl.ds(0, 64)], a6.at[s, 1], peer(0, -1)),
+                rc(k, 14, q.at[k % 9, zi(1), x, pl.ds(64, 64)], b6.at[s, 0], peer(1, 0)),
+                rc(k, 15, q.at[k % 9, zi(-1), x, pl.ds(64, 64)], b6.at[s, 1], peer(-1, 0))]
     def add(k, i, j, rows, *terms):
-        t = q[k, i, j, rows].astype(f32)
+        t = q[k % 9, i, j, rows].astype(f32)
         for s in terms:
             t = t + s.astype(f32)
-        q[k, i, j, rows] = t.astype(jnp.bfloat16)
-
-    def stage1(k):
+        q[k % 9, i, j, rows] = t.astype(low)
+
+    def compute(k):
+        cols = pl.ds(pl.multiple_of((k // 2) * 256, 256), 256)
+        def piece(cc, put):
+            rows = pl.ds(pl.multiple_of(cc * 2048, 2048), 2048)
+            @pl.when(k == 0)
+            def _(): act_load(cc).wait()
+            @pl.when(k % 2 == 0)
+            def _():
+                put(jnp.dot(acts[rows, 0:wide], down_ref[:, cols], preferred_element_type=f32))
+            @pl.when(k % 2 == 1)
+            def _():
+                put(lax.dot_general(acts[rows, wide:], w_ref[cols, :], (((1,), (1,)), ((), ())),
+                                    preferred_element_type=f32))
+        def put_stage(r):
+            stage[k % 2] = r.astype(low).reshape(4, 4, 128, 256)
+        def put_own(r):
+            q[k % 9] = r.astype(low).reshape(4, 4, 128, 256)
+        piece(1 - c, put_stage)
         for cp in sibs(k): cp.start()
-        for cp in loads(k): cp.start()
+        piece(c, put_own)
+
+    def weight_part(k):
+        @pl.when(k % 2 == 0)
+        def _():
+            for cp in x_load(0, k): cp.wait()
+            for cp in u_load(k // 2, k + 1): cp.start()
+        @pl.when(k % 2 == 1)
+        def _():
+            for cp in u_load(0, k): cp.wait()
+        @pl.when((k + 1 < nk) & (k % 2 == 1))
+        def _():
+            for cp in x_load(k // 2 + 1, k + 1): cp.start()
+        slot = (k // 2) % 3
+        def make(lanes):
+            return lax.dot_general(xu[k % 2], acts[:, lanes], (((0,), (0,)), ((), ())), preferred_element_type=f32)
+        @pl.when(k % 2 == 0)
+        def _():
+            acc[...] = make(slice(wide, None))
+            dwb[slot, :, :, 0 : 2 * wide] = acc[:, 0 : 2 * wide].astype(low).reshape(4, 64, 2 * wide)
+            router_out[pl.ds(pl.multiple_of((k // 2) * 256, 256), 256), :] = acc[:, 2 * wide :]
+        @pl.when(k % 2 == 1)
+        def _():
+            acc[:, 0:wide] = make(slice(0, wide))
+            dwb[slot, :, :, 2 * wide :] = acc[:, 0:wide].astype(low).reshape(4, 64, wide)
+
+    def yrc(j, n, src, dst, to):
+        return pltpu.make_async_remote_copy(src_ref=src, dst_ref=dst, send_sem=ysend.at[j, n], recv_sem=yrecv.at[j, n],
+                                            device_id=to, device_id_type=MESH)
+    def ycopies1(j):
+        s = j % 3
+        return [yrc(j, 0, dwb.at[s, yi(2), pl.ds(0, 32)], ya.at[j % 4, 0], ypeer(1)),
+                yrc(j, 1, dwb.at[s, yi(2), pl.ds(32, 32)], ya.at[j % 4, 1], ypeer(-1))]
+    def ycopies2(j):
+        s = j % 3
+        return [yrc(j, 2, dwb.at[s, yi(1)], yb.at[j % 4, 0], ypeer(1)),
+                yrc(j, 3, dwb.at[s, yi(-1)], yb.at[j % 4, 1], ypeer(-1))]
+    def ystage1(j):
+        for cp in ycopies1(j): cp.start()
+    def ystage2(j):
+        for cp in ycopies1(j): cp.wait_recv()
+        s = j % 3
+        for d, r, m in ((1, 0, 0), (-1, 32, 1)):
+            dwb[s, yi(d), pl.ds(r, 32)] = (dwb[s, yi(d), pl.ds(r, 32)].astype(f32) + ya[j % 4, m].astype(f32)).astype(low)
+        for cp in ycopies2(j): cp.start()
+    def ystage3(j):
+        for cp in ycopies2(j): cp.wait_recv()
+        dw_out[j] = (dwb[j % 3, y].astype(f32) + yb[j % 4, 0].astype(f32) + yb[j % 4, 1].astype(f32)).astype(low)
+        for cp in ycopies1(j) + ycopies2(j): cp.wait_send()
+
     def stage2(k):
-        for cp in loads(k): cp.wait()
-        for cp in sibs(k): cp.wait_recv()
+        for cp in sibs(k): cp.wait()
         def body(n, _):
-            add(k, n // 4, n % 4, pl.ds(0, 128), sib[k, n // 4, n % 4])
+            add(k, n // 4, n % 4, pl.ds(0, 128), sib[k % 2, n // 4, n % 4])
             return 0
         lax.fori_loop(0, 16, body, 0)
         for cp in copies3(k): cp.start()
     def stage4(k):
         for cp in copies3(k): cp.wait_recv()
+        s = k % 4
         def body(n, _):
-            add(k, zi(1), n, pl.ds(0, 32), a3[k, 0, n])
-            add(k, zi(-1), n, pl.ds(32, 32), a3[k, 1, n])
-            add(k, n, xi(1), pl.ds(64, 32), b3[k, 0, n])
-            add(k, n, xi(-1), pl.ds(96, 32), b3[k, 1, n])
+            add(k, zi(1), n, pl.ds(0, 32), a3[s, 0, n])
+            add(k, zi(-1), n, pl.ds(32, 32), a3[s, 1, n])
+            add(k, n, xi(1), pl.ds(64, 32), b3[s, 0, n])
+            add(k, n, xi(-1), pl.ds(96, 32), b3[s, 1, n])
             return 0
         lax.fori_loop(0, 4, body, 0)
         for cp in copies4(k): cp.start()
     def stage5(k):
         for cp in copies4(k): cp.wait_recv()
+        s = k % 4
         def body(n, _):
-            add(k, z, n, pl.ds(0, 64), a4[k, 0, n], a4[k, 1, n])
-            add(k, n, x, pl.ds(64, 64), b4[k, 0, n], b4[k, 1, n])
+            add(k, z, n, pl.ds(0, 64), a4[s, 0, n], a4[s, 1, n])
+            add(k, n, x, pl.ds(64, 64), b4[s, 0, n], b4[s, 1, n])
             return 0
         lax.fori_loop(0, 4, body, 0)
         for cp in copies5(k): cp.start()
     def stage6(k):
         for cp in copies5(k): cp.wait_recv()
-        add(k, z, xi(1), pl.ds(0, 32), a5[k, 0])
-        add(k, z, xi(-1), pl.ds(32, 32), a5[k, 1])
-        add(k, zi(1), x, pl.ds(64, 32), b5[k, 0])
-        add(k, zi(-1), x, pl.ds(96, 32), b5[k, 1])
+        s = k % 4
+        add(k, z, xi(1), pl.ds(0, 32), a5[s, 0])
+        add(k, z, xi(-1), pl.ds(32, 32), a5[s, 1])
+        add(k, zi(1), x, pl.ds(64, 32), b5[s, 0])
+        add(k, zi(-1), x, pl.ds(96, 32), b5[s, 1])
         for cp in copies6(k): cp.start()
     def stage7(k):
         for cp in copies6(k): cp.wait_recv()
+        s = k % 4
         for h, m in ((0, a6), (64, b6)):
-            t = q[k, z, x, pl.ds(h, 64)].astype(f32) + m[k, 0].astype(f32) + m[k, 1].astype(f32)
-            out[0, pl.ds(h, 64), cols(k)] = t[:, :128]
-            out[1, pl.ds(h, 64), cols(k)] = t[:, 128:]
-        for cp in sibs(k) + copies3(k) + copies4(k) + copies5(k) + copies6(k): cp.wait_send()
+            t = q[k % 9, z, x, pl.ds(h, 64)].astype(f32) + m[s, 0].astype(f32) + m[s, 1].astype(f32)
+            out[k % 2, pl.ds(h, 64), pl.ds(pl.multiple_of((k // 2) * 256, 256), 256)] = t
+        for cp in copies3(k) + copies4(k) + copies5(k) + copies6(k): cp.wait_send()
+
     def step(i, _):
-        for lag, st in ((8, stage7), (7, stage6), (5, stage5), (3, stage4), (1, stage2), (0, stage1)):
+        for lag, st in ((8, stage7), (7, stage6), (5, stage5), (3, stage4), (1, stage2)):
             k = i - lag
             @pl.when((k >= 0) & (k < nk))
             def _():
                 st(k)
+        for lag, st in ((5, ystage3), (3, ystage2)):
+            k = i - lag
+            @pl.when((k >= 0) & (k < nk) & (k % 2 == 0))
+            def _():
+                st(k // 2)
+        @pl.when(i < nk)
+        def _():
+            compute(i)
+            weight_part(i)
+            @pl.when(i % 2 == 1)
+            def _():
+                ystage1(i // 2)
         return 0
     lax.fori_loop(0, nk + 8, step, 0)
 
-def rs_plane(p0, p1, cid, nk=12):
+
+def expert_back(acts, x, u, w_all, down, cid):
     bf = jnp.bfloat16
-    width = p0.shape[-1]
-    p0 = p0.reshape(4, 2, 4, 128, width); p1 = p1.reshape(4, 2, 4, 128, width)
     V = pltpu.VMEM
+    nk = 12
+    u = u.reshape(4, 2, 512, 1536)
+    D = pltpu.SemaphoreType.DMA
+    vm = pl.BlockSpec(memory_space=pltpu.VMEM)
+    anym = pl.BlockSpec(memory_space=pl.ANY)
     return pl.pallas_call(
-        functools.partial(rs_plane_kernel, nk),
-        out_shape=jax.ShapeDtypeStruct((2, 128, width), jnp.float32),
-        in_specs=[pl.BlockSpec(memory_space=pl.ANY)] * 2,
-        out_specs=pl.BlockSpec(memory_space=pltpu.VMEM),
-        scratch_shapes=[V((nk, 4, 4, 128, 256), bf), V((nk, 4, 4, 128, 256), bf),
-                        V((nk, 2, 4, 32, 256), bf), V((nk, 2, 4, 32, 256), bf),
-                        V((nk, 2, 4, 64, 256), bf), V((nk, 2, 4, 64, 256), bf),
-                        V((nk, 2, 32, 256), bf), V((nk, 2, 32, 256), bf),
-                        V((nk, 2, 64, 256), bf), V((nk, 2, 64, 256), bf),
-                        pltpu.SemaphoreType.DMA((nk, 2)), pltpu.SemaphoreType.DMA((nk, 2)), pltpu.SemaphoreType.DMA((nk, 2)),
-                        pltpu.SemaphoreType.DMA((nk, 16)), pltpu.SemaphoreType.DMA((nk, 16))],
-        compiler_params=pltpu.CompilerParams(collective_id=cid, has_side_effects=True, vmem_limit_bytes=56 << 20),
-        name="rs_plane",
-    )(p0, p1)
+        expert_back_kernel,
+        out_shape=(jax.ShapeDtypeStruct((2, 128, 1536), jnp.float32),
+                   jax.ShapeDtypeStruct((6, 64, 1920), bf),
+                   jax.ShapeDtypeStruct((1536, 128), jnp.float32)),
+        in_specs=[anym, anym, anym, vm, vm],
+        out_specs=(vm, vm, vm),
+        scratch_shapes=[V((4096, 2048), bf), V((2, 4, 4, 128, 256), bf), V((9, 4, 4, 128, 256), bf), V((2, 4, 4, 128, 256), bf),
+                        V((4, 2, 4, 32, 256), bf), V((4, 2, 4, 32, 256), bf),
+                        V((4, 2, 4, 64, 256), bf), V((4, 2, 4, 64, 256), bf),
+                        V((4, 2, 32, 256), bf), V((4, 2, 32, 256), bf),
+                        V((4, 2, 64, 256), bf), V((4, 2, 64, 256), bf),
+                        V((2, 4096, 256), bf), V((256, 1408), jnp.float32), V((3, 4, 64, 1920), bf),
+                        V((4, 2, 32, 1920), bf), V((4, 2, 64, 1920), bf),
+                        D((2,)), D((2, 2)), D((nk,)), D((nk,)), D((nk, 16)), D((nk, 16)), D((6, 4)), D((6, 4))],
+        compiler_params=pltpu.CompilerParams(collective_id=cid, has_side_effects=True, vmem_limit_bytes=63 << 20),
+        name="expert_back",
+    )(acts, x, u, w_all, down)
 
 
 def shards(
@@ -399,69 +570,27 @@
         raised = jnp.exp(logits - jnp.max(logits, -1, keepdims=True))
         return raised / jnp.sum(raised, -1, keepdims=True)
 
-    first_expert = lax.axis_index("expert") * local_experts
-    plane_gates = lax.dynamic_slice_in_dim(
-        dense_gates(plane_rows, plane_routes), first_expert, local_experts, 1
-    )
-    plane_len = plane_rows.shape[0]
     hidden = gate_weight.shape[2]
     wide = local_experts * hidden
-    gate_flat = gate_weight.transpose(1, 0, 2).reshape(width, wide)
-    up_flat = up_weight.transpose(1, 0, 2).reshape(width, wide)
+    router_pad = jnp.pad(router_weight, ((0, 0), (0, 64 - experts_all)))
+    in_weights = jnp.concatenate(
+        [
+            gate_weight.transpose(1, 0, 2).reshape(width, wide),
+            up_weight.transpose(1, 0, 2).reshape(width, wide),
+            router_pad,
+            router_pad,
+        ],
+        1,
+    )
     down_flat = down_weight.reshape(wide, width)
-    gate_pre = jnp.dot(plane_rows, gate_flat, preferred_element_type=jnp.float32)
-    up_pre = jnp.dot(plane_rows, up_flat, preferred_element_type=jnp.float32)
-    raw_grad = jnp.einsum(
-        "td,fd->tf", plane_upstream, down_flat, preferred_element_type=jnp.float32
-    )
-    gates_wide = jnp.repeat(plane_gates, hidden, axis=1)
-    sigmoid_gate = jax.nn.sigmoid(gate_pre)
-    silu_gate = gate_pre * sigmoid_gate
-    activated = silu_gate * up_pre
-    gate_grad_part = jnp.sum(
-        (activated * raw_grad).reshape(plane_len, local_experts, hidden), -1
-    )
-    gated = (gates_wide * activated).astype(jnp.bfloat16)
-    act_grad = gates_wide * raw_grad
-    gate_pre_grad = (
-        act_grad * up_pre * sigmoid_gate * (1.0 + gate_pre * (1.0 - sigmoid_gate))
-    ).astype(jnp.bfloat16)
-    up_pre_grad = (act_grad * silu_gate).astype(jnp.bfloat16)
-    mixture_part = jnp.dot(gated, down_flat, preferred_element_type=jnp.float32)
-    rows_part = jnp.einsum(
-        "tf,df->td", gate_pre_grad, gate_flat, preferred_element_type=jnp.float32
-    ) + jnp.einsum("tf,df->td", up_pre_grad, up_flat, preferred_element_type=jnp.float32)
-    weighted = plane_gates * gate_grad_part
-    weighted_high = weighted.astype(jnp.bfloat16)
-    weighted_low = (weighted - weighted_high.astype(jnp.float32)).astype(jnp.bfloat16)
-    own_router = lax.dynamic_slice_in_dim(router_weight, first_expert, local_experts, 1)
-    rows_part = rows_part + jnp.einsum(
-        "te,de->td", weighted_high, own_router, preferred_element_type=jnp.float32
-    )
-    mixture, route_rows = rs_plane(
-        mixture_part.astype(jnp.bfloat16), rows_part.astype(jnp.bfloat16), 2
-    )
+    acts = expert_forward(plane_rows, plane_upstream, plane_routes, in_weights, down_flat)
+    sums, weight_grads, router_pairs = expert_back(
+        acts, plane_rows, plane_upstream, in_weights, down_flat, 2
+    )
+    mixture, route_rows = sums[0], sums[1]
     layer_output = (residual + mixture).astype(jnp.bfloat16)
-    router_pairs = jnp.einsum(
-        "td,te->de",
-        plane_rows,
-        jnp.concatenate([weighted_high, weighted_low], 1),
-        preferred_element_type=jnp.float32,
-    )
-    router_pairs = router_pairs[:, :local_experts] + router_pairs[:, local_experts:]
-    down_local = jnp.einsum(
-        "tf,td->fd", gated, plane_upstream, preferred_element_type=jnp.float32
-    ).reshape(local_experts, hidden, width)
-    gate_local = (
-        jnp.einsum("td,tf->df", plane_rows, gate_pre_grad, preferred_element_type=jnp.float32)
-        .reshape(width, local_experts, hidden)
-        .transpose(1, 0, 2)
-    )
-    up_local = (
-        jnp.einsum("td,tf->df", plane_rows, up_pre_grad, preferred_element_type=jnp.float32)
-        .reshape(width, local_experts, hidden)
-        .transpose(1, 0, 2)
-    )
+    router_pairs = router_pairs[:, :experts_all] + router_pairs[:, 64 : 64 + experts_all]
+    weight_grads = lax.all_gather(weight_grads, "dp", axis=0)
     gates = dense_gates(second_low, expert_routes)
     upstream = out_cotangent.astype(jnp.float32)
     shared = gates * jnp.sum(mixture * upstream, -1, keepdims=True)
@@ -471,9 +600,7 @@
         shared,
         precision=highest,
         preferred_element_type=jnp.float32,
-    ) + lax.dynamic_update_slice_in_dim(
-        jnp.zeros((width, experts_all), jnp.float32), router_pairs, first_expert, 1
-    )
+    ) + router_pairs
     normed_back = route_rows - jnp.einsum(
         "te,de->td",
         shared,
@@ -565,11 +692,14 @@
     router_gradient, attention_gain_gradient, expert_gain_gradient = lax.psum(
         (router_local, attention_gain_local, expert_gain_local), ("dp", "expert", "tensor")
     )
-    gate_gradient, up_gradient, down_gradient = (
-        lax.psum(gate_local.astype(jnp.bfloat16), "dp").astype(jnp.float32),
-        lax.psum(up_local.astype(jnp.bfloat16), "dp").astype(jnp.float32),
-        lax.psum(down_local.astype(jnp.bfloat16), "dp").astype(jnp.float32),
-    )
+    weight_grads = weight_grads.transpose(1, 0, 2, 3).reshape(width, 3 * wide).astype(jnp.float32)
+    gate_gradient, up_gradient = (
+        weight_grads[:, part : part + wide]
+        .reshape(width, local_experts, hidden)
+        .transpose(1, 0, 2)
+        for part in (0, wide)
+    )
+    down_gradient = weight_grads[:, 2 * wide :].T.reshape(local_experts, hidden, width)
     return (
         layer_output,
         input_gradient,

time: 862 us -> 804 us (0.933)
  matrix products: 200 us -> 38.6 us
  Pallas kernels: 140 us -> 206 us
  local copies, waits for them, and re-layouts: 13.8 us -> 72.9 us
  other arithmetic: 57.2 us -> 36 us
  waiting for transfers between devices: 319 us -> 309 us
    dot_general x11 -> x0, matrix products: 155 us -> none  [the longest x1 22 us: shards(): jnp.einsum('te,de->td', weighted_high, own_router, preferred_element_type...]
    pallas_call x1 -> x2, Pallas kernels: 82.6 us -> 156 us  [the longest x1 115 us: expert_back(): pl.pallas_call(expert_back_kernel, out_shape=(jax.ShapeDtypeStruct((2, 12...]
    psum x1, waiting for transfers between devices: 53.7 us -> 111 us  [shards(): lax.psum(query_local.astype(jnp.bfloat16), ('dp', 'expert'))]
    psum x1 -> x0, waiting for transfers between devices: 53.5 us -> none  [shards(): lax.psum(gate_local.astype(jnp.bfloat16), 'dp').astype(jnp.float32)]
    transpose x0 -> x2, local copies, waits for them, and re-layouts: none -> 14.7 us  [shards(): weight_grads[:, 2 * wide:].T.reshape(local_experts, hidden, width)]
    psum x1, waiting for transfers between devices: 138 us -> 123 us  [shards(): lax.psum((router_local, attention_gain_local, expert_gain_local), ('dp',...]
    convert_element_type x5 -> x1, other arithmetic: 22 us -> 8.42 us  [shards(): weight_grads.transpose(1, 0, 2, 3).reshape(width, 3 * wide)]
    slice x0 -> x2, local copies, waits for them, and re-layouts: none -> 11 us  [shards(): weight_grads[:, part:part + wide].reshape(width, local_experts, hidden)]
  transfers between devices with their start and end apart: 8 -> 8, of which waited for: 6 -> 5; matrix products, arithmetic and copies ran while one was open for 14% -> 9% of each run, Pallas kernels for 7% -> 6%
where the time goes in v3:
time: 804 us; the launch traced here: 795 us
  waiting for transfers between devices  309 us (38%)
  Pallas kernels  206 us (26%)
  blocking collectives  116 us (14%)
  local copies, waits for them, and re-layouts  72.9 us (9%)
  matrix products  38.6 us (5%)
  other arithmetic  36 us (4%)
  between operations  16.8 us (2%)
    psum x1, waiting for transfers between devices, shards(): lax.psum((router_local, attention_gain_local, expert_gain_local), ('dp',...  123 us
    pallas_call x1, Pallas kernels, expert_back(): pl.pallas_call(expert_back_kernel, out_shape=(jax.ShapeDtypeStruct((2, 12...  115 us
    psum x1, waiting for transfers between devices, shards(): lax.psum(query_local.astype(jnp.bfloat16), ('dp', 'expert'))  111 us
    psum x1, blocking collectives, shards(): lax.psum((router_local, attention_gain_local, expert_gain_local), ('dp',...  67.4 us
    pallas_call x1, Pallas kernels, ag_plane(): pl.pallas_call(ag_plane_kernel, out_shape=jax.ShapeDtypeStruct((32, rows,...  49.3 us
    all_gather x1, blocking collectives, shards(): plane_routes = lax.all_gather(expert_routes, plane, axis=0, tiled=True)  48.7 us
    pallas_call x1, Pallas kernels, expert_forward(): pl.pallas_call(expert_forward_kernel, grid=(rows // block,), out_shape=ja...  41.2 us
    all_gather x1, waiting for transfers between devices, shards(): lax.all_gather(first_normed.astype(jnp.bfloat16), 'tensor', axis=0, tiled...  27.6 us
  transfers between devices with their start and end apart: 8, of which 5 were waited for; matrix products, arithmetic and copies ran while one was open for 9% of the time, Pallas kernels for 6%

profile of v3, /device:TPU:1, one launch (start us, length us, event | category | flops | bytes accessed | tf_op | source)
XLA Modules:
  0.0 795.1 jit_solution(12609941108008144766)
XLA Ops:
  8.1 1.2 fusion.25
  9.8 0.7 convert_element_type.128
  10.5 1.9 fusion.27
  12.4 0.9 convert_reduce_fusion
  13.7 1.0 fusion.20
  14.7 27.6 %all-gather.6.cloned.1.call-done = bf16[512,1536]{1,0:T(8,128)(2,1)} async-done(((bf16[128,1536]{1,0:T(8,128)(2,1)}), bf16[512,1536]{1,0:T(8,128)(2,1)}) %all-gather.6.cloned.1.call-update) | async-done | bytes 1572880 | tf_op jit(solution)/shard_map/all_gather | solution.py:502
  42.2 2.7 fusion.42
  45.1 0.7 fusion.41
  45.8 1.2 fusion.39
  47.1 0.9 fusion.3
  48.4 0.7 convolution_convert_fusion.6
  49.1 0.7 copy-done.2
  49.8 1.2 fusion.11
  51.1 2.1 convolution_convert_fusion
  53.9 2.3 copy.114
  56.2 2.8 copy.117
  59.0 4.0 copy.115
  63.0 4.0 copy.118
  67.4 7.1 concatenate.28.w_ref
  74.6 48.7 %all_gather.20.routes_ref = s32[4096,8]{1,0:T(8,128)S(1)} all-gather(s32[128,8]{1,0:T(8,128)S(1)} %copy.113), channel_id=1, replica_groups=mesh['dp'=4,'expert'=8,'tensor'=4] {'expert','tensor'}, dimensions={0}, use_global_device_ids=true | all-gather | bytes 135168 | tf_op jit(solution)/shard_map/all_gather | solution.py:562
  123.3 1.2 multiply_reduce_fusion.2
  125.1 1.9 multiply_convert_fusion.src
  127.0 49.3 %ag_plane.1 = bf16[32,128,1536]{2,1,0:T(8,128)(2,1)} custom-call(bf16[128,1536]{1,0:T(8,128)(2,1)} %multiply_convert_fusion.src), custom_call_target="tpu_custom_call" | custom-call | tf_op jit(solution)/shard_map/ag_plane/pallas_call | solution.py:160
  176.4 1.2 fusion.40
  178.1 1.5 copy-done.1
  179.6 41.2 %expert_forward.1.acts_hbm = bf16[4096,2048]{1,0:T(8,128)(2,1)} custom-call(bf16[4096,1536]{1,0:T(8,128)(2,1)} %bitcast.120, bf16[4096,1536]{1,0:T(8,128)(2,1)} %all-gather.8.cloned.1.call-done.u_ref, s32[4096,8]{1,0:T(8,128)S(1)} %all_gather.20.routes_ref, bf16[1536,1408]{1,0:T(8,128)(2,1)} %concatenate.28.w_ref, bf16[640,1536]{1,0:T(8,128)(2,1)S(1)} %bitcast.119), custom_call_target="tpu_custom_call" | custom-call | tf_op jit(solution)/shard_map/expert_forward/pallas_call | solution.py:220
  220.8 115.1 %expert_back.1 = (f32[2,128,1536]{2,1,0:T(8,128)}, bf16[6,64,1920]{2,1,0:T(8,128)(2,1)}, f32[1536,128]{1,0:T(8,128)}) custom-call(bf16[4096,2048]{1,0:T(8,128)(2,1)} %expert_forward.1.acts_hbm, bf16[4096,1536]{1,0:T(8,128)(2,1)} %bitcast.121, bf16[4,2,512,1536]{3,2,1,0:T(8,128)(2,1)} %bitcast.124, bf16[1536,1408]{1,0:T(8,128)(2,1)} %concatenate.28.w_ref, ...), custom_call_target="tpu_custom_call" | custom-call | tf_op jit(solution)/shard_map/expert_back/pallas_call | solution.py:452
  336.0 2.4 fusion.24
  338.3 2.2 multiply_reduce_fusion
  340.6 1.1 fusion.38
  341.8 2.9 fusion.10
  344.7 25.1 %all-gather.10.cloned.1.call-done = bf16[512,1536]{1,0:T(8,128)(2,1)} async-done(((bf16[128,1536]{1,0:T(8,128)(2,1)}), bf16[512,1536]{1,0:T(8,128)(2,1)}) %all-gather.10.cloned.1.call-update) | async-done | bytes 1572880 | tf_op jit(solution)/shard_map/all_gather | solution.py:613
  369.8 2.5 convolution_convert_fusion.5
  372.4 4.0 fusion.17
  376.5 4.3 fusion
  380.8 1.8 fusion.2
  382.7 1.1 fusion.16
  383.8 0.7 convolution_multiply_fusion
  385.3 1.8 convolution_convert_fusion.1
  387.1 1.4 convolution_convert_fusion.3
  388.5 2.0 convolution_convert_fusion.2
  390.5 1.4 convolution_convert_fusion.4
  392.3 2.3 fusion.43
  395.6 1.8 fusion.9
  397.4 0.7 all-gather.12.cloned.1.call-update
  398.1 123.4 %all-reduce.6.cloned.1.call-done = f32[1536,40]{1,0:T(8,128)} async-done(((f32[1536,40]{1,0:T(8,128)}), f32[1536,40]{1,0:T(8,128)}) %all-reduce.6.cloned.1.call-update) | async-done | bytes 245776 | tf_op jit(solution)/shard_map/psum | solution.py:692
  521.5 2.1 copy.127
  523.5 110.6 %all-reduce.8.cloned.1.call-done = (bf16[1536,384]{1,0:T(8,128)(2,1)}, bf16[1536,128]{1,0:T(8,128)(2,1)}, bf16[1536,128]{1,0:T(8,128)(2,1)}, bf16[384,1536]{1,0:T(8,128)(2,1)}) async-done(((bf16[1536,384]{1,0:T(8,128)(2,1)}, bf16[1536,128]{1,0:T(8,128)(2,1)}, bf16[1536,128]{1,0:T(8,128)(2,1)}, bf16[384,1536]{1,0:T(8,128)(2,1)}), (bf16[1536,384]{1,0:T(8,128)(2,1)}, bf16[1536,128]{1,0:T(8,128)(2,1)}, ...) | async-done | bytes 3145744 | tf_op jit(solution)/shard_map/psum | solution.py:687
  634.2 2.9 convert_element_type.153
  637.2 1.7 convert_element_type.159
  638.9 0.9 convert_element_type.155
  639.8 0.9 convert_element_type.157
  640.7 20.5 %reduce-scatter.5.cloned.1.call-done = bf16[128,1536]{1,0:T(8,128)(2,1)} async-done(((bf16[512,1536]{1,0:T(8,128)(2,1)}), bf16[128,1536]{1,0:T(8,128)(2,1)}) %reduce-scatter.5.cloned.1.call-update) | async-done | bytes 393232 | tf_op jit(solution)/shard_map/reduce_scatter | solution.py:681
  661.3 1.3 fusion.31
  662.5 67.4 %all-reduce.1 = (f32[1536]{0:T(1024)}, f32[1536]{0:T(1024)}) all-reduce(f32[1536]{0:T(1024)S(1)} %get-tuple-element.149, f32[1536]{0:T(1024)S(1)} %get-tuple-element.147), channel_id=1, replica_groups=mesh['dp'=4,'expert'=8,'tensor'=4] {'dp','expert','tensor'}, use_global_device_ids=true, to_apply=%region_15.16 | all-reduce | flops 3072 | bytes 24576 | tf_op jit(solution)/shard_map/psum | solution.py:692
  729.9 2.5 fusion.23
  732.4 8.4 %convert_bitcast_fusion = f32[6,4,64,1920]{3,2,0,1:T(8,128)} fusion(bf16[4,6,64,1920]{3,2,1,0:T(8,128)(2,1)} %bitcast.130), kind=kLoop, calls=%fused_computation | loop fusion | flops 2949120 | bytes 17694720 | tf_op jit(solution)/shard_map/convert_element_type | solution.py:695
  740.8 9.9 %copy.123 = f32[6,4,64,1920]{3,2,1,0:T(8,128)} copy(f32[6,4,64,1920]{3,2,0,1:T(8,128)} %convert_bitcast_fusion) | data formatting | bytes 23592960 | tf_op jit(solution)/shard_map/convert_element_type | solution.py:695
  750.7 9.2 %slice_bitcast_fusion = (f32[640,1536]{0,1:T(8,128)}, f32[1536,640]{1,0:T(8,128)}, f32[1536,640]{1,0:T(8,128)}) fusion(f32[1536,1920]{1,0:T(8,128)} %bitcast.125), kind=kLoop, calls=%fused_computation.12 | loop fusion | bytes 23592960 | tf_op jit(solution)/shard_map/transpose | solution.py:702
  759.9 5.5 copy.124
  765.4 5.4 copy.128
  770.8 5.5 copy.125
  776.3 5.4 copy.129
  781.8 5.4 copy.126
  (124 shorter events, 6.2 us)
Async XLA Ops:
  8.0 37.1 %copy-start = (bf16[1536,128]{1,0:T(8,128)(2,1)S(1)}, bf16[1536,128]{1,0:T(8,128)(2,1)}, u32[]{:S(2)}) copy-start(bf16[1536,128]{1,0:T(8,128)(2,1)} %param.19) | copy-start | bytes 1179652
  8.0 34.2 %all-gather.6.cloned.1.call-start = ((), (), s32[]{:S(2)}) async-start(), calls=%async_computation.2 | async-start | bytes 1966080 | tf_op jit(solution)/shard_map/all_gather | solution.py:502
  12.4 110.9 %reduce-scatter.3.cloned.1.call-start = ((), (), s32[]{:S(2)}) async-start(), calls=%async_computation.3 | async-start | bytes 1966080 | tf_op jit(solution)/shard_map/reduce_scatter | solution.py:553
  42.2 2.8 copy-start.4
  45.1 2.0 copy-start.16
  45.1 2.0 copy-start.18
  45.8 1.3 copy-start.26
  45.8 1.3 copy-start.28
  47.1 2.7 copy-start.2
  47.1 1.3 copy-start.11
  48.4 2.6 copy-start.30
  49.1 2.0 copy-start.20
  49.8 1.3 copy-start.13
  51.0 5.1 copy-start.22
  51.0 2.8 copy-start.34
  51.0 2.8 copy-start.10
  53.2 124.9 %all-gather.8.cloned.1.call-start = ((), (), s32[]{:S(2)}) async-start(), calls=%async_computation.4 | async-start | bytes 12976128 | tf_op jit(solution)/shard_map/all_gather | solution.py:563
  53.8 316.0 %all-gather.10.cloned.1.call-start = ((), (), s32[]{:S(2)}) async-start(), calls=%async_computation.5 | async-start | bytes 1966080 | tf_op jit(solution)/shard_map/all_gather | solution.py:613
  59.0 8.0 %copy-start.15 = (bf16[1536,40]{0,1:T(8,128)(2,1)S(1)}, bf16[1536,40]{0,1:T(8,128)(2,1)}, u32[]{:S(2)}) copy-start(bf16[1536,40]{0,1:T(8,128)(2,1)} %param.23) | copy-start | bytes 368644
  63.0 4.2 copy-start.32
  67.4 55.9 %copy-start.3 = (bf16[128,1536]{1,0:T(8,128)(2,1)S(1)}, bf16[128,1536]{1,0:T(8,128)(2,1)}, u32[]{:S(2)}) copy-start(bf16[128,1536]{1,0:T(8,128)(2,1)} %param.14) | copy-start | bytes 1179652
  127.0 49.3 %copy-start.8 = (bf16[128,1536]{1,0:T(8,128)(2,1)S(1)}, bf16[128,1536]{1,0:T(8,128)(2,1)}, u32[]{:S(2)}) copy-start(bf16[128,1536]{1,0:T(8,128)(2,1)} %multiply_convert_fusion.src) | copy-start | bytes 1179652
  178.1 1.5 copy-start.1
  335.9 4.6 copy-start.6
  336.0 4.6 copy-start.7
  336.0 4.6 copy-start.35
  338.3 3.4 copy-start.31
  338.3 3.5 copy-start.9
  338.3 3.5 copy-start.33
  340.5 31.9 %copy-start.37 = (f32[128]{0:T(128)}, f32[128]{0:T(128)S(1)}, u32[]{:S(2)}) copy-start(f32[128]{0:T(128)S(1)} %broadcast_multiply_fusion.1) | copy-start | bytes 1540
  341.7 179.8 %all-reduce.6.cloned.1.call-start = ((), (), s32[]{:S(2)}) async-start(), calls=%async_computation.7 | async-start | bytes 1572864 | tf_op jit(solution)/shard_map/psum | solution.py:692
  344.7 289.5 %all-reduce.8.cloned.1.call-start = ((), (), s32[]{:S(2)}) async-start(), calls=%async_computation.9 | async-start | bytes 6291456 | tf_op jit(solution)/shard_map/psum | solution.py:687
  372.4 4.0 copy-start.21
  372.4 8.4 %slice-start = ((s8[6291456]{0:T(1024)(128)(4,1)}), s8[4194304]{0:T(1024)(128)(4,1)S(1)}, s32[]{:S(2)}) async-start(s8[6291456]{0:T(1024)(128)(4,1)} %bitcast.122), calls=%async_computation.10 | async-start | bytes 8388608
  376.5 4.3 slice-start.1
  380.8 1.9 copy-start.17
  380.8 1.9 copy-start.19
  382.7 1.1 copy-start.27
  382.7 1.1 copy-start.29
  383.8 1.0 copy-start.23
  383.8 1.5 copy-start.40
  384.5 2.6 copy-start.5
  391.9 269.3 %reduce-scatter.5.cloned.1.call-start = ((), (), s32[]{:S(2)}) async-start(), calls=%async_computation.6 | async-start | bytes 1966080 | tf_op jit(solution)/shard_map/reduce_scatter | solution.py:681
  394.6 1.0 copy-start.12
  397.3 335.1 %all-gather.12.cloned.1.call-start = ((), (), s32[]{:S(2)}) async-start(), calls=%async_computation.8 | async-start | bytes 7372800 | tf_op jit(solution)/shard_map/all_gather | solution.py:593
  634.2 3.0 copy-start.14
  634.2 4.7 copy-start.25
  637.1 2.7 copy-start.24
  637.1 92.8 %copy-start.36 = (f32[128]{0:T(128)S(1)}, f32[128]{0:T(128)}, u32[]{:S(2)}) copy-start(f32[128]{0:T(128)} %get-tuple-element.174) | copy-start | bytes 1540
  637.1 92.8 %copy-start.38 = (f32[128]{0:T(128)S(1)}, f32[128]{0:T(128)}, u32[]{:S(2)}) copy-start(f32[128]{0:T(128)} %copy-done.37) | copy-start | bytes 1540
  637.1 92.8 %copy-start.39 = (f32[128]{0:T(128)S(1)}, f32[128]{0:T(128)}, u32[]{:S(2)}) copy-start(f32[128]{0:T(128)} %get-tuple-element.172) | copy-start | bytes 1540
Sparse Core Ops, SparseCore 0:
  12.5 29.6 all-gather.5
  53.4 30.0 reduce-scatter.2
  341.8 27.9 all-gather.9
  374.9 146.4 all-reduce.5
  525.6 108.5 all-reduce.7
  637.0 24.1 reduce-scatter.4
  662.9 64.5 all-gather.11
Sparse Core Ops, SparseCore 1:
  56.0 76.4 all-gather.7

commit v4 on v3

--- a/solution.py
+++ b/solution.py
@@ -60,48 +60,112 @@
 
 MESH = pl.DeviceIdType.MESH
 
-def ag_plane_kernel(src, out, own_sem, send_sem, recv_sem, sib_send, sib_recv):
+def ring_gather_kernel(src, out, own_sem, ssem, rsem):
+    x = lax.axis_index("tensor")
+    def xi(d): return (x + d) % 4
+    def peer(o): return {"tensor": xi(o)}
+    barrier = pltpu.get_barrier_semaphore()
+    for o in (1, -1):
+        pl.semaphore_signal(barrier, inc=1, device_id=peer(o), device_id_type=MESH)
+    pl.semaphore_wait(barrier, 2)
+    def copy(n, block, half, to, own):
+        rows = pl.ds(64 * half, 64)
+        return pltpu.make_async_remote_copy(
+            src_ref=src.at[rows] if own else out.at[block, rows], dst_ref=out.at[block, rows],
+            send_sem=ssem.at[n], recv_sem=rsem.at[n], device_id=peer(to), device_id_type=MESH)
+    right = [copy(0, x, 0, 1, True), copy(1, x, 1, 1, True)]
+    left = [copy(2, x, 1, -1, True), copy(3, x, 0, -1, True)]
+    for a, b in zip(right, left):
+        a.start(); b.start()
+    mine = pltpu.make_async_copy(src, out.at[x], own_sem)
+    mine.start()
+    copy(0, xi(-1), 0, 1, False).wait_recv()
+    on_right = copy(4, xi(-1), 0, 1, False)
+    on_right.start()
+    copy(2, xi(1), 1, -1, False).wait_recv()
+    on_left = copy(5, xi(1), 1, -1, False)
+    on_left.start()
+    copy(1, xi(-1), 1, 1, False).wait_recv()
+    copy(3, xi(1), 0, -1, False).wait_recv()
+    copy(4, xi(2), 0, 1, False).wait_recv()
+    copy(5, xi(2), 1, -1, False).wait_recv()
+    mine.wait()
+    for cp in right + left + [on_right, on_left]:
+        cp.wait_send()
+
+
+def ring_gather(shard, cid):
+    rows, width = shard.shape
+    D = pltpu.SemaphoreType.DMA
+    return pl.pallas_call(
+        ring_gather_kernel,
+        out_shape=jax.ShapeDtypeStruct((4, rows, width), shard.dtype),
+        in_specs=[pl.BlockSpec(memory_space=pltpu.VMEM)],
+        out_specs=pl.BlockSpec(memory_space=pltpu.VMEM),
+        scratch_shapes=[D(()), D((6,)), D((6,))],
+        compiler_params=pltpu.CompilerParams(collective_id=cid, has_side_effects=True),
+        name="ring_gather",
+    )(shard).reshape(4 * rows, width)
+
+
+def branch_gather_kernel(part, tokens, gain, residual, out, nr1, nb, nr2, low_rows, nsend, nrecv,
+                         own_sem, send_sem, recv_sem, sib_send, sib_recv):
+    f32, low = jnp.float32, jnp.bfloat16
     x = lax.axis_index("tensor"); e = lax.axis_index("expert")
     z = e // 2; c = e % 2
+    def xi(d): return (x + d) % 4
     def peer(ox, oz):
-        return {"expert": ((z + oz) % 4) * 2 + c, "tensor": (x + ox) % 4}
+        return {"expert": ((z + oz) % 4) * 2 + c, "tensor": xi(ox)}
     sib = {"expert": z * 2 + 1 - c}
-    def blk(dx, dz):
-        return (c * 4 + (z + dz) % 4) * 4 + (x + dx) % 4
-    def sblk(dx, dz):
-        return ((1 - c) * 4 + (z + dz) % 4) * 4 + (x + dx) % 4
+    def blk(dx, dz): return (c * 4 + (z + dz) % 4) * 4 + xi(dx)
+    def sblk(dx, dz): return ((1 - c) * 4 + (z + dz) % 4) * 4 + xi(dx)
     barrier = pltpu.get_barrier_semaphore()
     near = [peer(1, 0), peer(-1, 0), peer(0, 1), peer(0, -1), sib]
     for p in near:
         pl.semaphore_signal(barrier, inc=1, device_id=p, device_id_type=MESH)
     pl.semaphore_wait(barrier, len(near))
-    n = [0]
     pend = []
-    def desc(dx, dz, ox, oz, q, nq, sidx, own=False):
+    def go(cps):
+        for cp in cps: cp.start()
+        pend.extend(cps)
+        return cps
+    def nrc(n, src, dst, to):
+        return pltpu.make_async_remote_copy(src_ref=src, dst_ref=dst, send_sem=nsend.at[n], recv_sem=nrecv.at[n],
+                                            device_id=peer(to, 0), device_id_type=MESH)
+    n1 = go([nrc(0, part.at[xi(2), pl.ds(0, 64)], nr1.at[0], 1), nrc(1, part.at[xi(2), pl.ds(64, 64)], nr1.at[1], -1)])
+    n2 = go([nrc(2, part.at[xi(1), pl.ds(64, 64)], nr2.at[0, pl.ds(64, 64)], 1),
+             nrc(3, part.at[xi(-1), pl.ds(0, 64)], nr2.at[1, pl.ds(0, 64)], -1)])
+    n1[0].wait_recv()
+    nb[0] = (part[xi(1), 0:64].astype(f32) + nr1[0].astype(f32)).astype(low)
+    n3 = go([nrc(4, nb.at[0], nr2.at[0, pl.ds(0, 64)], 1)])
+    n1[1].wait_recv()
+    nb[1] = (part[xi(-1), 64:128].astype(f32) + nr1[1].astype(f32)).astype(low)
+    n3 += go([nrc(5, nb.at[1], nr2.at[1, pl.ds(64, 64)], -1)])
+    for cp in n2 + n3: cp.wait_recv()
+    total = tokens[...].astype(f32) + part[x].astype(f32) + nr2[0].astype(f32) + nr2[1].astype(f32)
+    residual[...] = total
+    scale = lax.rsqrt(jnp.mean(total * total, -1, keepdims=True) + epsilon)
+    low_rows[...] = (total * scale * gain[...]).astype(low)
+    src = low_rows
+
+    count = [0]
+    def desc(dx, dz, ox, oz, q, nq, n, own=False):
         rows = pl.ds(q * 32, nq * 32)
-        s = src.at[rows] if own else out.at[blk(dx, dz), rows]
         return pltpu.make_async_remote_copy(
-            src_ref=s, dst_ref=out.at[blk(dx, dz), rows],
-            send_sem=send_sem.at[sidx],
-            recv_sem=recv_sem.at[(dx - ox) % 4, (dz - oz) % 4, q],
+            src_ref=src.at[rows] if own else out.at[blk(dx, dz), rows], dst_ref=out.at[blk(dx, dz), rows],
+            send_sem=send_sem.at[n], recv_sem=recv_sem.at[(dx - ox) % 4, (dz - oz) % 4, q],
             device_id=peer(ox, oz), device_id_type=MESH)
     def send(dx, dz, ox, oz, q, nq, own=False):
-        cp = desc(dx, dz, ox, oz, q, nq, n[0], own)
-        n[0] += 1
-        cp.start(); pend.append(cp)
+        go([desc(dx, dz, ox, oz, q, nq, count[0], own)])
+        count[0] += 1
     def recv(dx, dz, q, nq):
-        rows = pl.ds(q * 32, nq * 32)
-        pltpu.make_async_remote_copy(
-            src_ref=out.at[blk(dx, dz), rows], dst_ref=out.at[blk(dx, dz), rows],
-            send_sem=send_sem.at[0], recv_sem=recv_sem.at[dx % 4, dz % 4, q],
-            device_id=peer(1, 0), device_id_type=MESH).wait_recv()
-    sn = [0]
-    def sibsend(dx, dz, own=False):
-        cp = pltpu.make_async_remote_copy(
-            src_ref=src if own else out.at[blk(dx, dz)], dst_ref=out.at[blk(dx, dz)],
+        desc(dx, dz, 0, 0, q, nq, 0).wait_recv()
+    def sibcopy(block, dx, dz, own=False):
+        return pltpu.make_async_remote_copy(
+            src_ref=src if own else out.at[block], dst_ref=out.at[block],
             send_sem=sib_send.at[dx % 4, dz % 4], recv_sem=sib_recv.at[dx % 4, dz % 4],
             device_id=sib, device_id_type=MESH)
-        cp.start(); pend.append(cp)
+    def sibsend(dx, dz, own=False): go([sibcopy(blk(dx, dz), dx, dz, own)])
     for ox, oz in ((1, 0), (-1, 0), (0, 1), (0, -1)):
         send(0, 0, ox, oz, 0, 4, own=True)
     mine = pltpu.make_async_copy(src, out.at[blk(0, 0)], own_sem)
@@ -139,48 +203,262 @@
     for dx in (1, -1):
         for dz in (1, -1):
             sibsend(dx, dz)
-    for dx in (1, -1, 2):
-        recv(dx, 2, 0, 1); recv(dx, 2, 1, 1)
-        recv(2, dx, 2, 1); recv(2, dx, 3, 1)
-    for dx in (1, -1, 2):
-        sibsend(dx, 2)
-        if dx != 2: sibsend(2, dx)
+    for d in (1, -1, 2):
+        recv(d, 2, 0, 1); recv(d, 2, 1, 1)
+        recv(2, d, 2, 1); recv(2, d, 3, 1)
+    for d in (1, -1, 2):
+        sibsend(d, 2)
+        if d != 2: sibsend(2, d)
     for dx in range(4):
         for dz in range(4):
-            pltpu.make_async_remote_copy(
-                src_ref=src, dst_ref=out.at[sblk(dx, dz)],
-                send_sem=sib_send.at[dx, dz], recv_sem=sib_recv.at[dx, dz],
-                device_id=sib, device_id_type=MESH).wait_recv()
+            sibcopy(sblk(dx, dz), dx, dz).wait_recv()
     mine.wait()
-    for cp in pend:
-        cp.wait_send()
-
-def ag_plane(shard, cid):
-    rows, width = shard.shape
+    for cp in pend: cp.wait_send()
+
+
+def branch_gather(part, tokens, gain, cid):
+    bf = jnp.bfloat16
+    V = pltpu.VMEM
+    D = pltpu.SemaphoreType.DMA
+    vm = pl.BlockSpec(memory_space=pltpu.VMEM)
+    rows, width = tokens.shape
     return pl.pallas_call(
-        ag_plane_kernel,
-        out_shape=jax.ShapeDtypeStruct((32, rows, width), shard.dtype),
-        in_specs=[pl.BlockSpec(memory_space=pl.ANY)],
-        out_specs=pl.BlockSpec(memory_space=pl.ANY),
-        scratch_shapes=[pltpu.SemaphoreType.DMA(()), pltpu.SemaphoreType.DMA((40,)),
-                        pltpu.SemaphoreType.DMA((4, 4, 4)), pltpu.SemaphoreType.DMA((4, 4)), pltpu.SemaphoreType.DMA((4, 4))],
-        compiler_params=pltpu.CompilerParams(collective_id=cid, has_side_effects=True),
-        name="ag_plane",
-    )(shard)
-
-
-def expert_forward_kernel(x_ref, u_ref, routes_ref, w_ref, down_ref, acts_ref):
+        branch_gather_kernel,
+        out_shape=(jax.ShapeDtypeStruct((rows, width), jnp.float32), jax.ShapeDtypeStruct((32, rows, width), bf)),
+        in_specs=[vm, vm, vm],
+        out_specs=(vm, pl.BlockSpec(memory_space=pl.ANY)),
+        scratch_shapes=[V((2, 64, width), bf), V((2, 64, width), bf), V((2, 128, width), bf), V((rows, width), bf),
+                        D((6,)), D((6,)), D(()), D((40,)), D((4, 4, 4)), D((4, 4)), D((4, 4))],
+        compiler_params=pltpu.CompilerParams(collective_id=cid, has_side_effects=True, vmem_limit_bytes=32 << 20),
+        name="branch_gather",
+    )(part.reshape(4, rows, width), tokens, gain)
+
+
+def grad_layout_kernel(src, gate, up, down):
+    f32 = jnp.float32
+    for n in range(5):
+        for i, ref in enumerate((gate, up)):
+            ref[n] = src[:, 0, :, pl.ds(640 * i + 128 * n, 128)].astype(f32).reshape(256, 128)
+        down[n] = src[:, 0, :, pl.ds(1280 + 128 * n, 128)].astype(f32).reshape(256, 128).T
+
+
+def grad_layout(sums):
+    return pl.pallas_call(
+        grad_layout_kernel,
+        grid=(6,),
+        out_shape=(jax.ShapeDtypeStruct((5, 1536, 128), jnp.float32),) * 2 + (jax.ShapeDtypeStruct((5, 128, 1536), jnp.float32),),
+        in_specs=[pl.BlockSpec((4, 1, 64, 1920), lambda j: (0, j, 0, 0))],
+        out_specs=(pl.BlockSpec((5, 256, 128), lambda j: (0, j, 0)),) * 2 + (pl.BlockSpec((5, 128, 256), lambda j: (0, 0, j)),),
+        compiler_params=pltpu.CompilerParams(vmem_limit_bytes=32 << 20),
+        name="grad_layout",
+    )(sums)
+
+
+def grad_sum_kernel(g, n_part, g_out, n_out, q, sib, a3a, a3b, b3, a4, b4, a5a, a5b, b5, a6, b6, extra,
+                    nr1, nb, nr2, sib_sems, ssem, rsem, gsend, grecv, gsib_send, gsib_recv, esend, erecv, nsend, nrecv):
+    f32, low = jnp.float32, jnp.bfloat16
+    x = lax.axis_index("tensor"); e = lax.axis_index("expert"); y = lax.axis_index("dp")
+    z = e // 2; c = e % 2
+    def zi(d): return (z + d) % 4
+    def yi(d): return (y + d) % 4
+    def xi(d): return (x + d) % 4
+    def peer(oz, oy):
+        return {"expert": zi(oz) * 2 + c, "dp": yi(oy)}
+    def xpeer(o):
+        return {"tensor": xi(o)}
+    partner = {"expert": z * 2 + 1 - c}
+    barrier = pltpu.get_barrier_semaphore()
+    near = [peer(1, 0), peer(-1, 0), peer(0, 1), peer(0, -1), partner, xpeer(1), xpeer(2), xpeer(3)]
+    for p in near:
+        pl.semaphore_signal(barrier, inc=1, device_id=p, device_id_type=MESH)
+    pl.semaphore_wait(barrier, len(near))
+    A0, A1, B0, B1 = pl.ds(0, 384), pl.ds(384, 256), pl.ds(640, 256), pl.ds(896, 256)
+    A, B = pl.ds(0, 640), pl.ds(640, 512)
+    sent = []
+    def rc(n, src, dst, to):
+        cp = pltpu.make_async_remote_copy(src_ref=src, dst_ref=dst, send_sem=ssem.at[n], recv_sem=rsem.at[n],
+                                          device_id=to, device_id_type=MESH)
+        return cp
+    def go(cps):
+        for cp in cps: cp.start()
+        sent.extend(cps)
+        return cps
+    def nrc(n, src, dst, to):
+        return pltpu.make_async_remote_copy(src_ref=src, dst_ref=dst, send_sem=nsend.at[n], recv_sem=nrecv.at[n],
+                                            device_id=to, device_id_type=MESH)
+    sibling = go([pltpu.make_async_remote_copy(src_ref=g.at[1 - c], dst_ref=sib, send_sem=sib_sems.at[0], recv_sem=sib_sems.at[1],
+                                               device_id=partner, device_id_type=MESH)])
+    n1 = go([nrc(0, n_part.at[xi(2), pl.ds(0, 64)], nr1.at[0], xpeer(1)),
+             nrc(1, n_part.at[xi(2), pl.ds(64, 64)], nr1.at[1], xpeer(-1))])
+    sibling[0].wait_recv()
+    def body(n, _):
+        i, j = n // 4, n % 4
+        q[i, j] = (g[c, i, j].astype(f32) + sib[i, j].astype(f32)).astype(low)
+        return 0
+    lax.fori_loop(0, 16, body, 0)
+    def add(i, j, cols, *terms):
+        t = q[i, j, :, cols].astype(f32)
+        for s in terms:
+            t = t + s.astype(f32)
+        q[i, j, :, cols] = t.astype(low)
+    c3 = go([rc(0, q.at[zi(2), :, :, A0], a3a, peer(1, 0)),
+             rc(1, q.at[zi(2), :, :, A1], a3b, peer(-1, 0)),
+             rc(2, q.at[:, yi(2), :, B0], b3.at[0], peer(0, 1)),
+             rc(3, q.at[:, yi(2), :, B1], b3.at[1], peer(0, -1))])
+    for cp in n1: cp.wait_recv()
+    nb[0, 0:64] = (n_part[xi(1), 0:64].astype(f32) + nr1[0].astype(f32)).astype(low)
+    nb[0, 64:128] = n_part[xi(1), 64:128]
+    nb[1, 0:64] = n_part[xi(-1), 0:64]
+    nb[1, 64:128] = (n_part[xi(-1), 64:128].astype(f32) + nr1[1].astype(f32)).astype(low)
+    n2 = go([nrc(2, nb.at[0], nr2.at[0], xpeer(1)), nrc(3, nb.at[1], nr2.at[1], xpeer(-1))])
+    for cp in c3: cp.wait_recv()
+    def body4(n, _):
+        add(zi(1), n, A0, a3a[n])
+        add(zi(-1), n, A1, a3b[n])
+        add(n, yi(1), B0, b3[0, n])
+        add(n, yi(-1), B1, b3[1, n])
+        return 0
+    lax.fori_loop(0, 4, body4, 0)
+    c4 = go([rc(4, q.at[zi(1), :, :, A], a4.at[0], peer(1, 0)),
+             rc(5, q.at[zi(-1), :, :, A], a4.at[1], peer(-1, 0)),
+             rc(6, q.at[:, yi(1), :, B], b4.at[0], peer(0, 1)),
+             rc(7, q.at[:, yi(-1), :, B], b4.at[1], peer(0, -1))])
+    for cp in c4: cp.wait_recv()
+    def body5(n, _):
+        add(z, n, A, a4[0, n], a4[1, n])
+        add(n, y, B, b4[0, n], b4[1, n])
+        return 0
+    lax.fori_loop(0, 4, body5, 0)
+    c5 = go([rc(8, q.at[z, yi(2), :, A0], a5a, peer(0, 1)),
+             rc(9, q.at[z, yi(2), :, A1], a5b, peer(0, -1)),
+             rc(10, q.at[zi(2), y, :, B0], b5.at[0], peer(1, 0)),
+             rc(11, q.at[zi(2), y, :, B1], b5.at[1], peer(-1, 0))])
+    for cp in n2: cp.wait_recv()
+    n_out[...] = n_part[x].astype(f32) + nr2[0].astype(f32) + nr2[1].astype(f32)
+    for cp in c5: cp.wait_recv()
+    add(z, yi(1), A0, a5a[...])
+    add(z, yi(-1), A1, a5b[...])
+    add(zi(1), y, B0, b5[0])
+    add(zi(-1), y, B1, b5[1])
+    c6 = go([rc(12, q.at[z, yi(1), :, A], a6.at[0], peer(0, 1)),
+             rc(13, q.at[z, yi(-1), :, A], a6.at[1], peer(0, -1)),
+             rc(14, q.at[zi(1), y, :, B], b6.at[0], peer(1, 0)),
+             rc(15, q.at[zi(-1), y, :, B], b6.at[1], peer(-1, 0))])
+    for cp in c6: cp.wait_recv()
+    own = g_out.at[c, z, y]
+    own[:, A] = (q[z, y, :, A].astype(f32) + a6[0].astype(f32) + a6[1].astype(f32)).astype(low)
+    last = q[z, y, :, B].astype(f32) + b6[0].astype(f32) + b6[1].astype(f32)
+    own[:, pl.ds(640, 384)] = last[:, 0:384].astype(low)
+    extra[0] = last[:, 384:512].astype(low)
+    es = go([pltpu.make_async_remote_copy(src_ref=extra.at[0], dst_ref=extra.at[o], send_sem=esend.at[o], recv_sem=erecv.at[o],
+                                          device_id=xpeer(o), device_id_type=MESH) for o in (1, 2, 3)])
+    for cp in es: cp.wait_recv()
+    own[:, pl.ds(1024, 128)] = (extra[0].astype(f32) + extra[1].astype(f32) + extra[2].astype(f32) + extra[3].astype(f32)).astype(low)
+
+    starts = (0, 384, 640, 896, 1152)
+    def part(qq, nq): return pl.ds(starts[qq], starts[qq + nq] - starts[qq])
+    count = [0]
+    def send(dy, dz, oy, oz, qq, nq):
+        cp = pltpu.make_async_remote_copy(
+            src_ref=g_out.at[c, zi(dz), yi(dy), :, part(qq, nq)], dst_ref=g_out.at[c, zi(dz), yi(dy), :, part(qq, nq)],
+            send_sem=gsend.at[count[0]], recv_sem=grecv.at[(dy - oy) % 4, (dz - oz) % 4, qq],
+            device_id=peer(oz, oy), device_id_type=MESH)
+        count[0] += 1
+        go([cp])
+    def recv(dy, dz, qq, nq):
+        ref = g_out.at[c, zi(dz), yi(dy), :, part(qq, nq)]
+        pltpu.make_async_remote_copy(src_ref=ref, dst_ref=ref, send_sem=gsend.at[0], recv_sem=grecv.at[dy % 4, dz % 4, qq],
+                                     device_id=peer(1, 0), device_id_type=MESH).wait_recv()
+    def sibcopy(cc, dy, dz):
+        ref = g_out.at[cc, zi(dz), yi(dy)]
+        return pltpu.make_async_remote_copy(src_ref=ref, dst_ref=ref, send_sem=gsib_send.at[dy % 4, dz % 4],
+                                            recv_sem=gsib_recv.at[dy % 4, dz % 4], device_id=partner, device_id_type=MESH)
+    def sibsend(dy, dz): go([sibcopy(c, dy, dz)])
+    for oy, oz in ((1, 0), (-1, 0), (0, 1), (0, -1)):
+        send(0, 0, oy, oz, 0, 4)
+    sibsend(0, 0)
+    for s in (1, -1):
+        recv(s, 0, 0, 4)
+        if s == -1:
+            send(s, 0, 1, 0, 1, 2)
+        else:
+            send(s, 0, -1, 0, 0, 1); send(s, 0, -1, 0, 3, 1)
+        for oz in (1, -1):
+            send(s, 0, 0, oz, 0, 2)
+        recv(0, s, 0, 4)
+        if s == -1:
+            send(0, s, 0, 1, 1, 2)
+        else:
+            send(0, s, 0, -1, 0, 1); send(0, s, 0, -1, 3, 1)
+        for oy in (1, -1):
+            send(0, s, oy, 0, 2, 2)
+        sibsend(s, 0); sibsend(0, s)
+    recv(2, 0, 1, 2); recv(2, 0, 0, 1); recv(2, 0, 3, 1)
+    for oz in (1, -1):
+        send(2, 0, 0, oz, 0, 2)
+    recv(0, 2, 1, 2); recv(0, 2, 0, 1); recv(0, 2, 3, 1)
+    for oy in (1, -1):
+        send(0, 2, oy, 0, 2, 2)
+    sibsend(2, 0); sibsend(0, 2)
+    for dy in (1, -1, 2):
+        for s in (1, -1):
+            recv(dy, s, 0, 2)
+            send(dy, s, 0, -s, 0 if s == 1 else 1, 1)
+            recv(s, dy, 2, 2)
+            send(s, dy, -s, 0, 2 if s == 1 else 3, 1)
+    for dy in (1, -1):
+        for dz in (1, -1):
+            sibsend(dy, dz)
+    for d in (1, -1, 2):
+        recv(d, 2, 0, 1); recv(d, 2, 1, 1)
+        recv(2, d, 2, 1); recv(2, d, 3, 1)
+    for d in (1, -1, 2):
+        sibsend(d, 2)
+        if d != 2: sibsend(2, d)
+    for dy in range(4):
+        for dz in range(4):
+            sibcopy(1 - c, dy, dz).wait_recv()
+    for cp in sent: cp.wait_send()
+
+
+def grad_sum(g, n_part, cid):
+    bf = jnp.bfloat16
+    V = pltpu.VMEM
+    D = pltpu.SemaphoreType.DMA
+    vm = pl.BlockSpec(memory_space=pltpu.VMEM)
+    g = g.reshape(2, 4, 4, 48, 1152)
+    n_part = n_part.reshape(4, 128, 1536)
+    total, rows = pl.pallas_call(
+        grad_sum_kernel,
+        out_shape=(jax.ShapeDtypeStruct((2, 4, 4, 48, 1152), bf), jax.ShapeDtypeStruct((128, 1536), jnp.float32)),
+        in_specs=[vm, vm], out_specs=(vm, vm),
+        scratch_shapes=[V((4, 4, 48, 1152), bf), V((4, 4, 48, 1152), bf),
+                        V((4, 48, 384), bf), V((4, 48, 256), bf), V((2, 4, 48, 256), bf),
+                        V((2, 4, 48, 640), bf), V((2, 4, 48, 512), bf),
+                        V((48, 384), bf), V((48, 256), bf), V((2, 48, 256), bf),
+                        V((2, 48, 640), bf), V((2, 48, 512), bf), V((4, 48, 128), bf),
+                        V((2, 64, 1536), bf), V((2, 128, 1536), bf), V((2, 128, 1536), bf),
+                        D((2,)), D((16,)), D((16,)), D((40,)), D((4, 4, 4)), D((4, 4)), D((4, 4)), D((4,)), D((4,)), D((4,)), D((4,))],
+        compiler_params=pltpu.CompilerParams(collective_id=cid, has_side_effects=True, vmem_limit_bytes=40 << 20),
+        name="grad_sum",
+    )(g, n_part)
+    return total.reshape(1536, 1152), rows
+
+
+def expert_forward_kernel(x_ref, u_ref, w_ref, down_ref, acts_ref):
     f32, low = jnp.float32, jnp.bfloat16
     rows = x_ref.shape[0]
     wide = down_ref.shape[0]
     count = wide // 128
     first = lax.axis_index("expert") * count
     pre = jnp.dot(x_ref[...], w_ref[...], preferred_element_type=f32)
-    raw = lax.dot_general(u_ref[...], down_ref[...], (((1,), (1,)), ((), ())), preferred_element_type=f32)
+    width = x_ref.shape[1]
+    raw = lax.dot_general(u_ref[:, 0:width], down_ref[...], (((1,), (1,)), ((), ())), preferred_element_type=f32)
     lane = lax.broadcasted_iota(jnp.int32, (rows, 128), 1)
-    named = lane == routes_ref[:, 0:1]
-    for n in range(1, routes_ref.shape[1]):
-        named = named | (lane == routes_ref[:, n : n + 1])
+    routes = u_ref[:, width : width + 128].astype(f32).astype(jnp.int32)
+    named = lane == routes[:, 0:1]
+    for n in range(1, 8):
+        named = named | (lane == routes[:, n : n + 1])
     logits = jnp.where(named, pre[:, 2 * wide :], -1e30)
     raised = jnp.exp(logits - jnp.max(logits, -1, keepdims=True))
     gates = raised / jnp.sum(raised, -1, keepdims=True)
@@ -207,7 +485,7 @@
     acts_ref[:, 3 * wide :] = weighted.astype(low)
 
 
-def expert_forward(x, u, routes, w_all, down, block=256):
+def expert_forward(x, u, w_all, down, block=256):
     rows, width = x.shape
     wide = down.shape[0]
     total = w_all.shape[1]
@@ -223,15 +501,14 @@
         out_shape=jax.ShapeDtypeStruct((rows, 3 * wide + 128), jnp.bfloat16),
         in_specs=[
             pl.BlockSpec((block, width), lambda i: (i, 0)),
-            pl.BlockSpec((block, width), lambda i: (place(i), 0)),
-            pl.BlockSpec((block, routes.shape[1]), lambda i: (place(i), 0)),
+            pl.BlockSpec((block, u.shape[1]), lambda i: (place(i), 0)),
             pl.BlockSpec((width, total), lambda i: (0, 0)),
             pl.BlockSpec((wide, width), lambda i: (0, 0)),
         ],
         out_specs=pl.BlockSpec((block, 3 * wide + 128), lambda i: (i, 0)),
         compiler_params=pltpu.CompilerParams(vmem_limit_bytes=48 << 20),
         name="expert_forward",
-    )(x, u, routes, w_all, down)
+    )(x, u, w_all, down)
 
 
 def expert_back_kernel(acts_hbm, x_hbm, u_hbm, w_ref, down_ref, out, dw_out, router_out,
@@ -445,7 +722,7 @@
     bf = jnp.bfloat16
     V = pltpu.VMEM
     nk = 12
-    u = u.reshape(4, 2, 512, 1536)
+    u = u.reshape(4, 2, 512, u.shape[1])
     D = pltpu.SemaphoreType.DMA
     vm = pl.BlockSpec(memory_space=pltpu.VMEM)
     anym = pl.BlockSpec(memory_space=pl.ANY)
@@ -498,8 +775,10 @@
     scale = 1.0 / math.sqrt(HEAD_SIZE)
     inputs = tokens.astype(jnp.float32)
     first_gain = attention_gain.astype(jnp.float32)
-    first_normed, first_scale = normalize(inputs, first_gain)
-    group_rows = lax.all_gather(first_normed.astype(jnp.bfloat16), "tensor", axis=0, tiled=True)
+    group_tokens = ring_gather(tokens, 5).astype(jnp.float32)
+    group_normed, group_scale = normalize(group_tokens, first_gain)
+    group_rows = group_normed.astype(jnp.bfloat16)
+    first_scale = lax.rsqrt(jnp.mean(inputs * inputs, -1, keepdims=True) + epsilon)
     index = jnp.arange(group_len, dtype=jnp.int32)
     positions = index - jnp.sum((documents[None, :] < documents[:, None]).astype(jnp.int32), 1)
     cosine_table, sine_table = rope_tables(positions, HEAD_SIZE)
@@ -550,18 +829,22 @@
     mixed_blocks, logsum_blocks = lax.map(forward_block, starts)
     attended = mixed_blocks.reshape(group_len, query_heads * HEAD_SIZE)
     head_part = jnp.dot(attended, output_weight, preferred_element_type=jnp.float32)
-    branch = lax.psum_scatter(
-        head_part.astype(jnp.bfloat16), "tensor", scatter_dimension=0, tiled=True
-    ).astype(jnp.float32)
-    residual = inputs + branch
     second_gain = expert_gain.astype(jnp.float32)
+    residual, plane_rows = branch_gather(
+        head_part.astype(jnp.bfloat16), tokens, second_gain.reshape(1, width), 6
+    )
+    plane_rows = plane_rows.reshape(-1, width)
     second_normed, second_scale = normalize(residual, second_gain)
     second_low = second_normed.astype(jnp.bfloat16)
     plane = ("expert", "tensor")
     experts_index = jnp.arange(experts_all, dtype=jnp.int32)
-    plane_routes = lax.all_gather(expert_routes, plane, axis=0, tiled=True)
-    plane_upstream = lax.all_gather(out_cotangent, plane, axis=0, tiled=True)
-    plane_rows = ag_plane(second_low, 1).reshape(-1, width)
+    lined_routes = jnp.pad(expert_routes, ((0, 0), (0, 128 - expert_routes.shape[1])))
+    plane_upstream = lax.all_gather(
+        jnp.concatenate([out_cotangent, lined_routes.astype(jnp.bfloat16)], 1),
+        plane,
+        axis=0,
+        tiled=True,
+    )
 
     def dense_gates(rows, routes):
         named = jnp.any(routes[:, :, None] == experts_index[None, None, :], 1)
@@ -583,7 +866,7 @@
         1,
     )
     down_flat = down_weight.reshape(wide, width)
-    acts = expert_forward(plane_rows, plane_upstream, plane_routes, in_weights, down_flat)
+    acts = expert_forward(plane_rows, plane_upstream, in_weights, down_flat)
     sums, weight_grads, router_pairs = expert_back(
         acts, plane_rows, plane_upstream, in_weights, down_flat, 2
     )
@@ -610,12 +893,12 @@
     )
     residual_back, expert_gain_local = norm_back(residual, second_scale, second_gain, normed_back)
     residual_grad = upstream + residual_back
-    group_grad = lax.all_gather(residual_grad.astype(jnp.bfloat16), "tensor", axis=0, tiled=True)
+    group_grad = ring_gather(residual_grad.astype(jnp.bfloat16), 7)
     attended_grad = jnp.einsum(
         "td,hd->th", group_grad, output_weight, preferred_element_type=jnp.float32
     ).astype(jnp.bfloat16)
     attended_grad = attended_grad.reshape(group_len, pair_heads, frequency_ratio, HEAD_SIZE)
-    output_local = jnp.einsum("th,td->hd", attended, group_grad, preferred_element_type=jnp.float32)
+    output_local = jnp.einsum("td,th->dh", group_grad, attended, preferred_element_type=jnp.float32)
 
     def backward_block(carry, pieces):
         key_acc, value_acc = carry
@@ -678,28 +961,33 @@
     normed_part = normed_part + jnp.einsum(
         "th,dh->td", value_back, value_matrix, preferred_element_type=jnp.float32
     )
-    normed_grad = lax.psum_scatter(
-        normed_part.astype(jnp.bfloat16), "tensor", scatter_dimension=0, tiled=True
-    ).astype(jnp.float32)
-    input_back, attention_gain_local = norm_back(inputs, first_scale, first_gain, normed_grad)
+    attention_gain_local = jnp.sum(normed_part * group_tokens * group_scale, 0)
+    small = jnp.concatenate(
+        [
+            router_local,
+            attention_gain_local[:, None],
+            expert_gain_local[:, None],
+            jnp.zeros((width, 126 - experts_all), jnp.float32),
+        ],
+        1,
+    )
+    grads = jnp.concatenate([query_local, key_local, value_local, output_local, small], 1)
+    grads, normed_grad = grad_sum(grads.astype(jnp.bfloat16), normed_part.astype(jnp.bfloat16), 4)
+    input_back, _ = norm_back(inputs, first_scale, first_gain, normed_grad)
     input_gradient = residual_grad + input_back
-    query_gradient, key_gradient, value_gradient, output_gradient = (
-        lax.psum(query_local.astype(jnp.bfloat16), ("dp", "expert")).astype(jnp.float32),
-        lax.psum(key_local.astype(jnp.bfloat16), ("dp", "expert")).astype(jnp.float32),
-        lax.psum(value_local.astype(jnp.bfloat16), ("dp", "expert")).astype(jnp.float32),
-        lax.psum(output_local.astype(jnp.bfloat16), ("dp", "expert")).astype(jnp.float32),
-    )
-    router_gradient, attention_gain_gradient, expert_gain_gradient = lax.psum(
-        (router_local, attention_gain_local, expert_gain_local), ("dp", "expert", "tensor")
-    )
-    weight_grads = weight_grads.transpose(1, 0, 2, 3).reshape(width, 3 * wide).astype(jnp.float32)
-    gate_gradient, up_gradient = (
-        weight_grads[:, part : part + wide]
-        .reshape(width, local_experts, hidden)
-        .transpose(1, 0, 2)
-        for part in (0, wide)
-    )
-    down_gradient = weight_grads[:, 2 * wide :].T.reshape(local_experts, hidden, width)
+    grads = grads.astype(jnp.float32)
+    query_wide = query_weight.shape[1]
+    key_wide = query_wide + key_matrix.shape[1]
+    value_wide = key_wide + value_matrix.shape[1]
+    output_wide = value_wide + query_wide
+    query_gradient = grads[:, :query_wide]
+    key_gradient = grads[:, query_wide:key_wide]
+    value_gradient = grads[:, key_wide:value_wide]
+    output_gradient = grads[:, value_wide:output_wide].T
+    router_gradient = grads[:, output_wide : output_wide + experts_all]
+    attention_gain_gradient = grads[:, output_wide + experts_all]
+    expert_gain_gradient = grads[:, output_wide + experts_all + 1]
+    gate_gradient, up_gradient, down_gradient = grad_layout(weight_grads)
     return (
         layer_output,
         input_gradient,

time: 804 us -> 471 us (0.59)
  waiting for transfers between devices: 309 us -> 0.04 us
  Pallas kernels: 206 us -> 331 us
  blocking collectives: 116 us -> 0 us
  other arithmetic: 36 us -> 17.4 us
    psum x2 -> x0, waiting for transfers between devices: 234 us -> none  [the longest x1 123 us: shards(): lax.psum((router_local, attention_gain_local, expert_gain_local), ('dp',...]
    pallas_call x1 -> x5, Pallas kernels: 49.3 us -> 174 us  [the longest x1 71.9 us: branch_gather(): pl.pallas_call(branch_gather_kernel, out_shape=(jax.ShapeDtypeStruct((row...]
    psum x1 -> x0, blocking collectives: 67.4 us -> none  [shards(): lax.psum((router_local, attention_gain_local, expert_gain_local), ('dp',...]
    all_gather x3 -> x1, waiting for transfers between devices: 52.7 us -> 0.01 us  [shards(): lax.all_gather(jnp.concatenate([out_cotangent, lined_routes.astype(jnp.bf...]
    all_gather x1 -> x0, blocking collectives: 48.7 us -> none  [shards(): plane_routes = lax.all_gather(expert_routes, plane, axis=0, tiled=True)]
    reduce_scatter x2 -> x0, waiting for transfers between devices: 20.6 us -> none  [the longest x1 20.5 us: shards(): lax.psum_scatter(normed_part.astype(jnp.bfloat16), 'tensor', scatter_dime...]
    convert_element_type x8 -> x6, other arithmetic: 19.8 us -> 4.04 us  [the longest x2 1.99 us: shards(): group_rows = group_normed.astype(jnp.bfloat16)]
    transpose x2 -> x0, local copies, waits for them, and re-layouts: 14.7 us -> none  [shards(): weight_grads[:, 2 * wide:].T.reshape(local_experts, hidden, width)]
  transfers between devices with their start and end apart: 8 -> 2, of which waited for: 5 -> 0; matrix products, arithmetic and copies ran while one was open for 9% -> 19% of each run, Pallas kernels for 6% -> 33%
where the time goes in v4:
time: 471 us; the launch traced here: 462 us
  Pallas kernels  331 us (70%)
  local copies, waits for them, and re-layouts  66.9 us (14%)
  matrix products  31.2 us (7%)
  other arithmetic  17.4 us (4%)
  between operations  15.4 us (3%)
    pallas_call x1, Pallas kernels, expert_back(): pl.pallas_call(expert_back_kernel, out_shape=(jax.ShapeDtypeStruct((2, 12...  115 us
    pallas_call x1, Pallas kernels, branch_gather(): pl.pallas_call(branch_gather_kernel, out_shape=(jax.ShapeDtypeStruct((row...  71.9 us
    pallas_call x1, Pallas kernels, grad_sum(): pl.pallas_call(grad_sum_kernel, out_shape=(jax.ShapeDtypeStruct((2, 4, 4,...  62.4 us
    pallas_call x1, Pallas kernels, expert_forward(): pl.pallas_call(expert_forward_kernel, grid=(rows // block,), out_shape=ja...  41.2 us
    pallas_call x2, Pallas kernels, ring_gather(): pl.pallas_call(ring_gather_kernel, out_shape=jax.ShapeDtypeStruct((4, row...  34.8 us
    unnamed x135, local copies, waits for them, and re-layouts  28.3 us
  transfers between devices with their start and end apart: 2, of which 0 were waited for; matrix products, arithmetic and copies ran while one was open for 19% of the time, Pallas kernels for 33%

profile of v4, /device:TPU:1, one launch (start us, length us, event | category | flops | bytes accessed | tf_op | source)
XLA Modules:
  0.0 461.8 jit_solution(5628901157783727939)
XLA Ops:
  7.3 0.8 convert.50
  8.2 1.8 fusion.36
  10.1 0.7 reshape.315.gain
  10.8 1.3 convert_element_type.152
  12.1 20.2 %ring_gather.2 = bf16[4,128,1536]{2,1,0:T(8,128)(2,1)} custom-call(bf16[128,1536]{1,0:T(8,128)(2,1)} %tokens.1), custom_call_target="tpu_custom_call" | custom-call | tf_op jit(solution)/shard_map/ring_gather/pallas_call | solution.py:100
  32.3 1.5 copy.118
  33.9 2.7 copy.121
  36.6 2.3 copy.124
  38.9 4.0 copy.122
  42.9 4.1 copy.125
  47.0 0.9 copy.123
  48.3 1.6 fusion.9
  49.9 2.8 copy.126
  53.5 2.1 fusion.49
  55.7 0.8 fusion.50
  57.1 0.7 convolution_convert_fusion.6
  57.8 1.2 fusion.47
  59.0 0.9 fusion.3
  59.9 1.7 copy-done.8
  61.7 1.2 fusion.18
  63.0 1.0 convolution_convert_fusion
  64.1 71.9 %branch_gather.1 = (f32[128,1536]{1,0:T(8,128)S(1)}, bf16[32,128,1536]{2,1,0:T(8,128)(2,1)S(1)}) custom-call(bf16[4,128,1536]{2,1,0:T(8,128)(2,1)S(1)} %bitcast.149, bf16[128,1536]{1,0:T(8,128)(2,1)S(1)} %copy-done.6, f32[1,1536]{1,0:T(1,128)S(1)} %reshape.315.gain), custom_call_target="tpu_custom_call" | custom-call | tf_op jit(solution)/shard_map/branch_gather/pallas_call | solution.py:225
  136.0 4.5 copy-done.1
  140.5 0.9 copy-done.2
  141.5 7.6 %concatenate.41.w_ref = bf16[1536,1408]{1,0:T(8,128)(2,1)} concatenate(bf16[1536,640]{1,0:T(8,128)(2,1)} %copy.124, bf16[1536,640]{1,0:T(8,128)(2,1)} %copy.125, bf16[1536,64]{1,0:T(8,128)(2,1)S(1)} %pad.10, bf16[1536,64]{1,0:T(8,128)(2,1)S(1)} %pad.10), dimensions={1} | concatenate | bytes 8650752 | tf_op jit(solution)/shard_map/concatenate | solution.py:859
  149.1 0.6 fusion.37
  149.8 0.6 log_add_fusion
  150.4 41.2 %expert_forward.1.acts_hbm = bf16[4096,2048]{1,0:T(8,128)(2,1)} custom-call(bf16[4096,1536]{1,0:T(8,128)(2,1)} %bitcast.145, bf16[4096,1664]{1,0:T(8,128)(2,1)} %all-gather.4.cloned.1.call-done.u_ref, bf16[1536,1408]{1,0:T(8,128)(2,1)} %concatenate.41.w_ref, bf16[640,1536]{1,0:T(8,128)(2,1)S(1)} %bitcast.148), custom_call_target="tpu_custom_call" | custom-call | tf_op jit(solution)/shard_map/expert_forward/pallas_call | solution.py:498
  191.6 115.1 %expert_back.1 = (f32[2,128,1536]{2,1,0:T(8,128)}, bf16[6,64,1920]{2,1,0:T(8,128)(2,1)}, f32[1536,128]{1,0:T(8,128)}) custom-call(bf16[4096,2048]{1,0:T(8,128)(2,1)} %expert_forward.1.acts_hbm, bf16[4096,1536]{1,0:T(8,128)(2,1)} %bitcast.146, bf16[4,2,512,1664]{3,2,1,0:T(8,128)(2,1)} %bitcast.154, bf16[1536,1408]{1,0:T(8,128)(2,1)} %concatenate.41.w_ref, ...), custom_call_target="tpu_custom_call" | custom-call | tf_op jit(solution)/shard_map/expert_back/pallas_call | solution.py:729
  306.8 2.5 fusion.29
  309.4 1.5 fusion.48
  311.0 1.3 multiply_reduce_fusion
  312.3 1.3 fusion.43
  313.6 14.6 %ring_gather.3 = bf16[4,128,1536]{2,1,0:T(8,128)(2,1)} custom-call(bf16[128,1536]{1,0:T(8,128)(2,1)} %get-tuple-element.95.src), custom_call_target="tpu_custom_call" | custom-call | tf_op jit(solution)/shard_map/ring_gather/pallas_call | solution.py:100
  328.2 2.2 convolution_convert_fusion.5
  330.6 4.3 fusion
  335.2 1.8 fusion.2
  337.1 1.1 fusion.23
  338.3 0.7 convolution_multiply_fusion
  339.6 1.0 fusion.51
  340.6 0.6 convolution_add_fusion.1
  341.2 1.1 fusion.24
  342.6 0.9 fusion.46
  343.6 0.7 concatenate.48
  344.3 2.9 copy.133
  347.3 1.5 concatenate.49
  348.8 3.0 fusion.17
  351.8 2.0 convolution_convert_fusion.3
  354.4 2.0 convolution_convert_fusion.2
  356.4 2.0 convolution_convert_fusion.1
  358.4 0.8 broadcast_in_dim.49
  359.2 6.6 %concatenate.47.g = bf16[2,4,4,48,1152]{4,3,2,1,0:T(8,128)(2,1)} concatenate(bf16[2,4,4,48,384]{4,3,2,1,0:T(8,128)(2,1)} %convolution_convert_fusion.2, bf16[2,4,4,48,128]{4,3,2,1,0:T(8,128)(2,1)S(1)} %convolution_convert_fusion.4, bf16[2,4,4,48,128]{4,3,2,1,0:T(8,128)(2,1)S(1)} %convolution_convert_fusion.3, bf16[2,4,4,48,384]{4,3,2,1,0:T(8,128)(2,1)} %convolution_convert_fusion.1, ...), dimensions={4} | concatenate | bytes 7077888 | tf_op jit(solution)/shard_map/concatenate | solution.py:974
  365.8 2.1 copy-done.4
  367.9 62.4 %grad_sum.1 = (bf16[2,4,4,48,1152]{4,3,2,1,0:T(8,128)(2,1)S(1)}, f32[128,1536]{1,0:T(8,128)S(1)}) custom-call(bf16[2,4,4,48,1152]{4,3,2,1,0:T(8,128)(2,1)S(1)} %copy-done.4, bf16[4,128,1536]{2,1,0:T(8,128)(2,1)S(1)} %bitcast.150), custom_call_target="tpu_custom_call" | custom-call | tf_op jit(solution)/shard_map/grad_sum/pallas_call | solution.py:431
  430.3 0.7 bitcast_convert_fusion
  431.1 2.7 fusion.44
  433.8 1.6 copy-done.11
  435.3 3.1 copy.157
  438.5 0.9 copy.158
  439.4 3.0 slice_reduce_fusion
  442.7 2.6 fusion.45
  445.3 1.2 fusion.33
  446.6 2.7 copy-done.7
  449.2 5.3 %grad_layout.1 = (f32[5,1536,128]{2,1,0:T(8,128)}, f32[5,1536,128]{2,1,0:T(8,128)}, f32[5,128,1536]{2,1,0:T(8,128)}) custom-call(bf16[4,6,64,1920]{3,2,1,0:T(8,128)(2,1)S(1)} %bitcast.151), custom_call_target="tpu_custom_call" | custom-call | tf_op jit(solution)/shard_map/grad_layout/pallas_call | solution.py:246
  (156 shorter events, 4.8 us)
Async XLA Ops:
  7.2 49.9 %copy-start = (bf16[1536,128]{1,0:T(8,128)(2,1)S(1)}, bf16[1536,128]{1,0:T(8,128)(2,1)}, u32[]{:S(2)}) copy-start(bf16[1536,128]{1,0:T(8,128)(2,1)} %param.20) | copy-start | bytes 1179652
  7.2 25.1 %copy-start.61 = (bf16[1536]{0:T(1024)(128)(2,1)S(1)}, bf16[1536]{0:T(1024)(128)(2,1)}, u32[]{:S(2)}) copy-start(bf16[1536]{0:T(1024)(128)(2,1)} %param.17) | copy-start | bytes 9220
  7.2 25.1 %copy-start.14 = (bf16[1536,384]{1,0:T(8,128)(2,1)S(1)}, bf16[1536,384]{1,0:T(8,128)(2,1)}, u32[]{:S(2)}) copy-start(bf16[1536,384]{1,0:T(8,128)(2,1)} %param.18) | copy-start | bytes 3538948
  7.2 26.5 %copy-start.23 = (bf16[1536,128]{1,0:T(8,128)(2,1)S(1)}, bf16[1536,128]{1,0:T(8,128)(2,1)}, u32[]{:S(2)}) copy-start(bf16[1536,128]{1,0:T(8,128)(2,1)} %param.19) | copy-start | bytes 1179652
  7.2 143.1 %all-gather.4.cloned.1.call-start = ((), (), s32[]{:S(2)}) async-start(), calls=%async_computation | async-start | bytes 14057472 | tf_op jit(solution)/shard_map/all_gather | solution.py:842
  10.0 436.5 %all-gather.6.cloned.1.call-start = ((), (), s32[]{:S(2)}) async-start(), calls=%async_computation.1 | async-start | bytes 7372800 | tf_op jit(solution)/shard_map/all_gather | solution.py:876
  32.3 24.4 %copy-start.45 = (f32[1536]{0:T(1024)}, f32[1536]{0:T(1024)S(1)}, u32[]{:S(2)}) copy-start(f32[1536]{0:T(1024)S(1)} %convert_element_type.141) | copy-start | bytes 18436
  38.9 8.1 %copy-start.31 = (bf16[1536,40]{0,1:T(8,128)(2,1)S(1)}, bf16[1536,40]{0,1:T(8,128)(2,1)}, u32[]{:S(2)}) copy-start(bf16[1536,40]{0,1:T(8,128)(2,1)} %param.23) | copy-start | bytes 368644
  42.9 5.0 %copy-start.9 = (bf16[4,128,1536]{2,1,0:T(8,128)(2,1)S(1)}, bf16[4,128,1536]{2,1,0:T(8,128)(2,1)}, u32[]{:S(2)}) copy-start(bf16[4,128,1536]{2,1,0:T(8,128)(2,1)} %ring_gather.2) | copy-start | bytes 4718596
  48.3 8.3 %copy-start.52 = (f32[512]{0:T(512)}, f32[512]{0:T(512)S(1)}, u32[]{:S(2)}) copy-start(f32[512]{0:T(512)S(1)} %get-tuple-element.117) | copy-start | bytes 6148
  48.3 4.4 copy-start.51
  52.7 2.9 copy-start.13
  52.7 2.9 copy-start.27
  55.6 2.1 copy-start.42
  56.6 2.4 copy-start.33
  56.6 2.4 copy-start.35
  57.8 2.2 copy-start.37
  59.0 2.6 copy-start.8
  59.0 2.7 copy-start.49
  61.7 1.3 copy-start.25
  62.9 1.2 copy-start.6
  62.9 78.5 %copy-start.22 = (bf16[1536,40]{1,0:T(8,128)(2,1)S(1)}, bf16[1536,40]{1,0:T(8,128)(2,1)}, u32[]{:S(2)}) copy-start(bf16[1536,40]{1,0:T(8,128)(2,1)} %copy.123) | copy-start | bytes 368644
  136.0 4.5 copy-start.1
  141.5 7.7 %copy-start.55 = (s32[128,8]{0,1:T(8,128)S(1)}, s32[128,8]{0,1:T(8,128)}, u32[]{:S(2)}) copy-start(s32[128,8]{0,1:T(8,128)} %param.16) | copy-start | bytes 12292
  141.5 8.3 %copy-start.50 = (f32[2,3,512]{2,1,0:T(4,128)S(1)}, f32[2,3,512]{2,1,0:T(4,128)}, u32[]{:S(2)}) copy-start(f32[2,3,512]{2,1,0:T(4,128)} %copy-done.49) | copy-start | bytes 36868
  141.5 8.9 %copy-start.5 = (bf16[5,128,1536]{2,1,0:T(8,128)(2,1)S(1)}, bf16[5,128,1536]{2,1,0:T(8,128)(2,1)}, u32[]{:S(2)}) copy-start(bf16[5,128,1536]{2,1,0:T(8,128)(2,1)} %param.26) | copy-start | bytes 5898244
  306.7 4.2 copy-start.3
  306.8 4.2 copy-start.21
  306.8 4.2 copy-start.32
  306.8 4.2 copy-start.47
  306.8 5.5 %copy-start.16 = (bf16[128,1536]{1,0:T(8,128)(2,1)S(1)}, bf16[128,1536]{1,0:T(8,128)(2,1)}, u32[]{:S(2)}) copy-start(bf16[128,1536]{1,0:T(8,128)(2,1)} %param.27) | copy-start | bytes 1179652
  309.3 2.9 copy-start.60
  309.4 4.2 copy-start.56
  310.9 1.4 copy-start.58
  310.9 17.3 %copy-start.41 = (f32[128,40]{0,1:T(8,128)}, f32[128,40]{0,1:T(8,128)S(1)}, u32[]{:S(2)}) copy-start(f32[128,40]{0,1:T(8,128)S(1)} %get-tuple-element.125) | copy-start | bytes 61444
  310.9 1.3 copy-start.59
  312.2 16.0 %copy-start.26 = (bf16[384,1536]{1,0:T(8,128)(2,1)S(1)}, bf16[384,1536]{1,0:T(8,128)(2,1)}, u32[]{:S(2)}) copy-start(bf16[384,1536]{1,0:T(8,128)(2,1)} %param.21) | copy-start | bytes 3538948
  328.2 2.3 copy-start.38
  328.2 2.3 copy-start.44
  330.5 4.3 slice-start
  330.6 4.7 %slice-start.1 = ((s8[6291456]{0:T(1024)(128)(4,1)}), s8[2097152]{0:T(1024)(128)(4,1)S(1)}, s32[]{:S(2)}) async-start(s8[6291456]{0:T(1024)(128)(4,1)} %bitcast.152), calls=%async_computation.3 | async-start | bytes 4194304
  335.2 1.8 copy-start.34
  335.2 1.9 copy-start.36
  338.2 2.4 copy-start.29
  338.2 1.3 copy-start.15
  338.9 1.7 copy-start.24
  339.1 1.5 copy-start.19
  341.2 1.4 copy-start.10
  341.2 1.4 copy-start.53
  342.3 1.2 copy-start.28
  343.6 3.7 copy-start.54
  343.6 5.2 %copy-start.48 = (f32[1536]{0:T(1024)S(1)}, f32[1536]{0:T(1024)}, u32[]{:S(2)}) copy-start(f32[1536]{0:T(1024)} %convert_element_type.152) | copy-start | bytes 18436
  344.3 4.4 copy-start.57
  348.8 5.0 %copy-start.12 = (bf16[1536,512]{1,0:T(8,128)(2,1)S(1)}, bf16[1536,512]{1,0:T(8,128)(2,1)}, u32[]{:S(2)}) copy-start(bf16[1536,512]{1,0:T(8,128)(2,1)} %copy.126) | copy-start | bytes 4718596
  348.8 5.0 %copy-start.30 = (bf16[512,2,64]{0,2,1:T(8,128)(2,1)S(1)}, bf16[512,2,64]{0,2,1:T(8,128)(2,1)}, u32[]{:S(2)}) copy-start(bf16[512,2,64]{0,2,1:T(8,128)(2,1)} %copy-done.29) | copy-start | bytes 393220
  348.8 5.6 %copy-start.20 = (bf16[512,6,64]{0,2,1:T(8,128)(2,1)S(1)}, bf16[512,6,64]{0,2,1:T(8,128)(2,1)}, u32[]{:S(2)}) copy-start(bf16[512,6,64]{0,2,1:T(8,128)(2,1)} %copy-done.19) | copy-start | bytes 1179652
  353.8 2.6 copy-start.18
  353.8 2.6 copy-start.40
  365.8 2.1 copy-start.4
  431.1 4.3 copy-start.11
  435.3 3.1 slice-start.2
  435.3 7.1 %copy-start.46 = (f32[1536]{0:T(1024)S(1)}, f32[1536]{0:T(1024)}, u32[]{:S(2)}) copy-start(f32[1536]{0:T(1024)} %copy-done.45) | copy-start | bytes 18436
  439.4 5.9 %copy-start.17 = (f32[128,1536]{1,0:T(8,128)S(1)}, f32[128,1536]{1,0:T(8,128)}, u32[]{:S(2)}) copy-start(f32[128,1536]{1,0:T(8,128)} %get-tuple-element.96) | copy-start | bytes 2359300
  446.6 2.7 copy-start.7
  (3 other events, 3.1 us)
Sparse Core Ops, SparseCore 0:
  10.9 76.1 all-gather.3
  330.6 73.2 all-gather.5
